TPU v7x, 512 devices: a whole 4x4x16 slice. The times are simulated.
512 devices in a mesh: slide: 8 (over y_lo, x), seq: 64 (over z, y_hi, core).
Axes of the slice: x: 4, y: 4 (y_hi: 2, y_lo: 2; y = y_hi * 2 + y_lo), z: 16, core: 2. Of those that a mesh axis runs over, the one named last changes fastest.
Arguments:
- tokens: bfloat16 [8, 8192, 768], P('slide', 'seq'), may hold values from -12 to 12
- lengths: int32 [8], P('slide'), may hold values from 2048 to 8192, as said below
- w_query: bfloat16 [768, 384], P('seq'), may hold values from -0.21875 to 0.21875
- w_key: bfloat16 [768, 384], P('seq'), may hold values from -0.21875 to 0.21875
- w_value: bfloat16 [768, 384], P('seq'), may hold values from -0.21875 to 0.21875
- w_out: bfloat16 [384, 768], P('seq'), may hold values from -0.3125 to 0.3125
- grad_out: bfloat16 [8, 8192, 768], P('slide', 'seq'), may hold values from -6 to 6
Outputs:
- mixed: bfloat16 [8, 8192, 768], P('slide', 'seq')
- grad_tokens: bfloat16 [8, 8192, 768], P('slide', 'seq')
- grad_value_weight: float32 [768, 384], P('seq')
- grad_out_weight: float32 [384, 768], P('seq')
Inputs may be any that keep to these rules, and one draw needn't show every extreme that they name: `lengths`: each slide's count of valid tile tokens lies between 2048 and 8192, and some slide is full.
All inputs are finite; a program needn't handle non-finite values.
Results may differ from a plain program's by a relative error of at most 0.013.
The roundings to bfloat16 on the way count: a program that leaves them out, or rounds other values in their place, can miss the bound.
Values may be sent and summed in bfloat16 or wider, within the bound.
No kernel may reach another device: no remote copies, remote signals or barrier semaphores. Data moves between devices by JAX's collectives and lax.ppermute only.
A program may use at most 64 MiB of HBM per device.

v0:
```python
import jax
import jax.numpy as jnp
from jax import lax
from jax.sharding import PartitionSpec as P

HEADS = 8
SCALES = 5


def from_partner(value, axis, distance):
    mask = 2**distance
    pairs = [(source, source ^ mask) for source in range(lax.axis_size(axis))]
    return lax.ppermute(value, axis, pairs)


def dilate(rows, rate, head_count):
    count = rows.shape[0] // rate
    shaped = rows.reshape(count, rate, 2, head_count, -1)
    pick = (
        jnp.arange(rate, dtype=jnp.int32)[:, None]
        == (jnp.arange(head_count, dtype=jnp.int32) % rate)[None, :]
    ).astype(rows.dtype)
    return jnp.sum(shaped * pick[None, :, None, :, None], axis=1).reshape(count, 2, -1)


def spread(rows, rate, head_count):
    count = rows.shape[0]
    pick = (
        jnp.arange(rate, dtype=jnp.int32)[:, None]
        == (jnp.arange(head_count, dtype=jnp.int32) % rate)[None, :]
    ).astype(rows.dtype)
    shaped = rows.reshape(count, 1, 2, head_count, -1) * pick[None, :, None, :, None]
    return shaped.reshape(count * rate, 2, -1)


def block_masks(block, length, tok, head_count):
    heads_index = jnp.arange(head_count, dtype=jnp.int32)
    rows_index = jnp.arange(tok, dtype=jnp.int32)
    masks = []
    for scale in range(SCALES):
        rate = 2**scale
        count = tok // rate
        start = block // rate * rate
        member = rows_index // count
        within = rows_index % count
        position = (
            (start + member)[None, :] * tok + within[None, :] * rate + (heads_index % rate)[:, None]
        )
        key_valid = position < length
        query_part = rows_index[None, :] % rate == heads_index[:, None] % rate
        masks.append(query_part[:, :, None] & key_valid[:, None, :])
    return jnp.concatenate(masks, axis=2)


def probabilities(query, keys, allowed):
    scale_factor = query.shape[1] ** (-0.5)
    scores = (
        lax.dot_general(query, keys, (((1,), (1,)), ((), ())), preferred_element_type=jnp.float32)
        * scale_factor
    )
    scores = jnp.where(allowed, scores, jnp.float32(-1000000000.0))
    top = jnp.max(scores, axis=1, keepdims=True)
    expo = jnp.exp(scores - top)
    return expo / jnp.sum(expo, axis=1, keepdims=True)


def forward_head(query, keys, values, allowed):
    probs = probabilities(query, keys, allowed)
    return jnp.dot(probs.astype(jnp.bfloat16), values, preferred_element_type=jnp.float32)


def backward_head(query, keys, values, allowed, upstream):
    scale_factor = query.shape[1] ** (-0.5)
    probs = probabilities(query, keys, allowed)
    weights = probs.astype(jnp.bfloat16)
    grad_probs = lax.dot_general(
        upstream, values, (((1,), (1,)), ((), ())), preferred_element_type=jnp.float32
    )
    delta = jnp.sum(probs * grad_probs, axis=1, keepdims=True)
    grad_scores = (probs * (grad_probs - delta)).astype(jnp.bfloat16)
    grad_query = jnp.dot(grad_scores, keys, preferred_element_type=jnp.float32) * scale_factor
    grad_key = (
        lax.dot_general(
            grad_scores, query, (((0,), (0,)), ((), ())), preferred_element_type=jnp.float32
        )
        * scale_factor
    )
    grad_value = lax.dot_general(
        weights, upstream, (((0,), (0,)), ((), ())), preferred_element_type=jnp.float32
    )
    return (grad_query, grad_key, grad_value)


def split_heads(rows, head_count):
    return rows.reshape(rows.shape[0], head_count, -1).transpose(1, 0, 2)


def on_device(tokens, lengths, w_query, w_key, w_value, w_out, grad_out):
    full_query, full_key, full_value, full_out = (
        lax.all_gather(w_query, "seq", axis=0, tiled=True),
        lax.all_gather(w_key, "seq", axis=0, tiled=True),
        lax.all_gather(w_value, "seq", axis=0, tiled=True),
        lax.all_gather(w_out, "seq", axis=0, tiled=True),
    )
    inputs = tokens[0]
    upstream = grad_out[0]
    length = lengths[0]
    tok = inputs.shape[0]
    inner = full_query.shape[1]
    head_count = HEADS
    block = lax.axis_index("seq")
    query = jnp.dot(inputs, full_query, preferred_element_type=jnp.float32).astype(jnp.bfloat16)
    pairs = jnp.stack(
        [
            jnp.dot(inputs, full_key, preferred_element_type=jnp.float32).astype(jnp.bfloat16),
            jnp.dot(inputs, full_value, preferred_element_type=jnp.float32).astype(jnp.bfloat16),
        ],
        axis=1,
    )
    dilated = [pairs] + [dilate(pairs, 2**scale, head_count) for scale in range(1, SCALES)]
    for scale in range(1, SCALES):
        current = dilated[scale]
        for bit in range(scale):
            other = from_partner(current, "seq", bit)
            upper = block // 2**bit % 2 == 1
            current = jnp.where(
                upper, jnp.concatenate([other, current], 0), jnp.concatenate([current, other], 0)
            )
        dilated[scale] = current
    keys = jnp.concatenate(dilated, 0)
    allowed = block_masks(block, length, tok, head_count)
    query_heads = split_heads(query, head_count)
    key_heads = split_heads(keys[:, 0], head_count)
    value_heads = split_heads(keys[:, 1], head_count)
    outputs = lax.map(
        lambda item: forward_head(*item), (query_heads, key_heads, value_heads, allowed)
    )
    valid = (block * tok + jnp.arange(tok, dtype=jnp.int32) < length)[:, None]
    attended = jnp.where(
        valid, outputs.transpose(1, 0, 2).reshape(tok, inner), jnp.float32(0.0)
    ).astype(jnp.bfloat16)
    mixed = jnp.dot(attended, full_out, preferred_element_type=jnp.float32).astype(jnp.bfloat16)
    out_weight_part = lax.dot_general(
        attended, upstream, (((0,), (0,)), ((), ())), preferred_element_type=jnp.float32
    )
    grad_attended = lax.dot_general(
        upstream, full_out, (((1,), (1,)), ((), ())), preferred_element_type=jnp.float32
    )
    grad_attended = jnp.where(valid, grad_attended, jnp.float32(0.0)).astype(jnp.bfloat16)
    grad_query, grad_key, grad_value = lax.map(
        lambda item: backward_head(*item),
        (query_heads, key_heads, value_heads, allowed, split_heads(grad_attended, head_count)),
    )
    grad_pairs = (
        jnp.stack([grad_key, grad_value], axis=2).transpose(1, 2, 0, 3).reshape(-1, 2, inner)
    )
    returned = [grad_pairs[scale * tok : (scale + 1) * tok] for scale in range(SCALES)]
    for scale in range(1, SCALES):
        current = returned[scale]
        for bit in reversed(range(scale)):
            half = current.shape[0] // 2
            upper = block // 2**bit % 2 == 1
            sending = jnp.where(upper, current[:half], current[half:])
            keeping = jnp.where(upper, current[half:], current[:half])
            current = keeping + from_partner(sending.astype(jnp.bfloat16), "seq", bit).astype(
                sending.dtype
            )
        returned[scale] = current
    local_grads = returned[0]
    for scale in range(1, SCALES):
        local_grads = local_grads + spread(returned[scale], 2**scale, head_count)
    grad_query_rows = grad_query.transpose(1, 0, 2).reshape(tok, inner).astype(jnp.bfloat16)
    grad_key_rows = local_grads[:, 0].astype(jnp.bfloat16)
    grad_value_rows = local_grads[:, 1].astype(jnp.bfloat16)
    contract = (((1,), (1,)), ((), ()))
    grad_inputs = (
        lax.dot_general(grad_query_rows, full_query, contract, preferred_element_type=jnp.float32)
        + lax.dot_general(grad_key_rows, full_key, contract, preferred_element_type=jnp.float32)
        + lax.dot_general(grad_value_rows, full_value, contract, preferred_element_type=jnp.float32)
    )
    value_weight_part = lax.dot_general(
        inputs, grad_value_rows, (((0,), (0,)), ((), ())), preferred_element_type=jnp.float32
    )
    value_rows = w_value.shape[0]
    out_rows = w_out.shape[0]
    totals = lax.psum((value_weight_part, out_weight_part), ("slide", "seq"))
    value_share = lax.dynamic_slice_in_dim(totals[0], block * value_rows, value_rows, 0)
    out_share = lax.dynamic_slice_in_dim(totals[1], block * out_rows, out_rows, 0)
    return (mixed[None], grad_inputs.astype(jnp.bfloat16)[None], value_share, out_share)


def solution(mesh):
    in_specs = (
        P("slide", "seq", None),
        P("slide"),
        P("seq", None),
        P("seq", None),
        P("seq", None),
        P("seq", None),
        P("slide", "seq", None),
    )
    out_specs = (P("slide", "seq", None), P("slide", "seq", None), P("seq", None), P("seq", None))
    return jax.shard_map(
        on_device, mesh=mesh, in_specs=in_specs, out_specs=out_specs, check_vma=False
    )
```

profile of v0, /device:TPU:2, one launch (start us, length us, event | category | flops | bytes accessed | tf_op | source)
XLA Modules:
  0.0 983.6 jit_solution(2175241238805501417)
XLA Ops:
  7.2 85.8 %all-gather.2 = bf16[64,12,384]{2,1,0:T(8,128)(2,1)S(1)} all-gather(bf16[1,12,384]{2,1,0:T(8,128)(2,1)} %bitcast.254), channel_id=1, replica_groups=mesh['slide'=8,'seq'=64] {'seq'}, dimensions={0}, use_global_device_ids=true | all-gather | bytes 599040 | tf_op jit(solution)/shard_map/all_gather | solution.py:102
  93.2 73.8 %all-gather.1 = bf16[64,12,384]{2,1,0:T(8,128)(2,1)S(1)} all-gather(bf16[1,12,384]{2,1,0:T(8,128)(2,1)S(1)} %bitcast.255), channel_id=1, replica_groups=mesh['slide'=8,'seq'=64] {'seq'}, dimensions={0}, use_global_device_ids=true | all-gather | bytes 599040 | tf_op jit(solution)/shard_map/all_gather | solution.py:101
  169.1 2.3 collective-permute-start
  173.4 2.1 collective-permute-start.1
  176.9 2.2 collective-permute-start.3
  180.5 2.1 collective-permute-start.6
  182.6 76.7 %all-gather.3 = bf16[64,6,768]{2,1,0:T(8,128)(2,1)S(1)} all-gather(bf16[1,6,768]{2,1,0:T(8,128)(2,1)S(1)} %bitcast.256), channel_id=1, replica_groups=mesh['slide'=8,'seq'=64] {'seq'}, dimensions={0}, use_global_device_ids=true | all-gather | bytes 599040 | tf_op jit(solution)/shard_map/all_gather | solution.py:103
  260.3 73.8 %all-gather = bf16[64,12,384]{2,1,0:T(8,128)(2,1)S(1)} all-gather(bf16[1,12,384]{2,1,0:T(8,128)(2,1)S(1)} %bitcast.257), channel_id=1, replica_groups=mesh['slide'=8,'seq'=64] {'seq'}, dimensions={0}, use_global_device_ids=true | all-gather | bytes 599040 | tf_op jit(solution)/shard_map/all_gather | solution.py:100
  345.0 5.1 collective-permute-start.7
  351.0 2.2 collective-permute-start.4
  353.2 1.9 collective-permute-start.8
  356.1 5.2 collective-permute-start.2
  361.3 3.9 collective-permute-start.5
  365.2 2.1 collective-permute-start.9
  368.5 5.0 collective-permute-done.9
  376.4 44.9 %while.25 = (s32[]{:T(128)}, bf16[8,128,48]{1,2,0:T(8,128)(2,1)S(1)}, f32[8,640,48]{1,2,0:T(8,128)}, f32[8,640,48]{1,2,0:T(8,128)}, pred[8,128,640]{2,1,0:T(32,1...) while((s32[]{:T(128)}, ...), condition=%wide.region_12.13_spmd, body=%wide.region_8.12_spmd.sunk | while | flops 40750720 | bytes 3730541 | solution.py:150
  427.3 25.9 %while.24 = (s32[]{:T(128)}, bf16[8,128,48]{1,2,0:T(8,128)(2,1)}, pred[8,128,640]{2,1,0:T(32,128)(4,1)}, bf16[8,128,48]{2,1,0:T(8,128)(2,1)}, bf16[8,640,48]{2,1...) while((s32[]{:T(128)}, bf16[8,128,48]{1,2,0:T(8,128)(2,1)}, pred[8,128,640]{2,1,0:T(32,128)(4,1)}, ...), condition=%wide.region_7.8_spmd, body=%wide.region_4.7_spmd.sunk | while | flops 16383746 | bytes 1455189 | solution.py:135
  438.4 1.8 fusion.132
  448.1 1.8 fusion.132
  453.2 2.0 collective-permute-start.16
  456.2 2.3 fusion.58
  459.9 3.0 collective-permute-start.13
  463.2 2.2 collective-permute-start.11
  465.4 1.9 collective-permute-start.10
  468.5 2.8 collective-permute-start.17
  471.4 5.1 collective-permute-start.14
  476.6 1.9 collective-permute-start.12
  479.8 3.4 collective-permute-start.18
  483.2 1.9 collective-permute-start.15
  485.9 4.6 collective-permute-done.18
  491.4 1.9 collective-permute-start.19
  503.3 470.2 %all-reduce.3.cloned.1.call-done = (f32[768,384]{0,1:T(8,128)}, f32[384,768]{1,0:T(8,128)}) async-done(((f32[768,384]{0,1:T(8,128)}, f32[384,768]{1,0:T(8,128)}), (f32[768,384]{0,1:T(8,128)}, f32[384,768]{1,0:T(8,128)})) %all-reduce.3.cloned.1.call-update) | async-done | bytes 2359312 | tf_op jit(solution)/shard_map/psum | solution.py:186
  (290 shorter events, 116.3 us)
Async XLA Ops:
  7.2 159.9 %copy-start = (bf16[1,128,768]{2,1,0:T(8,128)(2,1)S(1)}, bf16[1,128,768]{2,1,0:T(8,128)(2,1)}, u32[]{:S(2)}) copy-start(bf16[1,128,768]{2,1,0:T(8,128)(2,1)} %param.11) | copy-start | bytes 589828
  7.2 86.0 %copy-start.22 = (bf16[12,384]{1,0:T(8,128)(2,1)S(1)}, bf16[12,384]{1,0:T(8,128)(2,1)}, u32[]{:S(2)}) copy-start(bf16[12,384]{1,0:T(8,128)(2,1)} %param.14) | copy-start | bytes 27652
  7.2 966.3 %all-reduce.3.cloned.1.call-start = ((), (), s32[]{:S(2)}) async-start(), calls=%async_computation | async-start | bytes 4718592 | tf_op jit(solution)/shard_map/psum | solution.py:186
  93.1 74.2 %copy-start.2 = (bf16[768,384]{1,0:T(8,128)(2,1)}, bf16[768,384]{1,0:T(8,128)(2,1)S(1)}, u32[]{:S(2)}) copy-start(bf16[768,384]{1,0:T(8,128)(2,1)S(1)} %reshape.811) | copy-start | bytes 1769476
  169.1 198.2 %collective-permute-start = (bf16[64,2,384]{2,0,1:T(8,128)(2,1)S(1)}, bf16[64,2,384]{2,0,1:T(8,128)(2,1)}, u32[]{:S(2)}, u32[]{:S(2)}) collective-permute-start(bf16[64,2,384]{2,0,1:T(8,128)(2,1)S(1)} %reshape.800), channel_id=1, source_target_pairs={{0,1},{1,0},{2,3},{3,2},{4,5},{5,4},{6,7},{7,6},{8,9},{9,8},{10,11... | collective-permute-start | bytes 294920 | tf_op jit(solution)/shard_map/ppermute | solution.py:13
  173.4 181.7 %collective-permute-start.1 = (bf16[32,2,384]{2,0,1:T(8,128)(2,1)}, bf16[32,2,384]{2,0,1:T(8,128)(2,1)}, u32[]{:S(2)}, u32[]{:S(2)}) collective-permute-start(bf16[32,2,384]{2,0,1:T(8,128)(2,1)} %reshape.801), channel_id=1, source_target_pairs={{0,1},{1,0},{2,3},{3,2},{4,5},{5,4},{6,7},{7,6},{8,9},{9,8},{10,11... | collective-permute-start | bytes 147464 | tf_op jit(solution)/shard_map/ppermute | solution.py:13
  175.5 7.2 copy-start.23
  176.9 173.2 %collective-permute-start.3 = (bf16[16,2,384]{2,0,1:T(8,128)(2,1)}, bf16[16,2,384]{2,0,1:T(8,128)(2,1)}, u32[]{:S(2)}, u32[]{:S(2)}) collective-permute-start(bf16[16,2,384]{2,0,1:T(8,128)(2,1)} %reshape.802), channel_id=1, source_target_pairs={{0,1},{1,0},{2,3},{3,2},{4,5},{5,4},{6,7},{7,6},{8,9},{9,8},{10,11... | collective-permute-start | bytes 73736 | tf_op jit(solution)/shard_map/ppermute | solution.py:13
  180.4 79.8 %copy-start.24 = (bf16[12,384]{1,0:T(8,128)(2,1)S(1)}, bf16[12,384]{1,0:T(8,128)(2,1)}, u32[]{:S(2)}) copy-start(bf16[12,384]{1,0:T(8,128)(2,1)} %param.13) | copy-start | bytes 27652
  180.5 163.6 %collective-permute-start.6 = (bf16[8,2,384]{2,0,1:T(8,128)(2,1)S(1)}, bf16[8,2,384]{2,0,1:T(8,128)(2,1)}, u32[]{:S(2)}, u32[]{:S(2)}) collective-permute-start(bf16[8,2,384]{2,0,1:T(8,128)(2,1)S(1)} %reshape.803), channel_id=1, source_target_pairs={{0,1},{1,0},{2,3},{3,2},{4,5},{5,4},{6,7},{7,6},{8,9},{9,8},{10,11... | collective-permute-start | bytes 36872 | tf_op jit(solution)/shard_map/ppermute | solution.py:13
  259.5 76.4 %copy-start.4 = (bf16[384,768]{1,0:T(8,128)(2,1)}, bf16[384,768]{1,0:T(8,128)(2,1)S(1)}, u32[]{:S(2)}) copy-start(bf16[384,768]{1,0:T(8,128)(2,1)S(1)} %reshape.813) | copy-start | bytes 1769476
  345.0 8.2 collective-permute-start.7
  351.0 10.3 %collective-permute-start.4 = (bf16[32,2,384]{2,0,1:T(8,128)(2,1)S(1)}, bf16[32,2,384]{2,0,1:T(8,128)(2,1)S(1)}, u32[]{:S(2)}, u32[]{:S(2)}) collective-permute-start(bf16[32,2,384]{2,0,1:T(8,128)(2,1)S(1)} %maximum_select_fusion.7), channel_id=1, source_target_pairs={{0,2},{1,3},{2,0},{3,1},{4,6},{5,7},{6,4},{7,5},{8,10},{9,11},{10,... | collective-permute-start | bytes 147464 | tf_op jit(solution)/shard_map/ppermute | solution.py:13
  353.2 12.0 %collective-permute-start.8 = (bf16[32,2,384]{2,0,1:T(8,128)(2,1)S(1)}, bf16[32,2,384]{2,0,1:T(8,128)(2,1)S(1)}, u32[]{:S(2)}, u32[]{:S(2)}) collective-permute-start(bf16[32,2,384]{2,0,1:T(8,128)(2,1)S(1)} %maximum_select_fusion.8), channel_id=1, source_target_pairs={{0,4},{1,5},{2,6},{3,7},{4,0},{5,1},{6,2},{7,3},{8,12},{9,13},{10,... | collective-permute-start | bytes 147464 | tf_op jit(solution)/shard_map/ppermute | solution.py:13
  356.1 12.3 %collective-permute-start.2 = (bf16[64,2,384]{2,0,1:T(8,128)(2,1)S(1)}, bf16[64,2,384]{2,0,1:T(8,128)(2,1)S(1)}, u32[]{:S(2)}, u32[]{:S(2)}) collective-permute-start(bf16[64,2,384]{2,0,1:T(8,128)(2,1)S(1)} %maximum_select_fusion.4), channel_id=1, source_target_pairs={{0,2},{1,3},{2,0},{3,1},{4,6},{5,7},{6,4},{7,5},{8,10},{9,11},{10,... | collective-permute-start | bytes 294920 | tf_op jit(solution)/shard_map/ppermute | solution.py:13
  361.3 7.2 collective-permute-start.5
  365.2 8.3 collective-permute-start.9
  423.7 34.8 %copy-start.1 = (f32[640,2,8,48]{0,3,2,1:T(8,128)}, f32[640,2,8,48]{0,3,2,1:T(8,128)S(1)}, u32[]{:S(2)}) copy-start(f32[640,2,8,48]{0,3,2,1:T(8,128)S(1)} %maximum_bitcast_fusion) | copy-start | bytes 5898244
  427.3 28.0 %copy-start.27 = (pred[128]{0:T(512)(128)(4,1)S(1)}, pred[128]{0:T(512)(128)(4,1)}, u32[]{:S(2)}) copy-start(pred[128]{0:T(512)(128)(4,1)} %copy-done.26) | copy-start | bytes 388
  453.2 14.1 %collective-permute-start.16 = (bf16[64,2,384]{0,2,1:T(8,128)(2,1)}, bf16[64,2,384]{0,2,1:T(8,128)(2,1)}, u32[]{:S(2)}, u32[]{:S(2)}) collective-permute-start(bf16[64,2,384]{0,2,1:T(8,128)(2,1)} %bitcast.252), channel_id=1, source_target_pairs={{0,8},{1,9},{2,10},{3,11},{4,12},{5,13},{6,14},{7,15},{8,0},{9,1},... | collective-permute-start | bytes 294920 | tf_op jit(solution)/shard_map/ppermute | solution.py:13
  458.5 8.8 copy-start.12
  458.5 6.9 copy-start.20
  459.9 11.5 %collective-permute-start.13 = (bf16[64,2,384]{2,0,1:T(8,128)(2,1)S(1)}, bf16[64,2,384]{2,0,1:T(8,128)(2,1)S(1)}, u32[]{:S(2)}, u32[]{:S(2)}) collective-permute-start(bf16[64,2,384]{2,0,1:T(8,128)(2,1)S(1)} %copy.104), channel_id=1, source_target_pairs={{0,4},{1,5},{2,6},{3,7},{4,0},{5,1},{6,2},{7,3},{8,12},{9,13},{10,... | collective-permute-start | bytes 294920 | tf_op jit(solution)/shard_map/ppermute | solution.py:13
  463.2 13.4 %collective-permute-start.11 = (bf16[64,2,384]{2,0,1:T(8,128)(2,1)S(1)}, bf16[64,2,384]{2,0,1:T(8,128)(2,1)S(1)}, u32[]{:S(2)}, u32[]{:S(2)}) collective-permute-start(bf16[64,2,384]{2,0,1:T(8,128)(2,1)S(1)} %copy.102), channel_id=1, source_target_pairs={{0,2},{1,3},{2,0},{3,1},{4,6},{5,7},{6,4},{7,5},{8,10},{9,11},{10,... | collective-permute-start | bytes 294920 | tf_op jit(solution)/shard_map/ppermute | solution.py:13
  465.4 13.2 %collective-permute-start.10 = (bf16[64,2,384]{0,2,1:T(8,128)(2,1)S(1)}, bf16[64,2,384]{0,2,1:T(8,128)(2,1)S(1)}, u32[]{:S(2)}, u32[]{:S(2)}) collective-permute-start(bf16[64,2,384]{0,2,1:T(8,128)(2,1)S(1)} %bitcast.251), channel_id=1, source_target_pairs={{0,1},{1,0},{2,3},{3,2},{4,5},{5,4},{6,7},{7,6},{8,9},{9,8},{10,11... | collective-permute-start | bytes 294920 | tf_op jit(solution)/shard_map/ppermute | solution.py:13
  467.3 11.2 %copy-start.11 = (f32[64,2,8,48]{0,3,2,1:T(8,128)S(1)}, f32[64,2,8,48]{0,3,2,1:T(8,128)}, u32[]{:S(2)}) copy-start(f32[64,2,8,48]{0,3,2,1:T(8,128)} %get-tuple-element.192) | copy-start | bytes 589828
  468.5 10.9 %collective-permute-start.17 = (bf16[32,2,384]{0,2,1:T(8,128)(2,1)S(1)}, bf16[32,2,384]{0,2,1:T(8,128)(2,1)S(1)}, u32[]{:S(2)}, u32[]{:S(2)}) collective-permute-start(bf16[32,2,384]{0,2,1:T(8,128)(2,1)S(1)} %select_convert_fusion.2), channel_id=1, source_target_pairs={{0,4},{1,5},{2,6},{3,7},{4,0},{5,1},{6,2},{7,3},{8,12},{9,13},{10,... | collective-permute-start | bytes 147464 | tf_op jit(solution)/shard_map/ppermute | solution.py:13
  471.4 11.8 %collective-permute-start.14 = (bf16[32,2,384]{2,0,1:T(8,128)(2,1)S(1)}, bf16[32,2,384]{2,0,1:T(8,128)(2,1)S(1)}, u32[]{:S(2)}, u32[]{:S(2)}) collective-permute-start(bf16[32,2,384]{2,0,1:T(8,128)(2,1)S(1)} %select_convert_fusion.9), channel_id=1, source_target_pairs={{0,2},{1,3},{2,0},{3,1},{4,6},{5,7},{6,4},{7,5},{8,10},{9,11},{10,... | collective-permute-start | bytes 147464 | tf_op jit(solution)/shard_map/ppermute | solution.py:13
  476.6 8.5 collective-permute-start.12
  479.8 10.7 %collective-permute-start.18 = (bf16[16,2,384]{0,2,1:T(8,128)(2,1)S(1)}, bf16[16,2,384]{0,2,1:T(8,128)(2,1)S(1)}, u32[]{:S(2)}, u32[]{:S(2)}) collective-permute-start(bf16[16,2,384]{0,2,1:T(8,128)(2,1)S(1)} %select_convert_fusion.1), channel_id=1, source_target_pairs={{0,2},{1,3},{2,0},{3,1},{4,6},{5,7},{6,4},{7,5},{8,10},{9,11},{10,... | collective-permute-start | bytes 73736 | tf_op jit(solution)/shard_map/ppermute | solution.py:13
  483.2 10.1 %collective-permute-start.15 = (bf16[16,2,384]{2,0,1:T(8,128)(2,1)S(1)}, bf16[16,2,384]{2,0,1:T(8,128)(2,1)S(1)}, u32[]{:S(2)}, u32[]{:S(2)}) collective-permute-start(bf16[16,2,384]{2,0,1:T(8,128)(2,1)S(1)} %select_convert_fusion.11), channel_id=1, source_target_pairs={{0,1},{1,0},{2,3},{3,2},{4,5},{5,4},{6,7},{7,6},{8,9},{9,8},{10,11... | collective-permute-start | bytes 73736 | tf_op jit(solution)/shard_map/ppermute | solution.py:13
  491.4 3.5 collective-permute-start.19
  (19 other events, 42.8 us)
Sparse Core Ops, SparseCore 0:
  499.2 474.1 all-reduce.2
where the time goes:
time: 986 us; the launch traced here: 984 us
  waiting for transfers between devices  481 us (49%)
  blocking collectives  310 us (31%)
  matrix products  73.4 us (7%)
  starting transfers between devices  55.4 us (6%)
  local copies, waits for them, and re-layouts  25.8 us (3%)
  other arithmetic  22 us (2%)
  between operations  16.1 us (2%)
    psum x1, waiting for transfers between devices, on_device(): totals = lax.psum((value_weight_part, out_weight_part), ('slide', 'seq'))  470 us
    all_gather x1, blocking collectives, on_device(): lax.all_gather(w_value, 'seq', axis=0, tiled=True)  85.8 us
    all_gather x1, blocking collectives, on_device(): lax.all_gather(w_out, 'seq', axis=0, tiled=True)  76.7 us
    all_gather x1, blocking collectives, on_device(): lax.all_gather(w_key, 'seq', axis=0, tiled=True)  73.8 us
    all_gather x1, blocking collectives, on_device(): lax.all_gather(w_query, 'seq', axis=0, tiled=True)  73.8 us
    ppermute x20, starting transfers between devices, from_partner(): return lax.ppermute(value, axis, pairs)  55.4 us
  transfers between devices with their start and end apart: 21, of which 4 were waited for; matrix products, arithmetic and copies ran while one was open for 3% of the time, Pallas kernels for 0%

commit v1 on v0

v1 whole, which is shorter than its diff:
```python
import functools

import jax
import jax.numpy as jnp
from jax import lax
from jax.experimental import pallas as pl
from jax.experimental.pallas import tpu as pltpu
from jax.sharding import Mesh, PartitionSpec as P

HEADS = 8
SCALES = 5
D = 768
INNER = 384
TOK = 128
DIM = INNER // HEADS
KEYS = SCALES * TOK
BF = jnp.bfloat16
F32 = jnp.float32
SLIDE = ("yl", "x")
ZY = ("z", "yh")
VMEM_LIMIT = 48 * 1024 * 1024


def dot(a, b):
    return jnp.dot(a, b, preferred_element_type=F32)


def dot_nt(a, b):
    return lax.dot_general(a, b, (((1,), (1,)), ((), ())), preferred_element_type=F32)


def dot_tn(a, b):
    return lax.dot_general(a, b, (((0,), (0,)), ((), ())), preferred_element_type=F32)


def partner(value, axis, mask):
    size = lax.axis_size(axis)
    return lax.ppermute(value, axis, [(source, source ^ mask) for source in range(size)])


def exchange(value, bit):
    axis, mask = (("c", 1), ("yh", 1), ("z", 1), ("z", 2))[bit]
    return partner(value, axis, mask)


def reversed4(value):
    return ((value & 1) << 3) | ((value & 2) << 1) | ((value & 4) >> 1) | ((value & 8) >> 3)


def row_position(row):
    return ((row & 7) << 4) + reversed4(row >> 3)


def swap_rows(rows):
    lane = lax.broadcasted_iota(jnp.int32, (1, rows.shape[1]), 1)
    head = jnp.zeros_like(lane)
    for start in range(DIM, rows.shape[1], DIM):
        head = head + (lane >= start).astype(jnp.int32)
    head = jnp.broadcast_to(head, rows.shape)
    for bit in range(3):
        size = 64 >> bit
        blocks = [rows[start : start + size] for start in range(0, TOK, size)]
        moved = jnp.concatenate([blocks[index ^ 1] for index in range(len(blocks))], 0)
        rows = jnp.where((head >> bit) & 1 == 1, moved, rows)
    return rows


def key_value_kernel(tokens_ref, own_ref, other_ref, out_ref):
    rows = dot(tokens_ref[:, :INNER], own_ref[...]) + dot(tokens_ref[:, INNER:], other_ref[...])
    out_ref[...] = swap_rows(rows).astype(BF)


def query_kernel(
    tokens_ref, grad_out_ref, valid_ref, order_ref, inner_ref, columns_ref, own_ref, other_ref,
    query_ref, upstream_ref, out_ref, pair_ref, query_weight_ref, joined,
):
    query = dot(tokens_ref[:, :INNER], own_ref[INNER:, :INNER])
    query = query + dot(tokens_ref[:, INNER:], other_ref[INNER:, :INNER])
    query_ref[...] = swap_rows(query).astype(BF)
    half = INNER // 2
    for place, part in enumerate((own_ref, other_ref)):
        for side in range(2):
            joined[place * half : (place + 1) * half, side * INNER : (side + 1) * INNER] = part[
                INNER + side * half : INNER + (side + 1) * half, INNER:
            ]
    out_weight = dot(inner_ref[...], joined[...]).astype(BF)
    out_ref[...] = out_weight
    upstream = dot_nt(grad_out_ref[...], out_weight)
    upstream = jnp.where(valid_ref[...] > 0, upstream, 0.0).astype(BF)
    upstream = dot(order_ref[...], upstream)
    upstream_ref[...] = swap_rows(upstream).astype(BF)
    columns = columns_ref[...]
    pair = dot(columns[:, :INNER], own_ref[:INNER, :]) + dot(columns[:, INNER:], other_ref[:INNER, :])
    pair_ref[...] = pair.astype(BF)
    weight = dot(columns[:, :INNER], own_ref[INNER:, :INNER])
    weight = weight + dot(columns[:, INNER:], other_ref[INNER:, :INNER])
    query_weight_ref[...] = weight.astype(BF)


def attention_kernel(
    query_ref, upstream_ref, rows_ref, h0, r0, h1, r1, h2, r2, h3, r3, position_ref, limit_ref,
    valid_ref, order_ref, inner_ref, out_weight_ref, grad_out_ref,
    mixed_ref, grad_query_ref, out_part_ref, grads_ref, pairs, attended, grad_query,
):
    scale = DIM ** -0.5
    pairs[:TOK, :] = rows_ref[...]
    for index, part in enumerate((h0, r0, h1, r1, h2, r2, h3, r3)):
        pairs[TOK + index * 64 : TOK + (index + 1) * 64, :] = part[...]
    limit = limit_ref[...]
    for head in range(HEADS):
        lanes = slice(head * DIM, (head + 1) * DIM)
        value_lanes = slice(INNER + head * DIM, INNER + (head + 1) * DIM)
        query = query_ref[:, lanes]
        upstream = upstream_ref[:, lanes]
        keys = pairs[:, lanes]
        values = pairs[:, value_lanes]
        position = position_ref[:1, :] ^ head
        probs_parts = []
        grad_parts = []
        out_parts = []
        grad_query_parts = []
        for start, count in ((0, KEYS), (64, TOK)):
            rows = slice(start, start + 64)
            scores = dot_nt(query[rows], keys[:count]) * scale
            allowed = jnp.broadcast_to(position[:, :count], (64, count)) < limit[rows, :count]
            scores = jnp.where(allowed, scores, jnp.float32(-1e9))
            expo = jnp.exp(scores - jnp.max(scores, axis=1, keepdims=True))
            probs = expo * (1.0 / jnp.sum(expo, axis=1, keepdims=True))
            weights = probs.astype(BF)
            out_parts.append(dot(weights, values[:count]))
            grad_probs = dot_nt(upstream[rows], values[:count])
            delta = jnp.sum(probs * grad_probs, axis=1, keepdims=True)
            grad_scores = (probs * (grad_probs - delta)).astype(BF)
            grad_query_parts.append(dot(grad_scores, keys[:count]) * scale)
            probs_parts.append(weights)
            grad_parts.append(grad_scores)
        attended[:, lanes] = jnp.concatenate(out_parts, 0)
        grad_query[:, lanes] = jnp.concatenate(grad_query_parts, 0)
        for left, right, target, factor in (
            (grad_parts, query, lanes, scale), (probs_parts, upstream, value_lanes, None)
        ):
            near = dot_tn(jnp.concatenate([left[0][:, :TOK], left[1]], 0), right)
            far = dot_tn(left[0][:, TOK:], right[:64])
            if factor is not None:
                near, far = near * factor, far * factor
            grads_ref[:TOK, target] = near
            grads_ref[TOK:, target] = far
    order = order_ref[...]
    rows = swap_rows(attended[...]).astype(BF)
    rows = jnp.where(valid_ref[...] > 0, dot_tn(order, rows), 0.0).astype(BF)
    mixed_ref[...] = dot(rows, out_weight_ref[...]).astype(BF)
    rows = dot(rows, inner_ref[...]).astype(BF)
    out_part_ref[...] = dot_tn(rows, grad_out_ref[...])
    rows = swap_rows(grad_query[...]).astype(BF)
    grad_query_ref[...] = dot_tn(order, rows).astype(BF)


def gradient_kernel(
    first_ref, total_ref, grad_query_ref, order_ref, tokens_ref, query_weight_ref, pair_ref,
    grad_tokens_ref, part_ref,
):
    rows = jnp.concatenate([first_ref[:64] + total_ref[...], first_ref[64:]], 0)
    rows = jnp.concatenate([swap_rows(rows[:, :INNER]), swap_rows(rows[:, INNER:])], 1).astype(BF)
    rows = dot_tn(order_ref[...], rows).astype(BF)
    part_ref[...] = dot_tn(tokens_ref[...], rows[:, INNER:])
    grads = dot_nt(grad_query_ref[...], query_weight_ref[...]) + dot_nt(rows, pair_ref[...])
    grad_tokens_ref[...] = grads.astype(BF)


def call(kernel, shapes, *operands, scratch=(), flops=0):
    return pl.pallas_call(
        kernel,
        out_shape=shapes,
        scratch_shapes=list(scratch),
        compiler_params=pltpu.CompilerParams(vmem_limit_bytes=VMEM_LIMIT),
        cost_estimate=pl.CostEstimate(flops=flops, bytes_accessed=4_000_000, transcendentals=0),
    )(*operands)


def shape(*sizes, kind=BF):
    return jax.ShapeDtypeStruct(sizes, kind)


def gather_weights(pair, rest):
    x = lax.axis_index("x")
    yl = lax.axis_index("yl")
    mine = jnp.where(yl == 0, pair, rest)
    mine = lax.dynamic_slice_in_dim(mine, x * 3, 3, 0)
    rows = lax.all_to_all(jnp.broadcast_to(mine[None], (32, 3, D)), ZY, 0, 0, tiled=True)
    rows = rows.reshape(1, 96, D)
    rows = lax.all_to_all(jnp.broadcast_to(rows, (8, 96, D)), SLIDE, 0, 0, tiled=True)
    rows = rows.reshape(D, D)
    return rows, partner(rows, "c", 1)


def reduce_weights(value_part, out_part):
    sent = jnp.concatenate([value_part[INNER:].reshape(-1, INNER), out_part[192:, :INNER], out_part[192:, INNER:]], 0)
    kept = jnp.concatenate([value_part[:INNER].reshape(-1, INNER), out_part[:192, :INNER], out_part[:192, INNER:]], 0)
    both = kept + partner(sent.astype(BF), "c", 1).astype(F32)
    pieces = lax.all_to_all(both.astype(BF).reshape(8, 96, INNER), SLIDE, 0, 0, tiled=True)
    piece = jnp.sum(pieces.astype(F32), 0)
    pieces = lax.all_to_all(piece.astype(BF).reshape(32, 3, INNER), ZY, 0, 0, tiled=True)
    piece = jnp.sum(pieces.astype(F32), 0)
    full = lax.all_to_all(jnp.broadcast_to(piece[None], (8, 3, INNER)), SLIDE, 0, 0, tiled=True)
    value_share = full[:4].reshape(12, INNER)
    out_share = jnp.concatenate([full[4:6].reshape(6, INNER), full[6:].reshape(6, INNER)], 1)
    return value_share, out_share


def first_halves(rows, count):
    size = rows.shape[0] // count
    return rows.reshape(count, size, -1)[:, : size // 2].reshape(rows.shape[0] // 2, -1)


def on_device(tokens, lengths, w_query, w_key, w_value, w_out, grad_out):
    inputs, grad_out, length = tokens[0], grad_out[0], lengths[0]
    core = lax.axis_index("c")
    block = (lax.axis_index("z") * 2 + lax.axis_index("yh")) * 2 + core

    pair = jnp.concatenate([w_key, w_value], 1)
    rest = jnp.concatenate([w_query, jnp.concatenate([w_out[:, :INNER], w_out[:, INNER:]], 0)], 1)
    own, other = gather_weights(pair, rest)

    row = jnp.arange(TOK, dtype=jnp.int32)
    order = (row_position(row)[:, None] == row[None, :]).astype(BF)
    column = jnp.arange(D, dtype=jnp.int32)
    place, left = column // INNER, column % INNER
    source = left % 96 // 3 * 24 + (core ^ place) * 12 + left // 96 * 3 + left % 3
    columns = (column[:, None] == source[None, :]).astype(BF)
    column = jnp.arange(INNER, dtype=jnp.int32)
    place, left = column // 192, column % 192
    source = left % 96 // 3 * 12 + (core ^ place) * 6 + left // 96 * 3 + left % 3
    inner = (column[:, None] == source[None, :]).astype(BF)
    valid = (block * TOK + row < length).astype(F32)[:, None]

    parts, limits = [], []
    for scale in range(SCALES):
        size = TOK >> scale
        parts.append((block ^ (row // size)) * TOK + row_position(row % size))
        limits.append(jnp.where(row[:, None] < size, length, -1) + jnp.zeros((1, TOK), jnp.int32))
    position = jnp.broadcast_to(jnp.concatenate(parts)[None], (8, KEYS))
    limit = jnp.concatenate(limits, 1)

    tokens_columns = dot(inputs, columns).astype(BF)
    tokens_rows = dot(order, tokens_columns).astype(BF)

    rows = pl.pallas_call(
        key_value_kernel,
        grid=(1,),
        in_specs=[
            pl.BlockSpec((TOK, D), lambda i: (0, 0)),
            pl.BlockSpec((INNER, D), lambda i: (0, 0)),
            pl.BlockSpec((INNER, D), lambda i: (0, 0)),
        ],
        out_specs=pl.BlockSpec((TOK, D), lambda i: (0, 0)),
        out_shape=shape(TOK, D),
        compiler_params=pltpu.CompilerParams(vmem_limit_bytes=VMEM_LIMIT),
    )(tokens_rows, own, other)

    halves, received = [], []
    current = rows
    for bit in range(SCALES - 1):
        half = first_halves(current, 1 << bit)
        got = exchange(half, bit)
        halves.append(half)
        received.append(got)
        current = jnp.concatenate([half, got], 0)

    query, upstream, out_weight, pair_weight, query_weight = call(
        query_kernel,
        (shape(TOK, INNER), shape(TOK, INNER), shape(INNER, D), shape(D, D), shape(D, INNER)),
        tokens_rows, grad_out, valid, order, inner, columns, own, other,
        scratch=[pltpu.VMEM((INNER, D), BF)],
        flops=3_000_000_000,
    )

    exchanged = [part for both in zip(halves, received) for part in both]
    mixed, grad_query, out_part, grads = call(
        attention_kernel,
        (shape(TOK, D), shape(TOK, INNER), shape(INNER, D, kind=F32), shape(KEYS, D, kind=F32)),
        query, upstream, rows, *exchanged, position, limit, valid, order, inner, out_weight, grad_out,
        scratch=[pltpu.VMEM((KEYS, D), BF), pltpu.VMEM((TOK, INNER), F32), pltpu.VMEM((TOK, INNER), F32)],
        flops=3_000_000_000,
    )

    total = None
    for scale in range(SCALES - 1, 0, -1):
        current = grads[scale * TOK : (scale + 1) * TOK]
        if total is not None:
            count = 1 << scale
            size = TOK // count
            current = current.reshape(count, size, D)
            added = current[:, : size // 2] + total.reshape(count, size // 2, D)
            current = jnp.concatenate([added, current[:, size // 2 :]], 1).reshape(TOK, D)
        total = current[:64] + exchange(current[64:].astype(BF), scale - 1).astype(F32)

    grad_tokens, value_part = call(
        gradient_kernel,
        (shape(TOK, D), shape(D, INNER, kind=F32)),
        grads[:TOK], total, grad_query, order, tokens_columns, query_weight, pair_weight,
    )
    value_share, out_share = reduce_weights(value_part, out_part)
    return mixed[None], grad_tokens[None], value_share, out_share


def solution(mesh):
    fine = Mesh(mesh.devices.reshape(2, 4, 16, 2, 2), ("yl", "x", "z", "yh", "c"))
    seq = ("z", "yh", "c")
    rows = P(seq, None)
    whole = P(SLIDE, seq, None)
    return jax.shard_map(
        on_device,
        mesh=fine,
        in_specs=(whole, P(SLIDE), rows, rows, rows, rows, whole),
        out_specs=(whole, whole, rows, rows),
        check_vma=False,
    )
```

time: 986 us -> 184 us (0.19)
  waiting for transfers between devices: 481 us -> 53.4 us
  blocking collectives: 310 us -> 45.8 us
  matrix products: 73.4 us -> 0.8 us
  local copies, waits for them, and re-layouts: 25.8 us -> 4.77 us
  other arithmetic: 22 us -> 2.85 us
  Pallas kernels: 0 us -> 18.5 us
  between operations: 16.1 us -> 1.71 us
    psum x1 -> x0, waiting for transfers between devices: 470 us -> none  [on_device(): totals = lax.psum((value_weight_part, out_weight_part), ('slide', 'seq'))]
    all_gather x4 -> x0, blocking collectives: 310 us -> none  [the longest x1 85.8 us: on_device(): lax.all_gather(w_value, 'seq', axis=0, tiled=True)]
    dot_general x66 -> x2, matrix products: 73.4 us -> 0.8 us  [dot(): return jnp.dot(a, b, preferred_element_type=F32)]
    all_to_all x0 -> x3, blocking collectives: none -> 45.8 us  [the longest x1 23.1 us: reduce_weights(): lax.all_to_all(piece.astype(BF).reshape(32, 3, INNER), ZY, 0, 0, tiled=True)]
    all_to_all x0 -> x2, waiting for transfers between devices: none -> 31.5 us  [the longest x1 18.4 us: gather_weights(): lax.all_to_all(jnp.broadcast_to(mine[None], (32, 3, D)), ZY, 0, 0, tiled=...]
    all_to_all x0 -> x2, starting transfers between devices: none -> 23.1 us  [the longest x1 18.1 us: gather_weights(): lax.all_to_all(jnp.broadcast_to(mine[None], (32, 3, D)), ZY, 0, 0, tiled=...]
    ppermute x20 -> x10, starting transfers between devices: 55.4 us -> 32.5 us  [partner(): lax.ppermute(value, axis, [(source, source ^ mask) for source in range(si...]
    pallas_call x0 -> x4, Pallas kernels: none -> 18.5 us  [the longest x3 18.2 us: call(): pl.pallas_call(kernel, out_shape=shapes, scratch_shapes=list(scratch), co...]
  transfers between devices with their start and end apart: 21 -> 12, of which waited for: 4 -> 12; matrix products, arithmetic and copies ran while one was open for 3% -> 1% of each run, Pallas kernels for 0% -> 2%
where the time goes in v1:
time: 184 us; the launch traced here: 183 us
  starting transfers between devices  55.5 us (30%)
  waiting for transfers between devices  53.4 us (29%)
  blocking collectives  45.8 us (25%)
  Pallas kernels  18.5 us (10%)
  local copies, waits for them, and re-layouts  4.77 us (3%)
  other arithmetic  2.85 us (2%)
    ppermute x10, starting transfers between devices, partner(): lax.ppermute(value, axis, [(source, source ^ mask) for source in range(si...  32.5 us
    all_to_all x1, blocking collectives, reduce_weights(): lax.all_to_all(piece.astype(BF).reshape(32, 3, INNER), ZY, 0, 0, tiled=True)  23.1 us
    ppermute x10, waiting for transfers between devices, partner(): lax.ppermute(value, axis, [(source, source ^ mask) for source in range(si...  21.9 us
    all_to_all x1, waiting for transfers between devices, gather_weights(): lax.all_to_all(jnp.broadcast_to(mine[None], (32, 3, D)), ZY, 0, 0, tiled=...  18.4 us
    pallas_call x3, Pallas kernels, call(): pl.pallas_call(kernel, out_shape=shapes, scratch_shapes=list(scratch), co...  18.2 us
    all_to_all x1, starting transfers between devices, gather_weights(): lax.all_to_all(jnp.broadcast_to(mine[None], (32, 3, D)), ZY, 0, 0, tiled=...  18.1 us
    all_to_all x1, blocking collectives, reduce_weights(): lax.all_to_all(both.astype(BF).reshape(8, 96, INNER), SLIDE, 0, 0, tiled=...  13.9 us
    all_to_all x1, waiting for transfers between devices, gather_weights(): lax.all_to_all(jnp.broadcast_to(rows, (8, 96, D)), SLIDE, 0, 0, tiled=True)  13.1 us
  transfers between devices with their start and end apart: 12, of which 12 were waited for; matrix products, arithmetic and copies ran while one was open for 1% of the time, Pallas kernels for 2%

profile of v1, /device:TPU:2, one launch (start us, length us, event | category | flops | bytes accessed | tf_op | source)
XLA Modules:
  0.0 183.4 jit_solution(3273709432468841366)
XLA Ops:
  0.7 0.7 fusion.94
  1.4 0.8 fusion.20
  2.9 18.1 %all-to-all-start = ((bf16[32,3,768]{2,1,0:T(4,128)(2,1)}), bf16[32,3,768]{2,1,0:T(4,128)(2,1)S(1)}, u32[]{:S(2)}, u32[]{:S(2)}) async-start(bf16[32,3,768]{2,1,0:T(4,128)(2,1)} %broadcast_in_dim.26), calls=%async_computation | async-start | bytes 393216 | tf_op jit(solution)/shard_map/all_to_all | solution.py:189
  21.9 18.4 %all-to-all-done = bf16[32,3,768]{2,1,0:T(4,128)(2,1)S(1)} async-done(((bf16[32,3,768]{2,1,0:T(4,128)(2,1)}), bf16[32,3,768]{2,1,0:T(4,128)(2,1)S(1)}, u32[]{:S(2)}, u32[]{:S(2)}) %all-to-all-start) | async-done | bytes 147488 | tf_op jit(solution)/shard_map/all_to_all | solution.py:189
  40.4 1.1 broadcast_in_dim.28
  41.5 4.9 %all-to-all-start.1 = ((bf16[8,96,768]{2,1,0:T(8,128)(2,1)}), bf16[8,96,768]{2,1,0:T(8,128)(2,1)S(1)}, u32[]{:S(2)}, u32[]{:S(2)}) async-start(bf16[8,96,768]{2,1,0:T(8,128)(2,1)} %broadcast_in_dim.28), calls=%async_computation.1 | async-start | bytes 2359296 | tf_op jit(solution)/shard_map/all_to_all | solution.py:191
  46.8 13.1 %all-to-all-done.1 = bf16[8,96,768]{2,1,0:T(8,128)(2,1)S(1)} async-done(((bf16[8,96,768]{2,1,0:T(8,128)(2,1)}), bf16[8,96,768]{2,1,0:T(8,128)(2,1)S(1)}, u32[]{:S(2)}, u32[]{:S(2)}) %all-to-all-start.1) | async-done | bytes 1179680 | tf_op jit(solution)/shard_map/all_to_all | solution.py:191
  60.0 1.9 %collective-permute-start = (bf16[768,768]{1,0:T(8,128)(2,1)S(1)}, bf16[768,768]{1,0:T(8,128)(2,1)S(1)}, u32[]{:S(2)}, u32[]{:S(2)}) collective-permute-start(bf16[768,768]{1,0:T(8,128)(2,1)S(1)} %bitcast.44), channel_id=1, source_target_pairs={{0,1},{1,0},{2,3},{3,2},{4,5},{5,4},{6,7},{7,6},{8,9},{9,8},{10,11... | collective-permute-start | bytes 3538952 | tf_op jit(solution)/shard_map/ppermute | solution.py:38
  63.3 1.4 collective-permute-done.other_ref
  65.7 2.2 %collective-permute-start.1 = (bf16[64,768]{1,0:T(8,128)(2,1)S(1)}, bf16[64,768]{1,0:T(8,128)(2,1)S(1)}, u32[]{:S(2)}, u32[]{:S(2)}) collective-permute-start(bf16[64,768]{1,0:T(8,128)(2,1)S(1)} %slice_bitcast_fusion.1.h0), channel_id=1, source_target_pairs={{0,1},{1,0},{2,3},{3,2},{4,5},{5,4},{6,7},{7,6},{8,9},{9,8},{10,11... | collective-permute-start | bytes 294920 | tf_op jit(solution)/shard_map/ppermute | solution.py:38
  67.9 1.1 collective-permute-done.1.r0
  69.1 5.4 %collective-permute-start.2 = (bf16[64,768]{1,0:T(8,128)(2,1)S(1)}, bf16[64,768]{1,0:T(8,128)(2,1)S(1)}, u32[]{:S(2)}, u32[]{:S(2)}) collective-permute-start(bf16[64,768]{1,0:T(8,128)(2,1)S(1)} %bitcast.49), channel_id=1, source_target_pairs={{0,2},{2,0},{1,3},{3,1},{4,6},{6,4},{5,7},{7,5},{8,10},{10,8},{9,1... | collective-permute-start | bytes 294920 | tf_op jit(solution)/shard_map/ppermute | solution.py:38
  74.5 3.1 %collective-permute-done.2.r1 = bf16[64,768]{1,0:T(8,128)(2,1)S(1)} collective-permute-done((bf16[64,768]{1,0:T(8,128)(2,1)S(1)}, bf16[64,768]{1,0:T(8,128)(2,1)S(1)}, u32[]{:S(2)}, u32[]{:S(2)}) %collective-permute-start.2) | collective-permute-done | bytes 98336 | tf_op jit(solution)/shard_map/ppermute | solution.py:38
  77.7 3.0 %collective-permute-start.3 = (bf16[64,768]{1,0:T(8,128)(2,1)S(1)}, bf16[64,768]{1,0:T(8,128)(2,1)S(1)}, u32[]{:S(2)}, u32[]{:S(2)}) collective-permute-start(bf16[64,768]{1,0:T(8,128)(2,1)S(1)} %bitcast.52), channel_id=1, source_target_pairs={{0,4},{4,0},{8,12},{12,8},{16,20},{20,16},{24,28},{28,24},{32,36},... | collective-permute-start | bytes 294920 | tf_op jit(solution)/shard_map/ppermute | solution.py:38
  80.7 3.4 %collective-permute-done.3.r2 = bf16[64,768]{1,0:T(8,128)(2,1)S(1)} collective-permute-done((bf16[64,768]{1,0:T(8,128)(2,1)S(1)}, bf16[64,768]{1,0:T(8,128)(2,1)S(1)}, u32[]{:S(2)}, u32[]{:S(2)}) %collective-permute-start.3) | collective-permute-done | bytes 98336 | tf_op jit(solution)/shard_map/ppermute | solution.py:38
  84.2 3.9 %collective-permute-start.4 = (bf16[64,768]{1,0:T(8,128)(2,1)S(1)}, bf16[64,768]{1,0:T(8,128)(2,1)S(1)}, u32[]{:S(2)}, u32[]{:S(2)}) collective-permute-start(bf16[64,768]{1,0:T(8,128)(2,1)S(1)} %slice_bitcast_fusion.h3), channel_id=1, source_target_pairs={{0,8},{4,12},{8,0},{12,4},{16,24},{20,28},{24,16},{28,20},{32,40},... | collective-permute-start | bytes 294920 | tf_op jit(solution)/shard_map/ppermute | solution.py:38
  88.2 4.3 %shard_map.102 = (bf16[128,384]{1,0:T(8,128)(2,1)S(1)}, bf16[128,384]{1,0:T(8,128)(2,1)S(1)}, bf16[384,768]{1,0:T(8,128)(2,1)S(1)}, bf16[768,768]{1,0:T(8,128)(2,1)S(1)}, bf16[768,384]{1,0:T(8,128)(2,1)S(1)}) custom-call(bf16[128,768]{1,0:T(8,128)(2,1)S(1)} %convolution_convert_fusion.tokens_ref, bf16[128,768]{1,0:T(8,128)(2,1)S(1)} %bitcast.55, ...), custom_call_target="tpu_custom_call" | custom-call | flops 3000000000 | bytes 4000000 | tf_op jit(solution)/shard_map/pallas_call | solution.py:171
  92.7 12.2 %shard_map.104 = (bf16[128,768]{1,0:T(8,128)(2,1)}, bf16[128,384]{1,0:T(8,128)(2,1)S(1)}, f32[384,768]{1,0:T(8,128)S(1)}, f32[640,768]{1,0:T(8,128)S(1)}) custom-call(bf16[128,384]{1,0:T(8,128)(2,1)S(1)} %get-tuple-element.15.query_ref, bf16[128,384]{1,0:T(8,128)(2,1)S(1)} %get-tuple-element.16.upstream_ref, bf16[128,768]{1,0:T(8,128)(2,1)S(1)} %shard_map.103.rows_ref, ...), custom_call_target="tpu_custom_call" | custom-call | flops 3000000000 | bytes 4000000 | tf_op jit(solution)/shard_map/pallas_call | solution.py:171
  104.9 2.8 %collective-permute-start.5 = (bf16[64,768]{1,0:T(8,128)(2,1)S(1)}, bf16[64,768]{1,0:T(8,128)(2,1)S(1)}, u32[]{:S(2)}, u32[]{:S(2)}) collective-permute-start(bf16[64,768]{1,0:T(8,128)(2,1)S(1)} %slice.211), channel_id=1, source_target_pairs={{0,8},{4,12},{8,0},{12,4},{16,24},{20,28},{24,16},{28,20},{32,40},... | collective-permute-start | bytes 294920 | tf_op jit(solution)/shard_map/ppermute | solution.py:38
  107.9 4.4 %collective-permute-done.5 = bf16[64,768]{1,0:T(8,128)(2,1)S(1)} collective-permute-done((bf16[64,768]{1,0:T(8,128)(2,1)S(1)}, bf16[64,768]{1,0:T(8,128)(2,1)S(1)}, u32[]{:S(2)}, u32[]{:S(2)}) %collective-permute-start.5) | collective-permute-done | bytes 98336 | tf_op jit(solution)/shard_map/ppermute | solution.py:38
  112.4 3.7 %collective-permute-start.6 = (bf16[64,768]{1,0:T(8,128)(2,1)S(1)}, bf16[64,768]{1,0:T(8,128)(2,1)S(1)}, u32[]{:S(2)}, u32[]{:S(2)}) collective-permute-start(bf16[64,768]{1,0:T(8,128)(2,1)S(1)} %bitcast.66), channel_id=1, source_target_pairs={{0,4},{4,0},{8,12},{12,8},{16,20},{20,16},{24,28},{28,24},{32,36},... | collective-permute-start | bytes 294920 | tf_op jit(solution)/shard_map/ppermute | solution.py:38
  116.1 2.8 %collective-permute-done.6 = bf16[64,768]{1,0:T(8,128)(2,1)S(1)} collective-permute-done((bf16[64,768]{1,0:T(8,128)(2,1)S(1)}, bf16[64,768]{1,0:T(8,128)(2,1)S(1)}, u32[]{:S(2)}, u32[]{:S(2)}) %collective-permute-start.6) | collective-permute-done | bytes 98336 | tf_op jit(solution)/shard_map/ppermute | solution.py:38
  119.0 5.5 %collective-permute-start.7 = (bf16[64,768]{1,0:T(8,128)(2,1)S(1)}, bf16[64,768]{1,0:T(8,128)(2,1)S(1)}, u32[]{:S(2)}, u32[]{:S(2)}) collective-permute-start(bf16[64,768]{1,0:T(8,128)(2,1)S(1)} %bitcast.67), channel_id=1, source_target_pairs={{0,2},{2,0},{1,3},{3,1},{4,6},{6,4},{5,7},{7,5},{8,10},{10,8},{9,1... | collective-permute-start | bytes 294920 | tf_op jit(solution)/shard_map/ppermute | solution.py:38
  124.5 2.6 %collective-permute-done.7 = bf16[64,768]{1,0:T(8,128)(2,1)S(1)} collective-permute-done((bf16[64,768]{1,0:T(8,128)(2,1)S(1)}, bf16[64,768]{1,0:T(8,128)(2,1)S(1)}, u32[]{:S(2)}, u32[]{:S(2)}) %collective-permute-start.7) | collective-permute-done | bytes 98336 | tf_op jit(solution)/shard_map/ppermute | solution.py:38
  127.1 1.9 %collective-permute-start.8 = (bf16[64,768]{1,0:T(8,128)(2,1)S(1)}, bf16[64,768]{1,0:T(8,128)(2,1)S(1)}, u32[]{:S(2)}, u32[]{:S(2)}) collective-permute-start(bf16[64,768]{1,0:T(8,128)(2,1)S(1)} %fusion.15), channel_id=1, source_target_pairs={{0,1},{1,0},{2,3},{3,2},{4,5},{5,4},{6,7},{7,6},{8,9},{9,8},{10,11... | collective-permute-start | bytes 294920 | tf_op jit(solution)/shard_map/ppermute | solution.py:38
  129.1 1.2 collective-permute-done.8
  130.4 1.7 shard_map.105
  132.1 2.1 %collective-permute-start.9 = (bf16[768,384]{1,0:T(8,128)(2,1)S(1)}, bf16[768,384]{1,0:T(8,128)(2,1)S(1)}, u32[]{:S(2)}, u32[]{:S(2)}) collective-permute-start(bf16[768,384]{1,0:T(8,128)(2,1)S(1)} %pad_maximum_fusion), channel_id=1, source_target_pairs={{0,1},{1,0},{2,3},{3,2},{4,5},{5,4},{6,7},{7,6},{8,9},{9,8},{10,11... | collective-permute-start | bytes 1769480 | tf_op jit(solution)/shard_map/ppermute | solution.py:38
  134.3 1.7 collective-permute-done.9
  136.2 13.9 %all_to_all.25 = bf16[8,96,384]{2,1,0:T(8,128)(2,1)S(1)} all-to-all(bf16[8,96,384]{2,1,0:T(8,128)(2,1)S(1)} %bitcast.57), channel_id=1, replica_groups=mesh['yl'=2,'x'=4,'z'=16,'yh'=2,'c'=2] {'yl','x'}, dimensions={0} | all-to-all | bytes 1179648 | tf_op jit(solution)/shard_map/all_to_all | solution.py:200
  150.2 23.1 %all_to_all.26 = bf16[32,3,384]{2,1,0:T(4,128)(2,1)S(1)} all-to-all(bf16[32,3,384]{2,1,0:T(4,128)(2,1)S(1)} %reshape.268), channel_id=1, replica_groups=mesh['yl'=2,'x'=4,'z'=16,'yh'=2,'c'=2] {'z','yh'}, dimensions={0} | all-to-all | bytes 147456 | tf_op jit(solution)/shard_map/all_to_all | solution.py:202
  173.4 8.8 %all_to_all.27 = f32[8,3,384]{2,1,0:T(4,128)S(1)} all-to-all(f32[8,3,384]{2,1,0:T(4,128)S(1)} %broadcast_in_dim.32), channel_id=1, replica_groups=mesh['yl'=2,'x'=4,'z'=16,'yh'=2,'c'=2] {'yl','x'}, dimensions={0} | all-to-all | bytes 73728 | tf_op jit(solution)/shard_map/all_to_all | solution.py:204
  (71 shorter events, 6.4 us)
Async XLA Ops:
  0.6 61.4 %copy-start = (bf16[1,128,768]{2,1,0:T(8,128)(2,1)S(1)}, bf16[1,128,768]{2,1,0:T(8,128)(2,1)}, u32[]{:S(2)}) copy-start(bf16[1,128,768]{2,1,0:T(8,128)(2,1)} %param.7) | copy-start | bytes 589828
  2.9 37.4 %all-to-all-start = ((bf16[32,3,768]{2,1,0:T(4,128)(2,1)}), bf16[32,3,768]{2,1,0:T(4,128)(2,1)S(1)}, u32[]{:S(2)}, u32[]{:S(2)}) async-start(bf16[32,3,768]{2,1,0:T(4,128)(2,1)} %broadcast_in_dim.26), calls=%async_computation | async-start | bytes 393216 | tf_op jit(solution)/shard_map/all_to_all | solution.py:189
  41.5 18.4 %all-to-all-start.1 = ((bf16[8,96,768]{2,1,0:T(8,128)(2,1)}), bf16[8,96,768]{2,1,0:T(8,128)(2,1)S(1)}, u32[]{:S(2)}, u32[]{:S(2)}) async-start(bf16[8,96,768]{2,1,0:T(8,128)(2,1)} %broadcast_in_dim.28), calls=%async_computation.1 | async-start | bytes 2359296 | tf_op jit(solution)/shard_map/all_to_all | solution.py:191
  60.0 4.7 %collective-permute-start = (bf16[768,768]{1,0:T(8,128)(2,1)S(1)}, bf16[768,768]{1,0:T(8,128)(2,1)S(1)}, u32[]{:S(2)}, u32[]{:S(2)}) collective-permute-start(bf16[768,768]{1,0:T(8,128)(2,1)S(1)} %bitcast.44), channel_id=1, source_target_pairs={{0,1},{1,0},{2,3},{3,2},{4,5},{5,4},{6,7},{7,6},{8,9},{9,8},{10,11... | collective-permute-start | bytes 3538952 | tf_op jit(solution)/shard_map/ppermute | solution.py:38
  64.7 1.0 copy-start.1
  65.7 22.4 %copy-start.2 = (bf16[1,128,768]{2,1,0:T(8,128)(2,1)S(1)}, bf16[1,128,768]{2,1,0:T(8,128)(2,1)}, u32[]{:S(2)}) copy-start(bf16[1,128,768]{2,1,0:T(8,128)(2,1)} %param.13) | copy-start | bytes 589828
  65.7 3.3 %collective-permute-start.1 = (bf16[64,768]{1,0:T(8,128)(2,1)S(1)}, bf16[64,768]{1,0:T(8,128)(2,1)S(1)}, u32[]{:S(2)}, u32[]{:S(2)}) collective-permute-start(bf16[64,768]{1,0:T(8,128)(2,1)S(1)} %slice_bitcast_fusion.1.h0), channel_id=1, source_target_pairs={{0,1},{1,0},{2,3},{3,2},{4,5},{5,4},{6,7},{7,6},{8,9},{9,8},{10,11... | collective-permute-start | bytes 294920 | tf_op jit(solution)/shard_map/ppermute | solution.py:38
  69.1 8.5 %collective-permute-start.2 = (bf16[64,768]{1,0:T(8,128)(2,1)S(1)}, bf16[64,768]{1,0:T(8,128)(2,1)S(1)}, u32[]{:S(2)}, u32[]{:S(2)}) collective-permute-start(bf16[64,768]{1,0:T(8,128)(2,1)S(1)} %bitcast.49), channel_id=1, source_target_pairs={{0,2},{2,0},{1,3},{3,1},{4,6},{6,4},{5,7},{7,5},{8,10},{10,8},{9,1... | collective-permute-start | bytes 294920 | tf_op jit(solution)/shard_map/ppermute | solution.py:38
  77.7 6.5 %collective-permute-start.3 = (bf16[64,768]{1,0:T(8,128)(2,1)S(1)}, bf16[64,768]{1,0:T(8,128)(2,1)S(1)}, u32[]{:S(2)}, u32[]{:S(2)}) collective-permute-start(bf16[64,768]{1,0:T(8,128)(2,1)S(1)} %bitcast.52), channel_id=1, source_target_pairs={{0,4},{4,0},{8,12},{12,8},{16,20},{20,16},{24,28},{28,24},{32,36},... | collective-permute-start | bytes 294920 | tf_op jit(solution)/shard_map/ppermute | solution.py:38
  84.2 8.5 %collective-permute-start.4 = (bf16[64,768]{1,0:T(8,128)(2,1)S(1)}, bf16[64,768]{1,0:T(8,128)(2,1)S(1)}, u32[]{:S(2)}, u32[]{:S(2)}) collective-permute-start(bf16[64,768]{1,0:T(8,128)(2,1)S(1)} %slice_bitcast_fusion.h3), channel_id=1, source_target_pairs={{0,8},{4,12},{8,0},{12,4},{16,24},{20,28},{24,16},{28,20},{32,40},... | collective-permute-start | bytes 294920 | tf_op jit(solution)/shard_map/ppermute | solution.py:38
  104.9 7.4 %collective-permute-start.5 = (bf16[64,768]{1,0:T(8,128)(2,1)S(1)}, bf16[64,768]{1,0:T(8,128)(2,1)S(1)}, u32[]{:S(2)}, u32[]{:S(2)}) collective-permute-start(bf16[64,768]{1,0:T(8,128)(2,1)S(1)} %slice.211), channel_id=1, source_target_pairs={{0,8},{4,12},{8,0},{12,4},{16,24},{20,28},{24,16},{28,20},{32,40},... | collective-permute-start | bytes 294920 | tf_op jit(solution)/shard_map/ppermute | solution.py:38
  112.4 6.5 %collective-permute-start.6 = (bf16[64,768]{1,0:T(8,128)(2,1)S(1)}, bf16[64,768]{1,0:T(8,128)(2,1)S(1)}, u32[]{:S(2)}, u32[]{:S(2)}) collective-permute-start(bf16[64,768]{1,0:T(8,128)(2,1)S(1)} %bitcast.66), channel_id=1, source_target_pairs={{0,4},{4,0},{8,12},{12,8},{16,20},{20,16},{24,28},{28,24},{32,36},... | collective-permute-start | bytes 294920 | tf_op jit(solution)/shard_map/ppermute | solution.py:38
  119.0 8.1 %collective-permute-start.7 = (bf16[64,768]{1,0:T(8,128)(2,1)S(1)}, bf16[64,768]{1,0:T(8,128)(2,1)S(1)}, u32[]{:S(2)}, u32[]{:S(2)}) collective-permute-start(bf16[64,768]{1,0:T(8,128)(2,1)S(1)} %bitcast.67), channel_id=1, source_target_pairs={{0,2},{2,0},{1,3},{3,1},{4,6},{6,4},{5,7},{7,5},{8,10},{10,8},{9,1... | collective-permute-start | bytes 294920 | tf_op jit(solution)/shard_map/ppermute | solution.py:38
  127.1 3.2 %collective-permute-start.8 = (bf16[64,768]{1,0:T(8,128)(2,1)S(1)}, bf16[64,768]{1,0:T(8,128)(2,1)S(1)}, u32[]{:S(2)}, u32[]{:S(2)}) collective-permute-start(bf16[64,768]{1,0:T(8,128)(2,1)S(1)} %fusion.15), channel_id=1, source_target_pairs={{0,1},{1,0},{2,3},{3,2},{4,5},{5,4},{6,7},{7,6},{8,9},{9,8},{10,11... | collective-permute-start | bytes 294920 | tf_op jit(solution)/shard_map/ppermute | solution.py:38
  132.1 3.9 %collective-permute-start.9 = (bf16[768,384]{1,0:T(8,128)(2,1)S(1)}, bf16[768,384]{1,0:T(8,128)(2,1)S(1)}, u32[]{:S(2)}, u32[]{:S(2)}) collective-permute-start(bf16[768,384]{1,0:T(8,128)(2,1)S(1)} %pad_maximum_fusion), channel_id=1, source_target_pairs={{0,1},{1,0},{2,3},{3,2},{4,5},{5,4},{6,7},{7,6},{8,9},{9,8},{10,11... | collective-permute-start | bytes 1769480 | tf_op jit(solution)/shard_map/ppermute | solution.py:38

commit v2 on v1

v2 whole, which is shorter than its diff:
```python
import jax
import jax.numpy as jnp
from jax import lax
from jax.experimental import pallas as pl
from jax.experimental.pallas import tpu as pltpu
from jax.sharding import Mesh, PartitionSpec as P

SCALES = 5
D = 768
INNER = 384
TOK = 128
PAIR = 2 * TOK
DIM = 48
LOCAL_HEADS = 4
HALF = LOCAL_HEADS * DIM
FAR = (SCALES - 1) * TOK
BF = jnp.bfloat16
F32 = jnp.float32
SLIDE = ("yl", "x")
Z = ("zh", "zl")
NEAR = ("zl", "yh")
PLANE = ("yl", "x", "yh", "c")
VMEM_LIMIT = 60 * 1024 * 1024


def dot(a, b):
    return jnp.dot(a, b, preferred_element_type=F32)


def dot_nt(a, b):
    return lax.dot_general(a, b, (((1,), (1,)), ((), ())), preferred_element_type=F32)


def dot_tn(a, b):
    return lax.dot_general(a, b, (((0,), (0,)), ((), ())), preferred_element_type=F32)


def partner(value, axis):
    return lax.ppermute(value, axis, [(0, 1), (1, 0)])


def reversed4(value):
    return ((value & 1) << 3) | ((value & 2) << 1) | ((value & 4) >> 1) | ((value & 8) >> 3)


def swap_rows(rows):
    lane = lax.broadcasted_iota(jnp.int32, (1, rows.shape[1]), 1)
    head = jnp.zeros_like(lane)
    for start in range(DIM, rows.shape[1], DIM):
        head = head + (lane >= start).astype(jnp.int32)
    head = jnp.broadcast_to(head, rows.shape)
    for bit in range(2):
        size = 128 >> bit
        blocks = [rows[start : start + size] for start in range(0, PAIR, size)]
        moved = jnp.concatenate([blocks[index ^ 1] for index in range(len(blocks))], 0)
        rows = jnp.where((head >> bit) & 1 == 1, moved, rows)
    return rows


def to_mixed(rows):
    return jnp.concatenate(
        [rows[block * TOK + group * 8 :][:8] for group in range(16) for block in range(2)], 0
    )


def to_split(rows):
    return jnp.concatenate(
        [rows[group * 16 + block * 8 :][:8] for block in range(2) for group in range(16)], 0
    )


def key_value_kernel(tokens_ref, weight_ref, mixed_ref, split_ref):
    rows = swap_rows(dot(tokens_ref[...], weight_ref[...]))
    mixed_ref[...] = rows.astype(BF)
    split_ref[...] = to_split(rows).astype(BF)


def query_kernel(
    low_ref, high_ref, grad_out_ref, valid_ref, order_ref, pick_ref, rest_ref,
    query_ref, query_split_ref, upstream_ref, upstream_split_ref, out_ref,
):
    query = dot(low_ref[...], rest_ref[:, :HALF]) + dot(high_ref[...], rest_ref[:, HALF:])
    query = swap_rows(query)
    query_ref[...] = query[:TOK].astype(BF)
    query_split_ref[...] = to_split(query).astype(BF)
    pick = pick_ref[...]
    out_weight = jnp.concatenate([dot(pick, rest_ref[:INNER, :]), dot(pick, rest_ref[INNER:, :])], 1)
    out_weight = out_weight.astype(BF)
    out_ref[...] = out_weight
    upstream = dot_nt(grad_out_ref[...], out_weight)
    upstream = jnp.where(valid_ref[...] > 0, upstream, 0.0).astype(BF)
    upstream = swap_rows(dot(order_ref[...], upstream))
    upstream_ref[...] = upstream[:TOK].astype(BF)
    upstream_split_ref[...] = to_split(upstream).astype(BF)


def attention_kernel(
    scalar_ref, query_ref, query_split_ref, upstream_ref, upstream_split_ref, split_ref, rows_ref,
    beside_ref, around_ref, near_position_ref, far_position_ref, limit_ref, valid_ref, order_ref,
    inner_ref, out_weight_ref, grad_out_ref,
    mixed_ref, grad_query_ref, out_part_ref, near_ref, beside_out_ref, around_out_ref,
    far_rows, far_ref, wide, attended, grad_query,
):
    scale = DIM ** -0.5
    length, start = scalar_ref[0], scalar_ref[1]
    far_rows[:TOK, :] = rows_ref[:TOK, :]
    far_rows[TOK : TOK + 64, :] = rows_ref[:64, :]
    far_rows[TOK + 64 : PAIR, :] = beside_ref[...]
    far_rows[PAIR : PAIR + TOK, :] = around_ref[pl.ds(start, 4)].reshape(TOK, INNER)
    far_rows[PAIR + TOK :, :] = around_ref[:, :16, :].reshape(TOK, INNER)
    limit = limit_ref[...]
    heads = range(LOCAL_HEADS)
    lanes = [slice(h * DIM, (h + 1) * DIM) for h in heads]
    value_lanes = [slice(HALF + h * DIM, HALF + (h + 1) * DIM) for h in heads]
    blocks = [slice(0, TOK), slice(TOK, PAIR)]

    near_scores, far_scores = [], []
    for h in heads:
        parts = []
        for b, rows in enumerate(blocks):
            scores = dot_nt(query_split_ref[rows, lanes[h]], split_ref[rows, lanes[h]]) * scale
            position = near_position_ref[b : b + 1, :] ^ h
            parts.append(jnp.where(position < length, scores, jnp.float32(-1e9)))
        near_scores.append(to_mixed(jnp.concatenate(parts, 0)))
        scores = dot_nt(query_ref[:, lanes[h]], far_rows[:, lanes[h]]) * scale
        position = far_position_ref[:1, :] ^ h
        far_scores.append(
            jnp.where(jnp.broadcast_to(position, scores.shape) < limit, scores, jnp.float32(-1e9))
        )
    near_grads, far_grads = [], []
    for h in heads:
        parts = [dot_nt(upstream_split_ref[rows, lanes[h]], split_ref[rows, value_lanes[h]]) for rows in blocks]
        near_grads.append(to_mixed(jnp.concatenate(parts, 0)))
        far_grads.append(dot_nt(upstream_ref[:, lanes[h]], far_rows[:, value_lanes[h]]))

    near_weights, far_weights, near_steps, far_steps = [], [], [], []
    for h in heads:
        top = jnp.max(near_scores[h], axis=1, keepdims=True)
        far_top = jnp.maximum(top[:TOK], jnp.max(far_scores[h], axis=1, keepdims=True))
        top = jnp.concatenate([far_top, top[TOK:]], 0)
        near = jnp.exp(near_scores[h] - top)
        far = jnp.exp(far_scores[h] - far_top)
        total = jnp.sum(near, axis=1, keepdims=True)
        total = jnp.concatenate([total[:TOK] + jnp.sum(far, axis=1, keepdims=True), total[TOK:]], 0)
        factor = 1.0 / total
        near = near * factor
        far = far * factor[:TOK]
        delta = jnp.sum(near * near_grads[h], axis=1, keepdims=True)
        far_delta = delta[:TOK] + jnp.sum(far * far_grads[h], axis=1, keepdims=True)
        delta = jnp.concatenate([far_delta, delta[TOK:]], 0)
        near_weights.append(to_split(near).astype(BF))
        far_weights.append(far.astype(BF))
        near_steps.append(to_split(near * (near_grads[h] - delta)).astype(BF))
        far_steps.append((far * (far_grads[h] - far_delta)).astype(BF))

    for h in heads:
        for target, near, far, source in (
            (attended, near_weights[h], far_weights[h], value_lanes[h]),
            (grad_query, near_steps[h], far_steps[h], lanes[h]),
        ):
            rows = jnp.concatenate([dot(near[b], split_ref[b, source]) for b in blocks], 0)
            rows = to_mixed(rows)
            far_part = dot(far, far_rows[:, source])
            rows = jnp.concatenate([rows[:TOK] + far_part, rows[TOK:]], 0)
            target[:, lanes[h]] = rows if target is attended else rows * scale
        for near, far, right, near_right, target, factor in (
            (near_steps[h], far_steps[h], query_ref, query_split_ref, lanes[h], scale),
            (near_weights[h], far_weights[h], upstream_ref, upstream_split_ref, value_lanes[h], 1.0),
        ):
            rows = jnp.concatenate([dot_tn(near[b], near_right[b, lanes[h]]) for b in blocks], 0)
            near_ref[:, target] = to_mixed(rows) * factor
            far_ref[:, target] = dot_tn(far, right[:, lanes[h]]) * factor

    near_ref[:64, :] += far_ref[:64, :] + far_ref[TOK : TOK + 64, :]
    near_ref[64:TOK, :] += far_ref[64:TOK, :]
    beside_out_ref[...] = far_ref[TOK + 64 : PAIR, :].astype(BF)
    wide[:, :16, :] = far_ref[PAIR + TOK :, :].reshape(8, 16, INNER)
    wide[:, 16:, :] = jnp.zeros((8, 16, INNER), F32)
    wide[pl.ds(start, 4)] += far_ref[PAIR : PAIR + TOK, :].reshape(4, 32, INNER)
    around_out_ref[...] = wide[...].astype(BF)

    order = order_ref[...]
    rows = swap_rows(attended[...]).astype(BF)
    rows = jnp.where(valid_ref[...] > 0, dot_tn(order, rows), 0.0).astype(BF)
    mixed_ref[...] = dot(rows, out_weight_ref[...])
    rows = dot(rows, inner_ref[...]).astype(BF)
    part = dot_tn(rows, grad_out_ref[...]).astype(BF)
    out_part_ref[:HALF, :] = part[:, :INNER]
    out_part_ref[HALF:, :] = part[:, INNER:]
    rows = swap_rows(grad_query[...]).astype(BF)
    grad_query_ref[...] = dot_tn(order, rows).astype(BF)


def value_kernel(
    near_ref, beside_ref, around_ref, order_ref, low_ref, high_ref, out_part_ref, rows_ref, part_ref
):
    first = jnp.sum(around_ref[...].astype(F32), 0)
    rows = near_ref[...]
    beside = rows[:64] + beside_ref[...].astype(F32)
    rows = jnp.concatenate([beside[:32] + first, beside[32:], rows[64:]], 0)
    rows = dot_tn(order_ref[...], swap_rows(rows).astype(BF)).astype(BF)
    rows_ref[...] = rows
    part_ref[:INNER, :HALF] = dot_tn(low_ref[...], rows[:, HALF:]).astype(BF)
    part_ref[:INNER, HALF:] = dot_tn(high_ref[...], rows[:, HALF:]).astype(BF)
    part_ref[INNER:, :] = out_part_ref[...]


def tokens_kernel(
    grad_query_ref, rows_ref, columns_ref, low_columns_ref, high_columns_ref, pair_ref, rest_ref, out_ref
):
    pair = dot(columns_ref[...], pair_ref[...]).astype(BF)
    weight = dot(low_columns_ref[...], rest_ref[:, :HALF])
    weight = (weight + dot(high_columns_ref[...], rest_ref[:, HALF:])).astype(BF)
    out_ref[...] = dot_nt(grad_query_ref[...], weight) + dot_nt(rows_ref[...], pair)


def call(kernel, shapes, *operands, scratch=(), flops=0, special={}):
    def whole(leaf):
        return pl.BlockSpec(leaf.shape, lambda step: (0,) * len(leaf.shape))

    specs = [special.get(index) or whole(leaf) for index, leaf in enumerate(operands)]
    return pl.pallas_call(
        kernel,
        grid=(1,),
        out_shape=shapes,
        in_specs=specs,
        out_specs=jax.tree.map(whole, shapes),
        scratch_shapes=list(scratch),
        compiler_params=pltpu.CompilerParams(vmem_limit_bytes=VMEM_LIMIT),
        cost_estimate=pl.CostEstimate(flops=flops, bytes_accessed=4_000_000, transcendentals=0),
    )(*operands)


PAIR_WEIGHT = pl.BlockSpec((D, INNER), lambda step: (0, 0))
REST_WEIGHT = pl.BlockSpec((D, INNER), lambda step: (1, 0))


def shape(*sizes, kind=BF):
    return jax.ShapeDtypeStruct(sizes, kind)


def gather_weights(w_query, w_key, w_value, w_out):
    yl, x = lax.axis_index("yl"), lax.axis_index("x")
    mine = None
    for index in range(4):
        rows, side = slice(3 * index, 3 * index + 3), slice((index >> 1) * INNER, (index >> 1) * INNER + INNER)
        out_rows = slice((index & 1) * 3, (index & 1) * 3 + 3)
        part = jnp.concatenate(
            [
                jnp.where(yl == 0, w_key[rows], w_query[rows]),
                jnp.where(yl == 0, w_value[rows], w_out[out_rows, side]),
            ],
            1,
        )
        mine = part if mine is None else jnp.where(x == index, part, mine)
    rows = lax.all_to_all(jnp.broadcast_to(mine[None], (16, 3, D)), Z, 0, 0, tiled=True)
    rows = rows.reshape(48, D)
    left, right = rows[:, :INNER], rows[:, INNER:]
    chunks = []
    for core in range(2):
        lanes = slice(core * HALF, (core + 1) * HALF)
        both = jnp.concatenate([left[:, lanes], right[:, lanes]], 1)
        query = jnp.concatenate([left[:24, lanes], left[24:, lanes]], 1)
        other = jnp.concatenate([query, right[core * 24 : (core + 1) * 24]], 0)
        chunks.append(jnp.where(yl == 0, both, other))
    chunks = jnp.broadcast_to(jnp.stack(chunks)[None], (16, 2, 48, INNER)).reshape(32, 48, INNER)
    return rows, lax.all_to_all(chunks, PLANE, 0, 0, tiled=True).reshape(2 * D, INNER)


def reduce_weights(part):
    pieces = lax.all_to_all(part.reshape(32, 24, INNER), PLANE, 0, 0, tiled=True).reshape(16, 2, 24, INNER)
    piece = jnp.sum(pieces.astype(F32), 0)
    value = jnp.stack(
        [jnp.concatenate([piece[0, :, lanes], piece[1, :, lanes]], 1) for lanes in (slice(0, HALF), slice(HALF, INNER))]
    )
    piece = jnp.where(lax.axis_index("yl") == 0, value, piece).astype(BF).reshape(16, 3, INNER)
    piece = jnp.sum(lax.all_to_all(piece, Z, 0, 0, tiled=True).astype(F32), 0)
    full = lax.all_to_all(jnp.broadcast_to(piece[None], (8, 3, INNER)), SLIDE, 0, 0, tiled=True)
    value_share = full[:4].reshape(12, INNER)
    out_share = jnp.concatenate([full[4:6].reshape(6, INNER), full[6:].reshape(6, INNER)], 1)
    return value_share, out_share


def one_hot(source, size):
    return (jnp.arange(size, dtype=jnp.int32)[:, None] == source[None, :]).astype(BF)


def on_device(tokens, lengths, w_query, w_key, w_value, w_out, grad_out):
    length = lengths[0]
    core, yh = lax.axis_index("c"), lax.axis_index("yh")
    zh, zl = lax.axis_index("zh"), lax.axis_index("zl")
    block = ((zh * 4 + zl) * 2 + yh) * 2 + core

    gathered, weights = gather_weights(w_query, w_key, w_value, w_out)

    own, gathered = lax.optimization_barrier((jnp.concatenate([tokens[0], grad_out[0]], 0), gathered))
    other = partner(own, "c")
    inputs = jnp.concatenate([own[:TOK], other[:TOK]], 0)
    upstream_rows = jnp.concatenate([own[TOK:], other[TOK:]], 0)

    row = jnp.arange(PAIR, dtype=jnp.int32)
    group, which = row >> 4, (row >> 3) & 1
    within = ((row & 7) << 4) + (reversed4(group) ^ (core * 4))
    order = one_hot(which * TOK + within, PAIR).T
    valid = ((block ^ (row >> 7)) * TOK + (row & 127) < length).astype(F32)[:, None]

    column = jnp.arange(D, dtype=jnp.int32)
    place, left = column // 48, column % 48
    x, middle = place >> 2, place & 3
    columns = one_hot((left // 3 * 4 + middle) * 12 + x * 3 + left % 3, D)
    low = (left // 3 * 4 + middle) * 12 + x * 3 + left % 3
    low_columns = one_hot(jnp.where(left < 24, low, -1), D)
    high_columns = one_hot(jnp.where(left < 24, low + 8 * 48, -1), D)
    column = jnp.arange(INNER, dtype=jnp.int32)
    place, left = column // 24, column % 24
    low = (left // 3 * 4 + (place & 3)) * 12 + (place >> 2) * 3 + left % 3
    low_short, high_short = one_hot(low, D), one_hot(low + 8 * 48, D)
    column = jnp.arange(HALF, dtype=jnp.int32)
    place, left = column // 24, column % 24
    inner = one_hot((left // 3 * 4 + (place & 3)) * 6 + (place >> 2) * 3 + left % 3, HALF)
    column = jnp.arange(INNER, dtype=jnp.int32)
    place, left = column // 48, column % 48 - 24
    source = (left // 3 * 4 + (place & 3)) * 6 + (place >> 2) * 3 + left % 3
    pick = one_hot(jnp.where(left >= 0, source, -1), HALF)

    def key_position(member, size):
        place = row[:size]
        return ((member ^ which[:size]) * TOK) + within[:size]

    near_position = jnp.stack([(block ^ b) * TOK + ((row[:TOK] & 7) << 4) + (reversed4(row[:TOK] >> 3) ^ (core * 4)) for b in range(2)])
    near_position = jnp.concatenate([near_position] * 4, 0)
    parts = [key_position(block, 128), key_position(block, 64), key_position(block ^ 2, 64)]
    start = (zl >> 1) * 2
    for member in range(4):
        parts.append(key_position(((zh * 4 + start + (member >> 1)) * 2 + (member & 1)) * 2 + core, 32))
    for member in range(8):
        parts.append(key_position(((zh * 4 + (member >> 1)) * 2 + (member & 1)) * 2 + core, 16))
    far_position = jnp.broadcast_to(jnp.concatenate(parts)[None], (8, FAR))
    limit = jnp.concatenate(
        [jnp.where(row[:TOK, None] < (PAIR >> scale), length, -1) + jnp.zeros((1, TOK), jnp.int32) for scale in range(1, SCALES)], 1
    )

    tokens_rows = dot(order, inputs).astype(BF)
    tokens_pair = dot(tokens_rows, columns).astype(BF)
    tokens_low, tokens_high = dot(tokens_rows, low_columns).astype(BF), dot(tokens_rows, high_columns).astype(BF)
    inputs_low, inputs_high = dot(inputs, low_short).astype(BF), dot(inputs, high_short).astype(BF)

    prepared = (
        upstream_rows, order, valid, columns, low_columns, high_columns, inner, pick, near_position, far_position,
        limit, tokens_pair, tokens_low, tokens_high, inputs_low, inputs_high,
    )
    (
        upstream_rows, order, valid, columns, low_columns, high_columns, inner, pick, near_position, far_position,
        limit, tokens_pair, tokens_low, tokens_high, inputs_low, inputs_high,
    ) = lax.optimization_barrier(prepared)

    rows, rows_split = call(
        key_value_kernel, (shape(PAIR, INNER), shape(PAIR, INNER)), tokens_pair, weights,
        special={1: PAIR_WEIGHT},
        flops=200_000_000,
    )
    around = lax.all_to_all(jnp.broadcast_to(rows[None, :32], (8, 32, INNER)), NEAR, 0, 0, tiled=True)
    beside = partner(rows[:64], "yh")

    query, query_split, upstream, upstream_split, out_weight = call(
        query_kernel,
        (shape(TOK, HALF), shape(PAIR, HALF), shape(TOK, HALF), shape(PAIR, HALF), shape(HALF, D)),
        tokens_low, tokens_high, upstream_rows, valid, order, pick, weights,
        special={6: REST_WEIGHT},
        flops=3_000_000_000,
    )

    scalars = jnp.stack([length, (zl >> 1) * 4]).astype(jnp.int32)
    mixed, grad_query, out_part, near_grads, beside, around = call(
        attention_kernel,
        (
            shape(PAIR, D, kind=F32), shape(PAIR, HALF), shape(INNER, INNER),
            shape(PAIR, INNER, kind=F32), shape(64, INNER), shape(8, 32, INNER),
        ),
        scalars, query, query_split, upstream, upstream_split, rows_split, rows, beside, around,
        near_position, far_position, limit, valid, order, inner, out_weight, upstream_rows,
        scratch=[
            pltpu.VMEM((FAR, INNER), BF), pltpu.VMEM((FAR, INNER), F32), pltpu.VMEM((8, 32, INNER), F32),
            pltpu.VMEM((PAIR, HALF), F32), pltpu.VMEM((PAIR, HALF), F32),
        ],
        special={0: pl.BlockSpec(memory_space=pltpu.SMEM)},
        flops=3_000_000_000,
    )

    around = lax.all_to_all(around, NEAR, 0, 0, tiled=True)
    beside = partner(beside, "yh")
    grad_rows, part = call(
        value_kernel,
        (shape(PAIR, INNER), shape(D, INNER)),
        near_grads, beside, around, order, inputs_low, inputs_high, out_part,
        flops=200_000_000,
    )
    value_share, out_share = reduce_weights(part)
    grad_tokens = call(
        tokens_kernel, shape(PAIR, D, kind=F32), grad_query, grad_rows, columns, low_columns, high_columns,
        weights, weights,
        special={5: PAIR_WEIGHT, 6: REST_WEIGHT},
        flops=3_000_000_000,
    )
    mixed = (mixed[:TOK] + partner(mixed[TOK:], "c")).astype(BF)
    grad_tokens = (grad_tokens[:TOK] + partner(grad_tokens[TOK:], "c")).astype(BF)
    return mixed[None], grad_tokens[None], value_share, out_share


def solution(mesh):
    fine = Mesh(mesh.devices.reshape(2, 4, 4, 4, 2, 2), ("yl", "x", "zh", "zl", "yh", "c"))
    seq = ("zh", "zl", "yh", "c")
    rows = P(seq, None)
    whole = P(SLIDE, seq, None)
    return jax.shard_map(
        on_device,
        mesh=fine,
        in_specs=(whole, P(SLIDE), rows, rows, rows, rows, whole),
        out_specs=(whole, whole, rows, rows),
        check_vma=False,
    )
```

time: 184 us -> 161 us (0.88)
  the two profiles are of different devices: /device:TPU:2 before, /device:TPU:16 now
where the time goes in v2:
time: 161 us; the launch traced here: 160 us
  starting transfers between devices  64.4 us (40%)
  waiting for transfers between devices  37 us (23%)
  Pallas kernels  24.2 us (15%)
  other arithmetic  14.3 us (9%)
  local copies, waits for them, and re-layouts  11.4 us (7%)
  matrix products  6.87 us (4%)
  between operations  1.66 us (1%)
    pallas_call x5, Pallas kernels, call(): pl.pallas_call(kernel, grid=(1,), out_shape=shapes, in_specs=specs, out_s...  24.2 us
    all_to_all x1, starting transfers between devices, gather_weights(): lax.all_to_all(jnp.broadcast_to(mine[None], (16, 3, D)), Z, 0, 0, tiled=T...  15.2 us
    all_to_all x1, waiting for transfers between devices, reduce_weights(): piece = jnp.sum(lax.all_to_all(piece, Z, 0, 0, tiled=True).astype(F32), 0)  10.9 us
    ppermute x5, starting transfers between devices, partner(): return lax.ppermute(value, axis, [(0, 1), (1, 0)])  10.4 us
    all_to_all x1, waiting for transfers between devices, gather_weights(): lax.all_to_all(chunks, PLANE, 0, 0, tiled=True).reshape(2 * D, INNER)  8.69 us
    ppermute x5, waiting for transfers between devices, partner(): return lax.ppermute(value, axis, [(0, 1), (1, 0)])  7.56 us
    all_to_all x1, starting transfers between devices, gather_weights(): lax.all_to_all(chunks, PLANE, 0, 0, tiled=True).reshape(2 * D, INNER)  7.52 us
    all_to_all x1, starting transfers between devices, on_device(): around = lax.all_to_all(around, NEAR, 0, 0, tiled=True)  7.51 us
  transfers between devices with their start and end apart: 12, of which 6 were waited for; matrix products, arithmetic and copies ran while one was open for 16% of the time, Pallas kernels for 6%

profile of v2, /device:TPU:16, one launch (start us, length us, event | category | flops | bytes accessed | tf_op | source)
XLA Modules:
  0.0 159.8 jit_solution(5328241150409489971)
XLA Ops:
  3.1 15.2 %all-to-all-start = ((bf16[16,3,768]{2,1,0:T(4,128)(2,1)}), bf16[16,3,768]{2,1,0:T(4,128)(2,1)S(1)}, u32[]{:S(2)}, u32[]{:S(2)}) async-start(bf16[16,3,768]{2,1,0:T(4,128)(2,1)} %broadcast_in_dim.31), calls=%async_computation | async-start | bytes 196608 | tf_op jit(solution)/shard_map/all_to_all | solution.py:256
  22.0 1.4 fusion.5.columns_ref
  25.3 2.3 %fusion.1 = (bf16[768,768]{1,0:T(8,128)(2,1)}, bf16[768,768]{1,0:T(8,128)(2,1)}) fusion(s32[768]{0:T(1024)S(1)} %add_select_fusion.3, s32[768]{0:T(1024)S(1)} %broadcast_select_fusion), kind=kLoop, calls=%fused_computation.2 | loop fusion | flops 2359296 | bytes 2365440 | tf_op jit(solution)/shard_map/convert_element_type | solution.py:285
  27.6 4.2 %all-to-all-done = bf16[16,3,768]{2,1,0:T(4,128)(2,1)S(1)} async-done(((bf16[16,3,768]{2,1,0:T(4,128)(2,1)}), bf16[16,3,768]{2,1,0:T(4,128)(2,1)S(1)}, u32[]{:S(2)}, u32[]{:S(2)}) %all-to-all-start) | async-done | bytes 73760 | tf_op jit(solution)/shard_map/all_to_all | solution.py:256
  32.1 1.9 %collective-permute-start = (bf16[256,768]{1,0:T(8,128)(2,1)S(1)}, bf16[256,768]{1,0:T(8,128)(2,1)S(1)}, u32[]{:S(2)}, u32[]{:S(2)}) collective-permute-start(bf16[256,768]{1,0:T(8,128)(2,1)S(1)} %pad_maximum_fusion), channel_id=1, source_target_pairs={{0,1},{1,0},{2,3},{3,2},{4,5},{5,4},{6,7},{7,6},{8,9},{9,8},{10,11... | collective-permute-start | bytes 1179656 | tf_op jit(solution)/shard_map/ppermute | solution.py:39
  34.3 1.1 broadcast_in_dim.35
  35.4 7.5 %all-to-all-start.1 = ((bf16[32,48,384]{2,1,0:T(8,128)(2,1)}), bf16[32,48,384]{2,1,0:T(8,128)(2,1)S(1)}, u32[]{:S(2)}, u32[]{:S(2)}) async-start(bf16[32,48,384]{2,1,0:T(8,128)(2,1)} %bitcast.14), calls=%async_computation.1 | async-start | bytes 2359296 | tf_op jit(solution)/shard_map/all_to_all | solution.py:267
  43.8 1.1 fusion.15.low_ref
  44.9 1.1 fusion.14.high_ref
  46.4 1.4 fusion.8.high_ref
  47.8 1.5 fusion.7.low_ref
  49.3 1.5 fusion.6.tokens_ref
  51.3 8.7 %all-to-all-done.1 = bf16[32,48,384]{2,1,0:T(8,128)(2,1)S(1)} async-done(((bf16[32,48,384]{2,1,0:T(8,128)(2,1)}), bf16[32,48,384]{2,1,0:T(8,128)(2,1)S(1)}, u32[]{:S(2)}, u32[]{:S(2)}) %all-to-all-start.1) | async-done | bytes 1179680 | tf_op jit(solution)/shard_map/all_to_all | solution.py:267
  61.0 2.3 %shard_map.103 = (bf16[256,384]{1,0:T(8,128)(2,1)}, bf16[256,384]{1,0:T(8,128)(2,1)}) custom-call(bf16[256,768]{1,0:T(8,128)(2,1)} %fusion.6.tokens_ref, bf16[1536,384]{1,0:T(8,128)(2,1)} %bitcast.50), custom_call_target="tpu_custom_call" | custom-call | flops 200000000 | bytes 4000000 | tf_op jit(solution)/shard_map/pallas_call | solution.py:222
  64.8 6.0 %all-to-all-start.2 = ((bf16[8,32,384]{2,1,0:T(8,128)(2,1)}), bf16[8,32,384]{2,1,0:T(8,128)(2,1)S(1)}, u32[]{:S(2)}, u32[]{:S(2)}) async-start(bf16[8,32,384]{2,1,0:T(8,128)(2,1)} %broadcast_in_dim.38), calls=%async_computation.2 | async-start | bytes 393216 | tf_op jit(solution)/shard_map/all_to_all | solution.py:362
  72.2 2.1 %collective-permute-start.1 = (bf16[64,384]{1,0:T(8,128)(2,1)S(1)}, bf16[64,384]{1,0:T(8,128)(2,1)S(1)}, u32[]{:S(2)}, u32[]{:S(2)}) collective-permute-start(bf16[64,384]{1,0:T(8,128)(2,1)S(1)} %slice.270), channel_id=1, source_target_pairs={{0,2},{2,0},{1,3},{3,1},{4,6},{6,4},{5,7},{7,5},{8,10},{10,8},{9,1... | collective-permute-start | bytes 147464 | tf_op jit(solution)/shard_map/ppermute | solution.py:39
  74.3 3.6 %shard_map.102 = (bf16[128,192]{1,0:T(8,128)(2,1)}, bf16[256,192]{1,0:T(8,128)(2,1)}, bf16[128,192]{1,0:T(8,128)(2,1)}, bf16[256,192]{1,0:T(8,128)(2,1)}, bf16[192,768]{1,0:T(8,128)(2,1)}) custom-call(bf16[256,768]{1,0:T(8,128)(2,1)} %fusion.7.low_ref, bf16[256,768]{1,0:T(8,128)(2,1)} %fusion.8.high_ref, bf16[256,768]{1,0:T(8,128)(2,1)} %pad_maximum_fusion.1.grad_out_ref, ...), custom_call_target="tpu_custom_call" | custom-call | flops 3000000000 | bytes 4000000 | tf_op jit(solution)/shard_map/pallas_call | solution.py:222
  77.9 1.8 %collective-permute-done.1.beside_ref = bf16[64,384]{1,0:T(8,128)(2,1)S(1)} collective-permute-done((bf16[64,384]{1,0:T(8,128)(2,1)S(1)}, bf16[64,384]{1,0:T(8,128)(2,1)S(1)}, u32[]{:S(2)}, u32[]{:S(2)}) %collective-permute-start.1) | collective-permute-done | bytes 49184 | tf_op jit(solution)/shard_map/ppermute | solution.py:39
  80.3 10.1 %shard_map.104 = (f32[256,768]{1,0:T(8,128)}, bf16[256,192]{1,0:T(8,128)(2,1)}, bf16[384,384]{1,0:T(8,128)(2,1)}, f32[256,384]{1,0:T(8,128)}, bf16[64,384]{1,0:T(8,128)(2,1)}, /*index=5*/bf16[8,32,384]{2,1,0:T(8,128)(2,1)}) custom-call(s32[2]{0:T(128)} %pad_add_fusion.1.scalar_ref, bf16[128,192]{1,0:T(8,128)(2,1)} %get-tuple-element.43.query_ref, ...), custom_call_target="tpu_custom_call" | custom-call | flops 3000000000 | bytes 4000000 | tf_op jit(solution)/shard_map/pallas_call | solution.py:222
  90.4 7.5 %all-to-all-start.3 = ((bf16[8,32,384]{2,1,0:T(8,128)(2,1)}), bf16[8,32,384]{2,1,0:T(8,128)(2,1)S(1)}, u32[]{:S(2)}, u32[]{:S(2)}) async-start(bf16[8,32,384]{2,1,0:T(8,128)(2,1)} %get-tuple-element.59), calls=%async_computation.3 | async-start | bytes 393216 | tf_op jit(solution)/shard_map/all_to_all | solution.py:390
  97.9 1.9 %collective-permute-start.3 = (bf16[64,384]{1,0:T(8,128)(2,1)}, bf16[64,384]{1,0:T(8,128)(2,1)S(1)}, u32[]{:S(2)}, u32[]{:S(2)}) collective-permute-start(bf16[64,384]{1,0:T(8,128)(2,1)} %get-tuple-element.58), channel_id=1, source_target_pairs={{0,2},{2,0},{1,3},{3,1},{4,6},{6,4},{5,7},{7,5},{8,10},{10,8},{9,1... | collective-permute-start | bytes 147464 | tf_op jit(solution)/shard_map/ppermute | solution.py:39
  99.8 5.8 %collective-permute-done.3.beside_ref = bf16[64,384]{1,0:T(8,128)(2,1)S(1)} collective-permute-done((bf16[64,384]{1,0:T(8,128)(2,1)}, bf16[64,384]{1,0:T(8,128)(2,1)S(1)}, u32[]{:S(2)}, u32[]{:S(2)}) %collective-permute-start.3) | collective-permute-done | bytes 49184 | tf_op jit(solution)/shard_map/ppermute | solution.py:39
  106.3 3.0 %shard_map.105 = (bf16[256,384]{1,0:T(8,128)(2,1)}, bf16[768,384]{1,0:T(8,128)(2,1)}) custom-call(f32[256,384]{1,0:T(8,128)} %get-tuple-element.57.near_ref, bf16[64,384]{1,0:T(8,128)(2,1)} %copy-done.7, bf16[8,32,384]{2,1,0:T(8,128)(2,1)} %copy-done.3, bf16[256,256]{1,0:T(8,128)(2,1)} %fusion.20.order_ref, bf16[256,384]{1,0:T(8,128)(2,1)} %fusion.15.low_ref, ...), custom_call_target="tpu_custom_call" | custom-call | flops 200000000 | bytes 4000000 | tf_op jit(solution)/shard_map/pallas_call | solution.py:222
  109.3 5.5 %all-to-all-start.4 = ((bf16[32,24,384]{2,1,0:T(8,128)(2,1)}), bf16[32,24,384]{2,1,0:T(8,128)(2,1)S(1)}, u32[]{:S(2)}, u32[]{:S(2)}) async-start(bf16[32,24,384]{2,1,0:T(8,128)(2,1)} %bitcast.55), calls=%async_computation.4 | async-start | bytes 1179648 | tf_op jit(solution)/shard_map/all_to_all | solution.py:271
  114.8 2.1 %collective-permute-start.2 = (f32[128,768]{1,0:T(8,128)S(1)}, f32[128,768]{1,0:T(8,128)}, u32[]{:S(2)}, u32[]{:S(2)}) collective-permute-start(f32[128,768]{1,0:T(8,128)S(1)} %slice.273), channel_id=1, source_target_pairs={{0,1},{1,0},{2,3},{3,2},{4,5},{5,4},{6,7},{7,6},{8,9},{9,8},{10,11... | collective-permute-start | bytes 1179656 | tf_op jit(solution)/shard_map/ppermute | solution.py:39
  116.8 5.3 %shard_map.106 = f32[256,768]{1,0:T(8,128)} custom-call(bf16[256,192]{1,0:T(8,128)(2,1)} %get-tuple-element.56.grad_query_ref, bf16[256,384]{1,0:T(8,128)(2,1)} %get-tuple-element.63.rows_ref, bf16[768,768]{1,0:T(8,128)(2,1)} %fusion.5.columns_ref, bf16[768,768]{1,0:T(8,128)(2,1)} %get-tuple-element.65.low_columns_ref, ...), custom_call_target="tpu_custom_call" | custom-call | flops 3000000000 | bytes 4000000 | tf_op jit(solution)/shard_map/pallas_call | solution.py:222
  123.1 2.4 %collective-permute-start.4 = (f32[128,768]{1,0:T(8,128)S(1)}, f32[128,768]{1,0:T(8,128)S(1)}, u32[]{:S(2)}, u32[]{:S(2)}) collective-permute-start(f32[128,768]{1,0:T(8,128)S(1)} %slice.296), channel_id=1, source_target_pairs={{0,1},{1,0},{2,3},{3,2},{4,5},{5,4},{6,7},{7,6},{8,9},{9,8},{10,11... | collective-permute-start | bytes 1179656 | tf_op jit(solution)/shard_map/ppermute | solution.py:39
  126.5 7.5 %all-to-all-start.5 = ((bf16[16,3,384]{2,1,0:T(4,128)(2,1)}), bf16[16,3,384]{2,1,0:T(4,128)(2,1)S(1)}, u32[]{:S(2)}, u32[]{:S(2)}) async-start(bf16[16,3,384]{2,1,0:T(4,128)(2,1)} %convert_element_type.89), calls=%async_computation.5 | async-start | bytes 98304 | tf_op jit(solution)/shard_map/all_to_all | solution.py:277
  134.0 1.7 %fusion.21 = bf16[1,128,768]{2,1,0:T(8,128)(2,1)} fusion(f32[128,768]{1,0:T(8,128)} %collective-permute-done.2, f32[256,768]{1,0:T(8,128)S(1)} %copy-done.1), kind=kLoop, calls=%fused_computation.37 | loop fusion | flops 196608 | bytes 983040 | tf_op jit(solution)/shard_map/broadcast_in_dim | solution.py:407
  135.7 10.9 %all-to-all-done.5 = bf16[16,3,384]{2,1,0:T(4,128)(2,1)S(1)} async-done(((bf16[16,3,384]{2,1,0:T(4,128)(2,1)}), bf16[16,3,384]{2,1,0:T(4,128)(2,1)S(1)}, u32[]{:S(2)}, u32[]{:S(2)}) %all-to-all-start.5) | async-done | bytes 36896 | tf_op jit(solution)/shard_map/all_to_all | solution.py:277
  147.3 4.9 %all-to-all-start.6 = ((f32[8,3,384]{2,1,0:T(4,128)}), f32[8,3,384]{2,1,0:T(4,128)S(1)}, u32[]{:S(2)}, u32[]{:S(2)}) async-start(f32[8,3,384]{2,1,0:T(4,128)} %broadcast_in_dim.41), calls=%async_computation.6 | async-start | bytes 98304 | tf_op jit(solution)/shard_map/all_to_all | solution.py:278
  153.0 5.6 %all-to-all-done.6 = f32[8,3,384]{2,1,0:T(4,128)S(1)} async-done(((f32[8,3,384]{2,1,0:T(4,128)}), f32[8,3,384]{2,1,0:T(4,128)S(1)}, u32[]{:S(2)}, u32[]{:S(2)}) %all-to-all-start.6) | async-done | bytes 36896 | tf_op jit(solution)/shard_map/all_to_all | solution.py:278
  (91 shorter events, 19.5 us)
Async XLA Ops:
  0.6 23.5 %copy-start.5 = (bf16[1,128,768]{2,1,0:T(8,128)(2,1)S(1)}, bf16[1,128,768]{2,1,0:T(8,128)(2,1)}, u32[]{:S(2)}) copy-start(bf16[1,128,768]{2,1,0:T(8,128)(2,1)} %param.13) | copy-start | bytes 589828
  0.6 23.5 %copy-start.6 = (bf16[1,128,768]{2,1,0:T(8,128)(2,1)S(1)}, bf16[1,128,768]{2,1,0:T(8,128)(2,1)}, u32[]{:S(2)}) copy-start(bf16[1,128,768]{2,1,0:T(8,128)(2,1)} %param.7) | copy-start | bytes 589828
  3.1 28.8 %all-to-all-start = ((bf16[16,3,768]{2,1,0:T(4,128)(2,1)}), bf16[16,3,768]{2,1,0:T(4,128)(2,1)S(1)}, u32[]{:S(2)}, u32[]{:S(2)}) async-start(bf16[16,3,768]{2,1,0:T(4,128)(2,1)} %broadcast_in_dim.31), calls=%async_computation | async-start | bytes 196608 | tf_op jit(solution)/shard_map/all_to_all | solution.py:256
  32.1 10.9 %collective-permute-start = (bf16[256,768]{1,0:T(8,128)(2,1)S(1)}, bf16[256,768]{1,0:T(8,128)(2,1)S(1)}, u32[]{:S(2)}, u32[]{:S(2)}) collective-permute-start(bf16[256,768]{1,0:T(8,128)(2,1)S(1)} %pad_maximum_fusion), channel_id=1, source_target_pairs={{0,1},{1,0},{2,3},{3,2},{4,5},{5,4},{6,7},{7,6},{8,9},{9,8},{10,11... | collective-permute-start | bytes 1179656 | tf_op jit(solution)/shard_map/ppermute | solution.py:39
  35.4 24.6 %all-to-all-start.1 = ((bf16[32,48,384]{2,1,0:T(8,128)(2,1)}), bf16[32,48,384]{2,1,0:T(8,128)(2,1)S(1)}, u32[]{:S(2)}, u32[]{:S(2)}) async-start(bf16[32,48,384]{2,1,0:T(8,128)(2,1)} %bitcast.14), calls=%async_computation.1 | async-start | bytes 2359296 | tf_op jit(solution)/shard_map/all_to_all | solution.py:267
  60.0 1.0 copy-start
  64.8 14.9 %all-to-all-start.2 = ((bf16[8,32,384]{2,1,0:T(8,128)(2,1)}), bf16[8,32,384]{2,1,0:T(8,128)(2,1)S(1)}, u32[]{:S(2)}, u32[]{:S(2)}) async-start(bf16[8,32,384]{2,1,0:T(8,128)(2,1)} %broadcast_in_dim.38), calls=%async_computation.2 | async-start | bytes 393216 | tf_op jit(solution)/shard_map/all_to_all | solution.py:362
  72.2 7.5 %collective-permute-start.1 = (bf16[64,384]{1,0:T(8,128)(2,1)S(1)}, bf16[64,384]{1,0:T(8,128)(2,1)S(1)}, u32[]{:S(2)}, u32[]{:S(2)}) collective-permute-start(bf16[64,384]{1,0:T(8,128)(2,1)S(1)} %slice.270), channel_id=1, source_target_pairs={{0,2},{2,0},{1,3},{3,1},{4,6},{6,4},{5,7},{7,5},{8,10},{10,8},{9,1... | collective-permute-start | bytes 147464 | tf_op jit(solution)/shard_map/ppermute | solution.py:39
  79.7 0.6 copy-start.8
  79.7 0.7 copy-start.4
  90.4 15.2 %all-to-all-start.3 = ((bf16[8,32,384]{2,1,0:T(8,128)(2,1)}), bf16[8,32,384]{2,1,0:T(8,128)(2,1)S(1)}, u32[]{:S(2)}, u32[]{:S(2)}) async-start(bf16[8,32,384]{2,1,0:T(8,128)(2,1)} %get-tuple-element.59), calls=%async_computation.3 | async-start | bytes 393216 | tf_op jit(solution)/shard_map/all_to_all | solution.py:390
  97.9 7.7 %collective-permute-start.3 = (bf16[64,384]{1,0:T(8,128)(2,1)}, bf16[64,384]{1,0:T(8,128)(2,1)S(1)}, u32[]{:S(2)}, u32[]{:S(2)}) collective-permute-start(bf16[64,384]{1,0:T(8,128)(2,1)} %get-tuple-element.58), channel_id=1, source_target_pairs={{0,2},{2,0},{1,3},{3,1},{4,6},{6,4},{5,7},{7,5},{8,10},{10,8},{9,1... | collective-permute-start | bytes 147464 | tf_op jit(solution)/shard_map/ppermute | solution.py:39
  105.6 0.6 copy-start.7
  105.6 0.7 copy-start.3
  106.3 8.4 %copy-start.1 = (f32[256,768]{1,0:T(8,128)S(1)}, f32[256,768]{1,0:T(8,128)}, u32[]{:S(2)}) copy-start(f32[256,768]{1,0:T(8,128)} %get-tuple-element.55) | copy-start | bytes 2359300
  109.3 16.3 %all-to-all-start.4 = ((bf16[32,24,384]{2,1,0:T(8,128)(2,1)}), bf16[32,24,384]{2,1,0:T(8,128)(2,1)S(1)}, u32[]{:S(2)}, u32[]{:S(2)}) async-start(bf16[32,24,384]{2,1,0:T(8,128)(2,1)} %bitcast.55), calls=%async_computation.4 | async-start | bytes 1179648 | tf_op jit(solution)/shard_map/all_to_all | solution.py:271
  114.8 19.3 %collective-permute-start.2 = (f32[128,768]{1,0:T(8,128)S(1)}, f32[128,768]{1,0:T(8,128)}, u32[]{:S(2)}, u32[]{:S(2)}) collective-permute-start(f32[128,768]{1,0:T(8,128)S(1)} %slice.273), channel_id=1, source_target_pairs={{0,1},{1,0},{2,3},{3,2},{4,5},{5,4},{6,7},{7,6},{8,9},{9,8},{10,11... | collective-permute-start | bytes 1179656 | tf_op jit(solution)/shard_map/ppermute | solution.py:39
  123.1 29.1 %copy-start.2 = (f32[256,768]{1,0:T(8,128)S(1)}, f32[256,768]{1,0:T(8,128)}, u32[]{:S(2)}) copy-start(f32[256,768]{1,0:T(8,128)} %shard_map.106) | copy-start | bytes 2359300
  123.1 29.1 %collective-permute-start.4 = (f32[128,768]{1,0:T(8,128)S(1)}, f32[128,768]{1,0:T(8,128)S(1)}, u32[]{:S(2)}, u32[]{:S(2)}) collective-permute-start(f32[128,768]{1,0:T(8,128)S(1)} %slice.296), channel_id=1, source_target_pairs={{0,1},{1,0},{2,3},{3,2},{4,5},{5,4},{6,7},{7,6},{8,9},{9,8},{10,11... | collective-permute-start | bytes 1179656 | tf_op jit(solution)/shard_map/ppermute | solution.py:39
  126.5 20.1 %all-to-all-start.5 = ((bf16[16,3,384]{2,1,0:T(4,128)(2,1)}), bf16[16,3,384]{2,1,0:T(4,128)(2,1)S(1)}, u32[]{:S(2)}, u32[]{:S(2)}) async-start(bf16[16,3,384]{2,1,0:T(4,128)(2,1)} %convert_element_type.89), calls=%async_computation.5 | async-start | bytes 98304 | tf_op jit(solution)/shard_map/all_to_all | solution.py:277
  147.3 11.2 %all-to-all-start.6 = ((f32[8,3,384]{2,1,0:T(4,128)}), f32[8,3,384]{2,1,0:T(4,128)S(1)}, u32[]{:S(2)}, u32[]{:S(2)}) async-start(f32[8,3,384]{2,1,0:T(4,128)} %broadcast_in_dim.41), calls=%async_computation.6 | async-start | bytes 98304 | tf_op jit(solution)/shard_map/all_to_all | solution.py:278

commit v3 on v2

v3 whole, which is shorter than its diff:
```python
import jax
import jax.numpy as jnp
from jax import lax
from jax.experimental import pallas as pl
from jax.experimental.pallas import tpu as pltpu
from jax.sharding import Mesh, PartitionSpec as P

D = 768
INNER = 384
TOK = 128
QUAD = 4 * TOK
DIM = 48
LOCAL_HEADS = 2
PART = LOCAL_HEADS * DIM
FAR = 3 * TOK
BF = jnp.bfloat16
F32 = jnp.float32
SLIDE = ("yl", "x")
Z = ("zh", "zl")
PLANE = ("yl", "x", "yh", "c")
VMEM_LIMIT = 60 * 1024 * 1024

SPLIT_TO_MIXED = [m * 128 + g * 8 for g in range(16) for m in range(4)]
MIXED_TO_SPLIT = [g * 32 + m * 8 for m in range(4) for g in range(16)]
PAIR_TO_MIXED = [(m >> 1) * 128 + g * 16 + (m & 1) * 8 for g in range(8) for m in range(4)]
MIXED_TO_PAIR = [g * 32 + (p * 2 + c) * 8 for p in range(2) for g in range(8) for c in range(2)]


def dot(a, b):
    return jnp.dot(a, b, preferred_element_type=F32)


def dot_nt(a, b):
    return lax.dot_general(a, b, (((1,), (1,)), ((), ())), preferred_element_type=F32)


def dot_tn(a, b):
    return lax.dot_general(a, b, (((0,), (0,)), ((), ())), preferred_element_type=F32)


def partner(value, axis):
    return lax.ppermute(value, axis, [(0, 1), (1, 0)])


def reversed4(value):
    return ((value & 1) << 3) | ((value & 2) << 1) | ((value & 4) >> 1) | ((value & 8) >> 3)


def regroup(rows, starts):
    return jnp.concatenate([rows[start : start + 8] for start in starts], 0)


def swap_rows(rows):
    lane = lax.broadcasted_iota(jnp.int32, rows.shape, 1)
    odd = (lane >= DIM) & (lane < 2 * DIM) | (lane >= 3 * DIM)
    moved = jnp.concatenate([rows[QUAD // 2 :], rows[: QUAD // 2]], 0)
    return jnp.where(odd, moved, rows)


def first_kernel(key_ref, value_ref, query_ref, out_weight_ref, out_ref):
    yl, x = lax.axis_index("yl"), lax.axis_index("x")
    query, key, value = (ref[...].astype(F32) for ref in (query_ref, key_ref, value_ref))
    out_weight = out_weight_ref[...].astype(F32)
    left = jnp.where(yl == 0, key, query)
    mine = None
    for index in range(4):
        rows = slice(3 * index, 3 * index + 3)
        out_rows = slice((index & 1) * 3, (index & 1) * 3 + 3)
        side = slice((index >> 1) * INNER, (index >> 1) * INNER + INNER)
        right = jnp.where(yl == 0, value[rows], out_weight[out_rows, side])
        part = jnp.concatenate([left[rows], right], 1)
        mine = part if mine is None else jnp.where(x == index, part, mine)
    out_ref[...] = jnp.broadcast_to(mine.astype(BF)[None], out_ref.shape)


def chunk_kernel(pieces_ref, out_ref, joined):
    yl = lax.axis_index("yl")
    for index in range(16):
        joined[3 * index : 3 * index + 3, :] = pieces_ref[index].astype(F32)
    rows = joined[...]
    for member in range(4):
        lanes = slice(member * PART, (member + 1) * PART)
        other = rows[member * 12 : (member + 1) * 12, INNER:]
        other = jnp.concatenate([other[:, q * PART : (q + 1) * PART] for q in range(4)], 0)
        right = jnp.where(yl == 0, rows[:, INNER:][:, lanes], other)
        chunk = jnp.concatenate([rows[:, lanes], right], 1).astype(BF)
        for place in range(8):
            out_ref[place, member] = chunk


def key_value_kernel(tokens_ref, weight_ref, split_ref, pair_ref, near_ref, sent_ref):
    rows = swap_rows(dot(tokens_ref[...], weight_ref[...]))
    split_ref[...] = regroup(rows, MIXED_TO_SPLIT).astype(BF)
    pair_ref[...] = regroup(rows, MIXED_TO_PAIR).astype(BF)
    near = rows[:TOK].astype(BF)
    near_ref[...] = near
    for member in range(4):
        sent_ref[member] = near[:64]


def query_kernel(
    tokens_ref, grad_out_ref, valid_ref, order_ref, pick_ref, rest_ref,
    query_split_ref, query_pair_ref, query_ref, upstream_split_ref, upstream_pair_ref, upstream_ref, out_ref,
):
    def store(rows, split_ref, pair_ref, near_ref):
        split_ref[...] = regroup(rows, MIXED_TO_SPLIT).astype(BF)
        pair_ref[...] = regroup(rows, MIXED_TO_PAIR).astype(BF)
        near_ref[...] = rows[:TOK].astype(BF)

    rest = rest_ref[...]
    query = swap_rows(dot(tokens_ref[...], rest[:, :PART]))
    store(query, query_split_ref, query_pair_ref, query_ref)
    blocks = []
    for side in range(2):
        block = dot(pick_ref[...], rest[side * INNER : (side + 1) * INNER, PART:])
        blocks += [block[q * PART : (q + 1) * PART] for q in range(4)]
    out_weight = jnp.concatenate(blocks, 1).astype(BF)
    out_ref[...] = out_weight
    upstream = dot_nt(grad_out_ref[...], out_weight)
    upstream = jnp.where(valid_ref[...] > 0, upstream, 0.0).astype(BF)
    upstream = swap_rows(dot(order_ref[...], upstream))
    store(upstream, upstream_split_ref, upstream_pair_ref, upstream_ref)


def attention_kernel(
    length_ref, query_split_ref, query_pair_ref, query_ref, upstream_split_ref, upstream_pair_ref, upstream_ref,
    split_ref, pair_ref, rows_ref, around_ref, near_position_ref, far_position_ref, limit_ref,
    attended_ref, grad_query_ref, near_ref, around_out_ref, far_rows, far_ref, wide, attended, grad_query,
):
    scale = DIM ** -0.5
    length, start = length_ref[0], (lax.axis_index("zl") >> 1) * 2
    far_rows[:TOK, :] = rows_ref[...]
    far_rows[TOK : 2 * TOK, :] = around_ref[pl.ds(start, 2)].reshape(TOK, 2 * PART)
    far_rows[2 * TOK :, :] = around_ref[:, :32, :].reshape(TOK, 2 * PART)
    limit = limit_ref[...]
    heads = range(LOCAL_HEADS)
    lanes = [slice(h * DIM, (h + 1) * DIM) for h in heads]
    value_lanes = [slice(PART + h * DIM, PART + (h + 1) * DIM) for h in heads]
    blocks = [slice(m * TOK, (m + 1) * TOK) for m in range(4)]
    pairs = blocks[:2]

    def grow(low, high, combine):
        size = low.shape[0]
        return jnp.concatenate([combine(high[:size], low), high[size:]], 0)

    scores, grads = [], []
    for h in heads:
        def masked(query, keys, position):
            position = position ^ h
            return jnp.where(position < length, dot_nt(query, keys) * scale, jnp.float32(-1e9))

        s0 = [masked(query_split_ref[b, lanes[h]], split_ref[b, lanes[h]], near_position_ref[m : m + 1, :]) for m, b in enumerate(blocks)]
        s1 = [masked(query_pair_ref[b, lanes[h]], pair_ref[b, lanes[h]], near_position_ref[4 + p : 5 + p, :]) for p, b in enumerate(pairs)]
        s2 = dot_nt(query_ref[:, lanes[h]], far_rows[:, lanes[h]]) * scale
        position = jnp.broadcast_to(far_position_ref[:1, :] ^ h, s2.shape)
        s2 = jnp.where(position < limit, s2, jnp.float32(-1e9))
        scores.append(
            [regroup(jnp.concatenate(s0, 0), SPLIT_TO_MIXED), regroup(jnp.concatenate(s1, 0), PAIR_TO_MIXED), s2]
        )
    for h in heads:
        g0 = [dot_nt(upstream_split_ref[b, lanes[h]], split_ref[b, value_lanes[h]]) for b in blocks]
        g1 = [dot_nt(upstream_pair_ref[b, lanes[h]], pair_ref[b, value_lanes[h]]) for b in pairs]
        g2 = dot_nt(upstream_ref[:, lanes[h]], far_rows[:, value_lanes[h]])
        grads.append(
            [regroup(jnp.concatenate(g0, 0), SPLIT_TO_MIXED), regroup(jnp.concatenate(g1, 0), PAIR_TO_MIXED), g2]
        )

    weights, steps = [], []
    for h in heads:
        def rows_of(values, reduce, combine):
            total = reduce(values[2], axis=1, keepdims=True)
            for value in (values[1], values[0]):
                total = grow(total, reduce(value, axis=1, keepdims=True), combine)
            return total

        top = rows_of(scores[h], jnp.max, jnp.maximum)
        expo = [jnp.exp(s - top[: s.shape[0]]) for s in scores[h]]
        factor = 1.0 / rows_of(expo, jnp.sum, jnp.add)
        probs = [e * factor[: e.shape[0]] for e in expo]
        delta = rows_of([p * g for p, g in zip(probs, grads[h])], jnp.sum, jnp.add)
        moved = [p * (g - delta[: p.shape[0]]) for p, g in zip(probs, grads[h])]
        for values, store in ((probs, weights), (moved, steps)):
            store.append(
                [
                    regroup(values[0], MIXED_TO_SPLIT).astype(BF),
                    regroup(values[1], MIXED_TO_PAIR).astype(BF),
                    values[2].astype(BF),
                ]
            )

    for h in heads:
        for target, left, source, factor in (
            (attended, weights[h], value_lanes[h], None), (grad_query, steps[h], lanes[h], scale)
        ):
            r0 = jnp.concatenate([dot(left[0][b], split_ref[b, source]) for b in blocks], 0)
            r1 = jnp.concatenate([dot(left[1][b], pair_ref[b, source]) for b in pairs], 0)
            r2 = dot(left[2], far_rows[:, source])
            rows = grow(r2, regroup(r1, PAIR_TO_MIXED), jnp.add)
            rows = grow(rows, regroup(r0, SPLIT_TO_MIXED), jnp.add)
            target[:, lanes[h]] = rows if factor is None else rows * factor
        for left, right, target, factor in (
            (steps[h], (query_split_ref, query_pair_ref, query_ref), lanes[h], scale),
            (weights[h], (upstream_split_ref, upstream_pair_ref, upstream_ref), value_lanes[h], None),
        ):
            r0 = jnp.concatenate([dot_tn(left[0][b], right[0][b, lanes[h]]) for b in blocks], 0)
            r1 = jnp.concatenate([dot_tn(left[1][b], right[1][b, lanes[h]]) for b in pairs], 0)
            r2 = dot_tn(left[2], right[2][:, lanes[h]])
            rows = grow(r2[:TOK], regroup(r1, PAIR_TO_MIXED), jnp.add)
            rows = grow(rows, regroup(r0, SPLIT_TO_MIXED), jnp.add)
            near_ref[:, target] = rows if factor is None else rows * factor
            far_ref[:, target] = r2[TOK:] if factor is None else r2[TOK:] * factor

    wide[:, :32, :] = far_ref[TOK:, :].reshape(4, 32, 2 * PART)
    wide[:, 32:, :] = jnp.zeros((4, 32, 2 * PART), F32)
    wide[pl.ds(start, 2)] += far_ref[:TOK, :].reshape(2, 64, 2 * PART)
    around_out_ref[...] = wide[...].astype(BF)
    attended_ref[...] = swap_rows(attended[...]).astype(BF)
    grad_query_ref[...] = swap_rows(grad_query[...]).astype(BF)


def finish_kernel(
    attended_ref, valid_ref, order_ref, pick_ref, grad_out_ref, rows_ref, part_ref
):
    rows = jnp.where(valid_ref[...] > 0, dot_tn(order_ref[...], attended_ref[...]), 0.0).astype(BF)
    rows_ref[...] = rows
    part = dot_tn(rows, grad_out_ref[...]).astype(BF)
    for side in range(2):
        stacked = jnp.concatenate(
            [part[:, side * INNER + q * PART : side * INNER + (q + 1) * PART] for q in range(4)], 0
        )
        part_ref[side * INNER : (side + 1) * INNER, :] = dot_tn(pick_ref[...], stacked).astype(BF)


def value_kernel(near_ref, around_ref, order_ref, tokens_ref, out_part_ref, rows_ref, part_ref):
    rows = near_ref[...]
    rows = jnp.concatenate([rows[:64] + jnp.sum(around_ref[...].astype(F32), 0), rows[64:]], 0)
    rows = dot_tn(order_ref[...], swap_rows(rows).astype(BF)).astype(BF)
    rows_ref[...] = rows
    part_ref[:D, :] = dot_tn(tokens_ref[...], rows[:, PART:]).astype(BF)
    part_ref[D:, :] = out_part_ref[...]


def middle_kernel(pieces_ref, out_ref):
    yl = lax.axis_index("yl")
    sums = [jnp.sum(pieces_ref[:, member].astype(F32), 0) for member in range(4)]
    value = jnp.concatenate(sums, 1)
    other = [
        jnp.concatenate([part[q * 12 : (q + 1) * 12] for q in range(4)], 1) for part in sums
    ]
    rows = jnp.where(yl == 0, value, jnp.concatenate(other, 0))
    for index in range(16):
        out_ref[index] = rows[3 * index : 3 * index + 3].astype(BF)


def tokens_kernel(
    attended_ref, out_weight_ref, grad_query_ref, order_ref, rows_ref, columns_ref, pair_ref, rest_ref,
    kept_ref, sent_ref,
):
    pair = dot(columns_ref[...], pair_ref[...]).astype(BF)
    query = dot(columns_ref[...], rest_ref[:, :PART]).astype(BF)
    grad_query = dot_tn(order_ref[...], grad_query_ref[...]).astype(BF)
    mixed = dot(attended_ref[...], out_weight_ref[...])
    grads = dot_nt(grad_query, query) + dot_nt(rows_ref[...], pair)
    for index, rows in enumerate((mixed, grads)):
        for side in range(2):
            start = side * 2 * TOK
            kept_ref[side, index] = rows[start : start + TOK]
            sent_ref[side, index] = rows[start + TOK : start + 2 * TOK]


SCALARS = pl.BlockSpec(memory_space=pltpu.SMEM)
PAIR_WEIGHT = pl.BlockSpec((D, 2 * PART), lambda step: (0, 0))
REST_WEIGHT = pl.BlockSpec((D, 2 * PART), lambda step: (1, 0))


def call(kernel, shapes, *operands, scratch=(), flops=0, special={}, limit=VMEM_LIMIT):
    def whole(leaf):
        return pl.BlockSpec(leaf.shape, lambda step: (0,) * len(leaf.shape))

    specs = [special.get(index) or whole(leaf) for index, leaf in enumerate(operands)]
    return pl.pallas_call(
        kernel,
        grid=(1,),
        out_shape=shapes,
        in_specs=specs,
        out_specs=jax.tree.map(whole, shapes),
        scratch_shapes=list(scratch),
        compiler_params=pltpu.CompilerParams(vmem_limit_bytes=limit),
        cost_estimate=pl.CostEstimate(flops=flops, bytes_accessed=4_000_000, transcendentals=0),
    )(*operands)


def shape(*sizes, kind=BF):
    return jax.ShapeDtypeStruct(sizes, kind)


def reduce_weights(part, kept, sent):
    pieces = lax.all_to_all(part.reshape(32, 48, PART), PLANE, 0, 0, tiled=True).reshape(8, 4, 48, PART)
    pieces, sent = lax.optimization_barrier((pieces, sent))
    both = kept + partner(sent, "c")
    beside = partner(both[1].astype(BF), "yh")
    piece = call(middle_kernel, shape(16, 3, INNER), pieces, limit=8 * 1024 * 1024)
    piece = lax.all_to_all(piece, Z, 0, 0, tiled=True)
    piece = jnp.sum(piece.astype(F32), 0)
    full = lax.all_to_all(jnp.broadcast_to(piece[None], (8, 3, INNER)), SLIDE, 0, 0, tiled=True)
    value_share = full[:4].reshape(12, INNER)
    out_share = jnp.concatenate([full[4:6].reshape(6, INNER), full[6:].reshape(6, INNER)], 1)
    mixed = (both[0, 0] + beside[0].astype(F32)).astype(BF)
    grad_tokens = (both[0, 1] + beside[1].astype(F32)).astype(BF)
    return mixed, grad_tokens, value_share, out_share


def one_hot(source, size):
    return (jnp.arange(size, dtype=jnp.int32)[:, None] == source[None, :]).astype(BF)


def on_device(tokens, lengths, w_query, w_key, w_value, w_out, grad_out):
    length = lengths[0]
    core, yh = lax.axis_index("c"), lax.axis_index("yh")
    zh, zl = lax.axis_index("zh"), lax.axis_index("zl")
    block = ((zh * 4 + zl) * 2 + yh) * 2 + core
    turn = (yh * 2 + core) * 2

    mine = call(first_kernel, shape(16, 3, D), w_key, w_value, w_query, w_out)
    tokens, grad_out, mine = lax.optimization_barrier((tokens, grad_out, mine))
    own = jnp.concatenate([tokens[0], grad_out[0]], 0)
    other = partner(own, "yh")
    rows = lax.all_to_all(mine, Z, 0, 0, tiled=True)
    own, rows, length, turn, block, zl = lax.optimization_barrier((own, rows, length, turn, block, zl))
    chunks = call(
        chunk_kernel, shape(8, 4, 48, 2 * PART), rows, scratch=[pltpu.VMEM((48, D), F32)], limit=8 * 1024 * 1024
    )
    weights = lax.all_to_all(chunks.reshape(32, 48, 2 * PART), PLANE, 0, 0, tiled=True).reshape(2 * D, 2 * PART)

    both = jnp.concatenate([own, other], 0)
    both = jnp.stack([both, partner(both, "c")]).reshape(2, 2, 2, TOK, D)
    inputs = both[:, :, 0].transpose(1, 0, 2, 3).reshape(QUAD, D)
    upstream_rows = both[:, :, 1].transpose(1, 0, 2, 3).reshape(QUAD, D)

    row = jnp.arange(QUAD, dtype=jnp.int32)
    which = (row >> 3) & 3
    within = ((row & 7) << 4) + (reversed4(row >> 5) ^ turn)
    order = one_hot(which * TOK + within, QUAD).T
    valid = ((block ^ (row >> 7)) * TOK + (row & 127) < length).astype(F32)[:, None]

    column = jnp.arange(D, dtype=jnp.int32)
    spot, left = column // 48, column % 48
    columns = one_hot((left // 3 * 4 + (spot & 3)) * 12 + (spot >> 2) * 3 + left % 3, D)
    column = jnp.arange(INNER, dtype=jnp.int32)
    spot, left = column // 48, column % 48
    inner = (left % 12 // 3 * 4 + (spot & 3)) * 6 + (spot >> 2) * 3 + left % 3
    pick = one_hot(left // 12 * PART + inner, INNER)

    def key_position(member, size):
        return ((member ^ which[:size]) * TOK) + within[:size]

    base = ((row[:TOK] & 7) << 4) + (reversed4(row[:TOK] >> 3) ^ turn)
    pair_base = ((row[:TOK] & 7) << 4) + (reversed4(row[:TOK] >> 4) ^ turn)
    near_position = [(block ^ m) * TOK + base for m in range(4)]
    near_position += [((block ^ (p * 2)) ^ ((row[:TOK] >> 3) & 1)) * TOK + pair_base for p in range(2)]
    near_position = jnp.stack(near_position + near_position[:2])
    parts = [key_position(block, TOK)]
    start = (zl >> 1) * 2
    for index in range(2):
        parts.append(key_position(((zh * 4 + start + index) * 2 + yh) * 2 + core, 64))
    for index in range(4):
        parts.append(key_position(((zh * 4 + index) * 2 + yh) * 2 + core, 32))
    far_position = jnp.broadcast_to(jnp.concatenate(parts)[None], (8, FAR))
    limit = jnp.concatenate(
        [jnp.where(row[:TOK, None] < (QUAD >> scale), length, -1) + jnp.zeros((1, TOK), jnp.int32) for scale in (2, 3, 4)], 1
    )

    inputs_columns = dot(inputs, columns).astype(BF)
    tokens_rows = dot(order, inputs_columns).astype(BF)
    (
        upstream_rows, order, valid, columns, pick, near_position, far_position, limit, inputs_columns, tokens_rows,
    ) = lax.optimization_barrier(
        (upstream_rows, order, valid, columns, pick, near_position, far_position, limit, inputs_columns, tokens_rows)
    )

    rows_split, rows_pair, rows_near, sent = call(
        key_value_kernel,
        (shape(QUAD, 2 * PART), shape(2 * TOK, 2 * PART), shape(TOK, 2 * PART), shape(4, 64, 2 * PART)),
        tokens_rows, weights,
        special={1: PAIR_WEIGHT},
        limit=8 * 1024 * 1024,
        flops=200_000_000,
    )
    around = lax.all_to_all(sent, "zl", 0, 0, tiled=True)

    parted = (shape(QUAD, PART), shape(2 * TOK, PART), shape(TOK, PART))
    *queries, out_weight = call(
        query_kernel,
        parted + parted + (shape(PART, D),),
        tokens_rows, upstream_rows, valid, order, pick, weights,
        special={5: REST_WEIGHT},
        flops=3_000_000_000,
    )

    attended, grad_query, near_grads, around = call(
        attention_kernel,
        (shape(QUAD, PART), shape(QUAD, PART), shape(QUAD, 2 * PART, kind=F32), shape(4, 64, 2 * PART)),
        lengths, *queries, rows_split, rows_pair, rows_near, around, near_position, far_position, limit,
        scratch=[
            pltpu.VMEM((FAR, 2 * PART), BF), pltpu.VMEM((2 * TOK, 2 * PART), F32), pltpu.VMEM((4, 64, 2 * PART), F32),
            pltpu.VMEM((QUAD, PART), F32), pltpu.VMEM((QUAD, PART), F32),
        ],
        special={0: SCALARS},
        flops=3_000_000_000,
    )

    around = lax.all_to_all(around, "zl", 0, 0, tiled=True)
    attended, out_part = call(
        finish_kernel,
        (shape(QUAD, PART), shape(D, PART)),
        attended, valid, order, pick, upstream_rows,
        flops=3_000_000_000,
    )
    grad_rows, part = call(
        value_kernel,
        (shape(QUAD, 2 * PART), shape(2 * D, PART)),
        near_grads, around, order, inputs_columns, out_part,
        limit=8 * 1024 * 1024,
        flops=200_000_000,
    )
    kept, sent = call(
        tokens_kernel,
        (shape(2, 2, TOK, D, kind=F32), shape(2, 2, TOK, D, kind=F32)),
        attended, out_weight, grad_query, order, grad_rows, columns, weights, weights,
        special={6: PAIR_WEIGHT, 7: REST_WEIGHT},
        flops=3_000_000_000,
    )
    mixed, grad_tokens, value_share, out_share = reduce_weights(part, kept, sent)
    return mixed[None], grad_tokens[None], value_share, out_share


def solution(mesh):
    fine = Mesh(mesh.devices.reshape(2, 4, 4, 4, 2, 2), ("yl", "x", "zh", "zl", "yh", "c"))
    seq = ("zh", "zl", "yh", "c")
    rows = P(seq, None)
    whole = P(SLIDE, seq, None)
    return jax.shard_map(
        on_device,
        mesh=fine,
        in_specs=(whole, P(SLIDE), rows, rows, rows, rows, whole),
        out_specs=(whole, whole, rows, rows),
        check_vma=False,
    )
```

time: 161 us -> 133 us (0.83)
  the two profiles are of different devices: /device:TPU:16 before, /device:TPU:2 now
where the time goes in v3:
time: 133 us; the launch traced here: 132 us
  starting transfers between devices  52.7 us (40%)
  waiting for transfers between devices  26 us (20%)
  Pallas kernels  24.6 us (18%)
  other arithmetic  9.07 us (7%)
  blocking collectives  9.03 us (7%)
  local copies, waits for them, and re-layouts  7.65 us (6%)
  between operations  1.57 us (1%)
  matrix products  1.47 us (1%)
    pallas_call x9, Pallas kernels, call(): pl.pallas_call(kernel, grid=(1,), out_shape=shapes, in_specs=specs, out_s...  24.6 us
    all_to_all x1, starting transfers between devices, on_device(): rows = lax.all_to_all(mine, Z, 0, 0, tiled=True)  15.2 us
    ppermute x4, starting transfers between devices, partner(): return lax.ppermute(value, axis, [(0, 1), (1, 0)])  12.7 us
    all_to_all x1, blocking collectives, reduce_weights(): lax.all_to_all(jnp.broadcast_to(piece[None], (8, 3, INNER)), SLIDE, 0, 0,...  9.03 us
    all_to_all x1, waiting for transfers between devices, reduce_weights(): piece = lax.all_to_all(piece, Z, 0, 0, tiled=True)  7.75 us
    all_to_all x1, starting transfers between devices, on_device(): lax.all_to_all(chunks.reshape(32, 48, 2 * PART), PLANE, 0, 0, tiled=True)  7.62 us
    all_to_all x1, starting transfers between devices, reduce_weights(): piece = lax.all_to_all(piece, Z, 0, 0, tiled=True)  5.49 us
    unnamed x23, local copies, waits for them, and re-layouts  5.34 us
  transfers between devices with their start and end apart: 10, of which 6 were waited for; matrix products, arithmetic and copies ran while one was open for 10% of the time, Pallas kernels for 11%

profile of v3, /device:TPU:2, one launch (start us, length us, event | category | flops | bytes accessed | tf_op | source)
XLA Modules:
  0.0 132.1 jit_solution(7772951861212616808)
XLA Ops:
  0.6 1.4 %shard_map.102 = bf16[16,3,768]{2,1,0:T(4,128)(2,1)} custom-call(bf16[12,384]{1,0:T(8,128)(2,1)} %key_ref.1, bf16[12,384]{1,0:T(8,128)(2,1)} %value_ref.1, bf16[12,384]{1,0:T(8,128)(2,1)} %query_ref.1, bf16[6,768]{1,0:T(8,128)(2,1)} %out_weight_ref.1), custom_call_target="tpu_custom_call" | custom-call | bytes 4000000 | tf_op jit(solution)/shard_map/pallas_call | solution.py:281
  2.1 15.2 %all-to-all-start = ((bf16[16,3,768]{2,1,0:T(4,128)(2,1)}), bf16[16,3,768]{2,1,0:T(4,128)(2,1)S(1)}, u32[]{:S(2)}, u32[]{:S(2)}) async-start(bf16[16,3,768]{2,1,0:T(4,128)(2,1)} %shard_map.102), calls=%async_computation | async-start | bytes 196608 | tf_op jit(solution)/shard_map/all_to_all | solution.py:328
  17.3 1.1 pad_maximum_fusion.1
  18.3 5.1 %collective-permute-start = (bf16[256,768]{1,0:T(8,128)(2,1)S(1)}, bf16[256,768]{1,0:T(8,128)(2,1)S(1)}, u32[]{:S(2)}, u32[]{:S(2)}) collective-permute-start(bf16[256,768]{1,0:T(8,128)(2,1)S(1)} %pad_maximum_fusion.1), channel_id=1, source_target_pairs={{0,2},{2,0},{1,3},{3,1},{4,6},{6,4},{5,7},{7,5},{8,10},{10,8},{9,1... | collective-permute-start | bytes 1179656 | tf_op jit(solution)/shard_map/ppermute | solution.py:42
  24.9 1.4 %fusion.1.columns_ref = bf16[768,768]{1,0:T(8,128)(2,1)} fusion(s32[768]{0:T(1024)S(1)} %fusion.24), kind=kLoop, calls=%fused_computation.2 | loop fusion | flops 1179648 | bytes 1182720 | tf_op jit(solution)/shard_map/convert_element_type | solution.py:314
  26.4 4.4 %all-to-all-done.pieces_ref = bf16[16,3,768]{2,1,0:T(4,128)(2,1)S(1)} async-done(((bf16[16,3,768]{2,1,0:T(4,128)(2,1)}), bf16[16,3,768]{2,1,0:T(4,128)(2,1)S(1)}, u32[]{:S(2)}, u32[]{:S(2)}) %all-to-all-start) | async-done | bytes 73760 | tf_op jit(solution)/shard_map/all_to_all | solution.py:328
  30.8 1.2 shard_map.103
  32.0 7.6 %all-to-all-start.1 = ((bf16[32,48,192]{2,1,0:T(8,128)(2,1)}), bf16[32,48,192]{2,1,0:T(8,128)(2,1)S(1)}, u32[]{:S(2)}, u32[]{:S(2)}) async-start(bf16[32,48,192]{2,1,0:T(8,128)(2,1)} %bitcast.17), calls=%async_computation.1 | async-start | bytes 1572864 | tf_op jit(solution)/shard_map/all_to_all | solution.py:333
  39.9 2.1 %collective-permute-start.1 = (bf16[512,768]{1,0:T(8,128)(2,1)S(1)}, bf16[512,768]{1,0:T(8,128)(2,1)S(1)}, u32[]{:S(2)}, u32[]{:S(2)}) collective-permute-start(bf16[512,768]{1,0:T(8,128)(2,1)S(1)} %constant_dynamic-update-slice_fusion), channel_id=1, source_target_pairs={{0,1},{1,0},{2,3},{3,2},{4,5},{5,4},{6,7},{7,6},{8,9},{9,8},{10,11... | collective-permute-start | bytes 2359304 | tf_op jit(solution)/shard_map/ppermute | solution.py:42
  44.4 0.9 fusion.4.order_ref
  45.5 0.9 copy.16
  46.5 0.8 fusion.2.tokens_ref
  48.6 4.7 %all-to-all-done.1 = bf16[32,48,192]{2,1,0:T(8,128)(2,1)S(1)} async-done(((bf16[32,48,192]{2,1,0:T(8,128)(2,1)}), bf16[32,48,192]{2,1,0:T(8,128)(2,1)S(1)}, u32[]{:S(2)}, u32[]{:S(2)}) %all-to-all-start.1) | async-done | bytes 589856 | tf_op jit(solution)/shard_map/all_to_all | solution.py:333
  53.3 1.0 shard_map.105
  56.3 3.3 %all-to-all-start.2 = ((bf16[4,64,192]{2,1,0:T(8,128)(2,1)}), bf16[4,64,192]{2,1,0:T(8,128)(2,1)S(1)}, u32[]{:S(2)}, u32[]{:S(2)}) async-start(bf16[4,64,192]{2,1,0:T(8,128)(2,1)} %get-tuple-element.69), calls=%async_computation.2 | async-start | bytes 262144 | tf_op jit(solution)/shard_map/all_to_all | solution.py:389
  59.6 3.8 %shard_map.104 = (bf16[512,96]{1,0:T(8,128)(2,1)}, bf16[256,96]{1,0:T(8,128)(2,1)}, bf16[128,96]{1,0:T(8,128)(2,1)}, bf16[512,96]{1,0:T(8,128)(2,1)}, bf16[256,9...) custom-call(bf16[512,768]{1,0:T(8,128)(2,1)} %copy-done.2, bf16[512,768]{1,0:T(8,128)(2,1)} %bitcast.55, ...), custom_call_target="tpu_custom_call" | custom-call | flops 3000000000 | bytes 4000000 | tf_op jit(solution)/shard_map/pallas_call | solution.py:281
  63.4 2.2 %all-to-all-done.2.around_ref = bf16[4,64,192]{2,1,0:T(8,128)(2,1)S(1)} async-done(((bf16[4,64,192]{2,1,0:T(8,128)(2,1)}), bf16[4,64,192]{2,1,0:T(8,128)(2,1)S(1)}, u32[]{:S(2)}, u32[]{:S(2)}) %all-to-all-start.2) | async-done | bytes 98336 | tf_op jit(solution)/shard_map/all_to_all | solution.py:389
  66.3 6.4 %shard_map.106 = (bf16[512,96]{1,0:T(8,128)(2,1)}, bf16[512,96]{1,0:T(8,128)(2,1)}, f32[512,192]{1,0:T(8,128)}, bf16[4,64,192]{2,1,0:T(8,128)(2,1)}) custom-call(s32[1]{0:T(128)} %copy.19.length_ref, bf16[512,96]{1,0:T(8,128)(2,1)} %get-tuple-element.60.query_split_ref, bf16[256,96]{1,0:T(8,128)(2,1)} %get-tuple-element.61.query_pair_ref, ...), custom_call_target="tpu_custom_call" | custom-call | flops 3000000000 | bytes 4000000 | tf_op jit(solution)/shard_map/pallas_call | solution.py:281
  72.7 3.3 %all-to-all-start.3 = ((bf16[4,64,192]{2,1,0:T(8,128)(2,1)}), bf16[4,64,192]{2,1,0:T(8,128)(2,1)S(1)}, u32[]{:S(2)}, u32[]{:S(2)}) async-start(bf16[4,64,192]{2,1,0:T(8,128)(2,1)} %get-tuple-element.78), calls=%async_computation.3 | async-start | bytes 262144 | tf_op jit(solution)/shard_map/all_to_all | solution.py:412
  76.1 3.3 %shard_map.107 = (bf16[512,96]{1,0:T(8,128)(2,1)}, bf16[768,96]{1,0:T(8,128)(2,1)}) custom-call(bf16[512,96]{1,0:T(8,128)(2,1)} %get-tuple-element.73.attended_ref, f32[512,1]{1,0:T(8,128)} %fusion.13.valid_ref, bf16[512,512]{1,0:T(8,128)(2,1)} %fusion.4.order_ref, bf16[384,384]{1,0:T(8,128)(2,1)} %fusion.6.pick_ref, bf16[512,768]{1,0:T(8,128)(2,1)} %bitcast.56), custom_call_target="tpu_custom_call" | custom-call | flops 3000000000 | bytes 4000000 | tf_op jit(solution)/shard_map/pallas_call | solution.py:281
  79.4 2.5 %all-to-all-done.3.around_ref = bf16[4,64,192]{2,1,0:T(8,128)(2,1)S(1)} async-done(((bf16[4,64,192]{2,1,0:T(8,128)(2,1)}), bf16[4,64,192]{2,1,0:T(8,128)(2,1)S(1)}, u32[]{:S(2)}, u32[]{:S(2)}) %all-to-all-start.3) | async-done | bytes 98336 | tf_op jit(solution)/shard_map/all_to_all | solution.py:412
  81.9 0.9 copy-done.4
  82.9 1.7 %shard_map.108 = (bf16[512,192]{1,0:T(8,128)(2,1)S(1)}, bf16[1536,96]{1,0:T(8,128)(2,1)}) custom-call(f32[512,192]{1,0:T(8,128)S(1)} %copy-done.3, bf16[4,64,192]{2,1,0:T(8,128)(2,1)S(1)} %all-to-all-done.3.around_ref, bf16[512,512]{1,0:T(8,128)(2,1)S(1)} %copy-done.1, bf16[512,768]{1,0:T(8,128)(2,1)S(1)} %fusion.2.tokens_ref, bf16[768,96]{1,0:T(8,128)(2,1)S(1)} %copy-done.4), custom_call_target="tpu_custom_call" | custom-call | flops 200000000 | bytes 4000000 | tf_op jit(solution)/shard_map/pallas_call | solution.py:281
  85.3 5.1 %all-to-all-start.4 = ((bf16[32,48,96]{2,1,0:T(8,128)(2,1)}), bf16[32,48,96]{2,1,0:T(8,128)(2,1)S(1)}, u32[]{:S(2)}, u32[]{:S(2)}) async-start(bf16[32,48,96]{2,1,0:T(8,128)(2,1)} %bitcast.19), calls=%async_computation.4 | async-start | bytes 786432 | tf_op jit(solution)/shard_map/all_to_all | solution.py:298
  90.3 5.0 %shard_map.109 = (f32[2,2,128,768]{3,2,1,0:T(8,128)}, f32[2,2,128,768]{3,2,1,0:T(8,128)}) custom-call(bf16[512,96]{1,0:T(8,128)(2,1)} %get-tuple-element.74.attended_ref, bf16[96,768]{1,0:T(8,128)(2,1)} %get-tuple-element.75.out_weight_ref, bf16[512,96]{1,0:T(8,128)(2,1)} %get-tuple-element.76.grad_query_ref, bf16[512,512]{1,0:T(8,128)(2,1)} %fusion.4.order_ref, ...), custom_call_target="tpu_custom_call" | custom-call | flops 3000000000 | bytes 4000000 | tf_op jit(solution)/shard_map/pallas_call | solution.py:281
  95.3 4.4 %all-to-all-done.4 = bf16[32,48,96]{2,1,0:T(8,128)(2,1)S(1)} async-done(((bf16[32,48,96]{2,1,0:T(8,128)(2,1)}), bf16[32,48,96]{2,1,0:T(8,128)(2,1)S(1)}, u32[]{:S(2)}, u32[]{:S(2)}) %all-to-all-start.4) | async-done | bytes 294944 | tf_op jit(solution)/shard_map/all_to_all | solution.py:298
  99.7 2.0 %collective-permute-start.2 = (f32[2,2,128,768]{3,2,1,0:T(8,128)}, f32[2,2,128,768]{3,2,1,0:T(8,128)S(1)}, u32[]{:S(2)}, u32[]{:S(2)}) collective-permute-start(f32[2,2,128,768]{3,2,1,0:T(8,128)} %get-tuple-element.86), channel_id=1, source_target_pairs={{0,1},{1,0},{2,3},{3,2},{4,5},{5,4},{6,7},{7,6},{8,9},{9,8},{10,11... | collective-permute-start | bytes 4718600 | tf_op jit(solution)/shard_map/ppermute | solution.py:42
  102.5 5.5 %all-to-all-start.5 = ((bf16[16,3,384]{2,1,0:T(4,128)(2,1)}), bf16[16,3,384]{2,1,0:T(4,128)(2,1)S(1)}, u32[]{:S(2)}, u32[]{:S(2)}) async-start(bf16[16,3,384]{2,1,0:T(4,128)(2,1)} %shard_map.110), calls=%async_computation.5 | async-start | bytes 98304 | tf_op jit(solution)/shard_map/all_to_all | solution.py:303
  108.0 1.6 %add.357 = f32[2,2,128,768]{3,2,1,0:T(8,128)S(1)} add(f32[2,2,128,768]{3,2,1,0:T(8,128)} %get-tuple-element.83, f32[2,2,128,768]{3,2,1,0:T(8,128)S(1)} %collective-permute-done.2) | non-fusion elementwise | flops 393216 | bytes 4718592 | tf_op jit(solution)/shard_map/add | solution.py:300
  109.7 3.5 %collective-permute-start.3 = (bf16[2,128,768]{2,1,0:T(8,128)(2,1)S(1)}, bf16[2,128,768]{2,1,0:T(8,128)(2,1)S(1)}, u32[]{:S(2)}, u32[]{:S(2)}) collective-permute-start(bf16[2,128,768]{2,1,0:T(8,128)(2,1)S(1)} %fusion.8), channel_id=1, source_target_pairs={{0,2},{2,0},{1,3},{3,1},{4,6},{6,4},{5,7},{7,5},{8,10},{10,8},{9,1... | collective-permute-start | bytes 1179656 | tf_op jit(solution)/shard_map/ppermute | solution.py:42
  113.2 7.7 %all-to-all-done.5 = bf16[16,3,384]{2,1,0:T(4,128)(2,1)S(1)} async-done(((bf16[16,3,384]{2,1,0:T(4,128)(2,1)}), bf16[16,3,384]{2,1,0:T(4,128)(2,1)S(1)}, u32[]{:S(2)}, u32[]{:S(2)}) %all-to-all-start.5) | async-done | bytes 36896 | tf_op jit(solution)/shard_map/all_to_all | solution.py:303
  121.0 9.0 %all_to_all.35 = f32[8,3,384]{2,1,0:T(4,128)S(1)} all-to-all(f32[8,3,384]{2,1,0:T(4,128)S(1)} %broadcast_in_dim.19), channel_id=1, replica_groups=mesh['yl'=2,'x'=4,'zh'=4,'zl'=4,'yh'=2,'c'=2] {'yl','x'}, dimensions={0} | all-to-all | bytes 73728 | tf_op jit(solution)/shard_map/all_to_all | solution.py:305
  (59 shorter events, 11.2 us)
Async XLA Ops:
  2.1 28.8 %all-to-all-start = ((bf16[16,3,768]{2,1,0:T(4,128)(2,1)}), bf16[16,3,768]{2,1,0:T(4,128)(2,1)S(1)}, u32[]{:S(2)}, u32[]{:S(2)}) async-start(bf16[16,3,768]{2,1,0:T(4,128)(2,1)} %shard_map.102), calls=%async_computation | async-start | bytes 196608 | tf_op jit(solution)/shard_map/all_to_all | solution.py:328
  18.3 21.5 %collective-permute-start = (bf16[256,768]{1,0:T(8,128)(2,1)S(1)}, bf16[256,768]{1,0:T(8,128)(2,1)S(1)}, u32[]{:S(2)}, u32[]{:S(2)}) collective-permute-start(bf16[256,768]{1,0:T(8,128)(2,1)S(1)} %pad_maximum_fusion.1), channel_id=1, source_target_pairs={{0,2},{2,0},{1,3},{3,1},{4,6},{6,4},{5,7},{7,5},{8,10},{10,8},{9,1... | collective-permute-start | bytes 1179656 | tf_op jit(solution)/shard_map/ppermute | solution.py:42
  32.0 21.3 %all-to-all-start.1 = ((bf16[32,48,192]{2,1,0:T(8,128)(2,1)}), bf16[32,48,192]{2,1,0:T(8,128)(2,1)S(1)}, u32[]{:S(2)}, u32[]{:S(2)}) async-start(bf16[32,48,192]{2,1,0:T(8,128)(2,1)} %bitcast.17), calls=%async_computation.1 | async-start | bytes 1572864 | tf_op jit(solution)/shard_map/all_to_all | solution.py:333
  39.9 5.5 %collective-permute-start.1 = (bf16[512,768]{1,0:T(8,128)(2,1)S(1)}, bf16[512,768]{1,0:T(8,128)(2,1)S(1)}, u32[]{:S(2)}, u32[]{:S(2)}) collective-permute-start(bf16[512,768]{1,0:T(8,128)(2,1)S(1)} %constant_dynamic-update-slice_fusion), channel_id=1, source_target_pairs={{0,1},{1,0},{2,3},{3,2},{4,5},{5,4},{6,7},{7,6},{8,9},{9,8},{10,11... | collective-permute-start | bytes 2359304 | tf_op jit(solution)/shard_map/ppermute | solution.py:42
  47.9 11.7 %copy-start.2 = (bf16[512,768]{1,0:T(8,128)(2,1)}, bf16[512,768]{1,0:T(8,128)(2,1)S(1)}, u32[]{:S(2)}) copy-start(bf16[512,768]{1,0:T(8,128)(2,1)S(1)} %convolution_convert_fusion.tokens_ref) | copy-start | bytes 2359300
  53.3 6.3 %copy-start = (bf16[32,48,192]{2,1,0:T(8,128)(2,1)}, bf16[32,48,192]{2,1,0:T(8,128)(2,1)S(1)}, u32[]{:S(2)}) copy-start(bf16[32,48,192]{2,1,0:T(8,128)(2,1)S(1)} %all-to-all-done.1) | copy-start | bytes 1769476
  54.3 0.7 copy-start.5
  55.0 0.7 copy-start.7
  55.6 0.6 copy-start.8
  56.3 9.4 %all-to-all-start.2 = ((bf16[4,64,192]{2,1,0:T(8,128)(2,1)}), bf16[4,64,192]{2,1,0:T(8,128)(2,1)S(1)}, u32[]{:S(2)}, u32[]{:S(2)}) async-start(bf16[4,64,192]{2,1,0:T(8,128)(2,1)} %get-tuple-element.69), calls=%async_computation.2 | async-start | bytes 262144 | tf_op jit(solution)/shard_map/all_to_all | solution.py:389
  65.6 0.7 copy-start.9
  72.7 9.2 %all-to-all-start.3 = ((bf16[4,64,192]{2,1,0:T(8,128)(2,1)}), bf16[4,64,192]{2,1,0:T(8,128)(2,1)S(1)}, u32[]{:S(2)}, u32[]{:S(2)}) async-start(bf16[4,64,192]{2,1,0:T(8,128)(2,1)} %get-tuple-element.78), calls=%async_computation.3 | async-start | bytes 262144 | tf_op jit(solution)/shard_map/all_to_all | solution.py:412
  76.1 5.9 %copy-start.1 = (bf16[512,512]{1,0:T(8,128)(2,1)S(1)}, bf16[512,512]{1,0:T(8,128)(2,1)}, u32[]{:S(2)}) copy-start(bf16[512,512]{1,0:T(8,128)(2,1)} %fusion.4.order_ref) | copy-start | bytes 1572868
  76.1 5.9 %copy-start.3 = (f32[512,192]{1,0:T(8,128)S(1)}, f32[512,192]{1,0:T(8,128)}, u32[]{:S(2)}) copy-start(f32[512,192]{1,0:T(8,128)} %get-tuple-element.77.near_ref) | copy-start | bytes 1179652
  81.9 0.9 copy-start.4
  84.5 0.7 copy-start.6
  85.3 14.4 %all-to-all-start.4 = ((bf16[32,48,96]{2,1,0:T(8,128)(2,1)}), bf16[32,48,96]{2,1,0:T(8,128)(2,1)S(1)}, u32[]{:S(2)}, u32[]{:S(2)}) async-start(bf16[32,48,96]{2,1,0:T(8,128)(2,1)} %bitcast.19), calls=%async_computation.4 | async-start | bytes 786432 | tf_op jit(solution)/shard_map/all_to_all | solution.py:298
  99.7 8.3 %collective-permute-start.2 = (f32[2,2,128,768]{3,2,1,0:T(8,128)}, f32[2,2,128,768]{3,2,1,0:T(8,128)S(1)}, u32[]{:S(2)}, u32[]{:S(2)}) collective-permute-start(f32[2,2,128,768]{3,2,1,0:T(8,128)} %get-tuple-element.86), channel_id=1, source_target_pairs={{0,1},{1,0},{2,3},{3,2},{4,5},{5,4},{6,7},{7,6},{8,9},{9,8},{10,11... | collective-permute-start | bytes 4718600 | tf_op jit(solution)/shard_map/ppermute | solution.py:42
  102.5 18.4 %all-to-all-start.5 = ((bf16[16,3,384]{2,1,0:T(4,128)(2,1)}), bf16[16,3,384]{2,1,0:T(4,128)(2,1)S(1)}, u32[]{:S(2)}, u32[]{:S(2)}) async-start(bf16[16,3,384]{2,1,0:T(4,128)(2,1)} %shard_map.110), calls=%async_computation.5 | async-start | bytes 98304 | tf_op jit(solution)/shard_map/all_to_all | solution.py:303
  109.7 21.6 %collective-permute-start.3 = (bf16[2,128,768]{2,1,0:T(8,128)(2,1)S(1)}, bf16[2,128,768]{2,1,0:T(8,128)(2,1)S(1)}, u32[]{:S(2)}, u32[]{:S(2)}) collective-permute-start(bf16[2,128,768]{2,1,0:T(8,128)(2,1)S(1)} %fusion.8), channel_id=1, source_target_pairs={{0,2},{2,0},{1,3},{3,1},{4,6},{6,4},{5,7},{7,5},{8,10},{10,8},{9,1... | collective-permute-start | bytes 1179656 | tf_op jit(solution)/shard_map/ppermute | solution.py:42

commit v4 on v3

v4 whole, which is shorter than its diff:
```python
import jax
import jax.numpy as jnp
from jax import lax
from jax.experimental import pallas as pl
from jax.experimental.pallas import tpu as pltpu
from jax.sharding import Mesh, PartitionSpec as P

D = 768
INNER = 384
TOK = 128
QUAD = 4 * TOK
DIM = 48
LOCAL_HEADS = 2
PART = LOCAL_HEADS * DIM
HALF = INNER // 2
STORED = QUAD + 3 * TOK
FAR = 3 * TOK
BF = jnp.bfloat16
F32 = jnp.float32
SLIDE = ("yl", "x")
Z = ("zh", "zl")
PLANE = ("yl", "x", "yh", "c")
VMEM_LIMIT = 24 * 1024 * 1024

SPLIT_TO_MIXED = [m * 128 + g * 8 for g in range(16) for m in range(4)]
MIXED_TO_SPLIT = [g * 32 + m * 8 for m in range(4) for g in range(16)]
PAIR_TO_MIXED = [(m >> 1) * 128 + g * 16 + (m & 1) * 8 for g in range(8) for m in range(4)]
MIXED_TO_PAIR = [g * 32 + (p * 2 + c) * 8 for p in range(2) for g in range(8) for c in range(2)]


def dot(a, b):
    return jnp.dot(a, b, preferred_element_type=F32)


def dot_nt(a, b):
    return lax.dot_general(a, b, (((1,), (1,)), ((), ())), preferred_element_type=F32)


def dot_tn(a, b):
    return lax.dot_general(a, b, (((0,), (0,)), ((), ())), preferred_element_type=F32)


def partner(value, axis):
    return lax.ppermute(value, axis, [(0, 1), (1, 0)])


def reversed4(value):
    return ((value & 1) << 3) | ((value & 2) << 1) | ((value & 4) >> 1) | ((value & 8) >> 3)


def regroup(rows, starts):
    return jnp.concatenate([rows[start : start + 8] for start in starts], 0)


def swap_rows(rows):
    lane = lax.broadcasted_iota(jnp.int32, rows.shape, 1)
    odd = (lane >= DIM) & (lane < 2 * DIM) | (lane >= 3 * DIM)
    moved = jnp.concatenate([rows[QUAD // 2 :], rows[: QUAD // 2]], 0)
    return jnp.where(odd, moved, rows)


def first_kernel(key_ref, value_ref, query_ref, out_weight_ref, out_ref):
    yl, x = lax.axis_index("yl"), lax.axis_index("x")
    query, key, value = (ref[...].astype(F32) for ref in (query_ref, key_ref, value_ref))
    out_weight = out_weight_ref[...].astype(F32)
    left = jnp.where(yl == 0, key, query)
    mine = None
    for index in range(4):
        rows = slice(3 * index, 3 * index + 3)
        out_rows = slice((index & 1) * 3, (index & 1) * 3 + 3)
        side = slice((index >> 1) * INNER, (index >> 1) * INNER + INNER)
        right = jnp.where(yl == 0, value[rows], out_weight[out_rows, side])
        part = jnp.concatenate([left[rows], right], 1)
        mine = part if mine is None else jnp.where(x == index, part, mine)
    out_ref[...] = jnp.broadcast_to(mine.astype(BF)[None], out_ref.shape)


def chunk_kernel(pieces_ref, out_ref, joined):
    yl = lax.axis_index("yl")
    for index in range(16):
        joined[3 * index : 3 * index + 3, :] = pieces_ref[index].astype(F32)
    rows = joined[...]
    for member in range(4):
        lanes = slice(member * PART, (member + 1) * PART)
        other = rows[member * 12 : (member + 1) * 12, INNER:]
        other = jnp.concatenate([other[:, q * PART : (q + 1) * PART] for q in range(4)], 0)
        right = jnp.where(yl == 0, rows[:, INNER:][:, lanes], other)
        chunk = jnp.concatenate([rows[:, lanes], right], 1)
        chunk = jnp.concatenate([chunk[:24], chunk[24:]], 1).astype(BF)
        for place in range(8):
            out_ref[place, member] = chunk


def project(rows, weight, lanes):
    low, high = slice(lanes.start, lanes.stop), slice(2 * PART + lanes.start, 2 * PART + lanes.stop)
    return dot(rows[:, :INNER], weight[:, low]) + dot(rows[:, INNER:], weight[:, high])


def store(out_ref, lanes, rows):
    out_ref[:QUAD, lanes] = regroup(rows, MIXED_TO_SPLIT).astype(BF)
    out_ref[QUAD : QUAD + 2 * TOK, lanes] = regroup(rows, MIXED_TO_PAIR).astype(BF)
    out_ref[QUAD + 2 * TOK :, lanes] = rows[:TOK].astype(BF)


def key_value_kernel(tokens_ref, weight_ref, out_ref, sent_ref):
    rows = swap_rows(project(tokens_ref[...], weight_ref[...], slice(0, 2 * PART)))
    store(out_ref, slice(0, 2 * PART), rows)
    for member in range(4):
        sent_ref[member] = rows[:64].astype(BF)


def query_kernel(tokens_ref, grad_out_ref, valid_ref, order_ref, pick_ref, rest_ref, rows_ref, out_ref):
    rest = rest_ref[...]
    query = swap_rows(project(tokens_ref[...], rest, slice(0, PART)))
    blocks = []
    for side in range(2):
        for lanes in (slice(PART, 2 * PART), slice(3 * PART, 4 * PART)):
            block = dot(pick_ref[...], rest[side * HALF : (side + 1) * HALF, lanes])
            blocks += [block[:PART], block[PART:]]
    out_weight = jnp.concatenate(blocks, 1).astype(BF)
    out_ref[...] = out_weight
    upstream = dot_nt(grad_out_ref[...], out_weight)
    upstream = jnp.where(valid_ref[...] > 0, upstream, 0.0).astype(BF)
    upstream = swap_rows(dot(order_ref[...], upstream))
    store(rows_ref, slice(0, 2 * PART), jnp.concatenate([query, upstream], 1))


def attention_kernel(
    length_ref, query_rows_ref, key_rows_ref, around_ref, position_ref,
    out_ref, near_ref, around_out_ref, far_rows, far_ref, wide, attended, grad_query,
):
    split, pair, near = slice(0, QUAD), slice(QUAD, QUAD + 2 * TOK), slice(QUAD + 2 * TOK, STORED)
    query_split_ref, query_pair_ref, query_ref = (query_rows_ref.at[rows] for rows in (split, pair, near))
    split_ref, pair_ref, rows_ref = (key_rows_ref.at[rows] for rows in (split, pair, near))
    scale = DIM ** -0.5
    length, start = length_ref[0], (lax.axis_index("zl") >> 1) * 2
    far_rows[:TOK, :] = rows_ref[...]
    far_rows[TOK : 2 * TOK, :] = around_ref[pl.ds(start, 2)].reshape(TOK, 2 * PART)
    far_rows[2 * TOK :, :] = around_ref[:, :32, :].reshape(TOK, 2 * PART)
    place = lax.broadcasted_iota(jnp.int32, (TOK, FAR), 0)
    lane = lax.broadcasted_iota(jnp.int32, (TOK, FAR), 1)
    used = jnp.where(lane < TOK, TOK, jnp.where(lane < 2 * TOK, TOK // 2, TOK // 4))
    limit = jnp.where(place < used, length, -1)
    heads = range(LOCAL_HEADS)
    lanes = [slice(h * DIM, (h + 1) * DIM) for h in heads]
    value_lanes = [slice(PART + h * DIM, PART + (h + 1) * DIM) for h in heads]
    blocks = [slice(m * TOK, (m + 1) * TOK) for m in range(4)]
    pairs = blocks[:2]

    def grow(low, high, combine):
        size = low.shape[0]
        return jnp.concatenate([combine(high[:size], low), high[size:]], 0)

    scores, grads = [], []
    for h in heads:
        def masked(query, keys, position):
            position = position ^ h
            return jnp.where(position < length, dot_nt(query, keys) * scale, jnp.float32(-1e9))

        s0 = [masked(query_split_ref[b, lanes[h]], split_ref[b, lanes[h]], position_ref[m : m + 1, :TOK]) for m, b in enumerate(blocks)]
        s1 = [masked(query_pair_ref[b, lanes[h]], pair_ref[b, lanes[h]], position_ref[4 + p : 5 + p, :TOK]) for p, b in enumerate(pairs)]
        s2 = dot_nt(query_ref[:, lanes[h]], far_rows[:, lanes[h]]) * scale
        position = jnp.broadcast_to(position_ref[:1, TOK:] ^ h, s2.shape)
        s2 = jnp.where(position < limit, s2, jnp.float32(-1e9))
        scores.append(
            [regroup(jnp.concatenate(s0, 0), SPLIT_TO_MIXED), regroup(jnp.concatenate(s1, 0), PAIR_TO_MIXED), s2]
        )
    for h in heads:
        g0 = [dot_nt(query_split_ref[b, value_lanes[h]], split_ref[b, value_lanes[h]]) for b in blocks]
        g1 = [dot_nt(query_pair_ref[b, value_lanes[h]], pair_ref[b, value_lanes[h]]) for b in pairs]
        g2 = dot_nt(query_ref[:, value_lanes[h]], far_rows[:, value_lanes[h]])
        grads.append(
            [regroup(jnp.concatenate(g0, 0), SPLIT_TO_MIXED), regroup(jnp.concatenate(g1, 0), PAIR_TO_MIXED), g2]
        )

    weights, steps = [], []
    for h in heads:
        def rows_of(values, reduce, combine):
            total = reduce(values[2], axis=1, keepdims=True)
            for value in (values[1], values[0]):
                total = grow(total, reduce(value, axis=1, keepdims=True), combine)
            return total

        top = rows_of(scores[h], jnp.max, jnp.maximum)
        expo = [jnp.exp(s - top[: s.shape[0]]) for s in scores[h]]
        factor = 1.0 / rows_of(expo, jnp.sum, jnp.add)
        probs = [e * factor[: e.shape[0]] for e in expo]
        delta = rows_of([p * g for p, g in zip(probs, grads[h])], jnp.sum, jnp.add)
        moved = [p * (g - delta[: p.shape[0]]) for p, g in zip(probs, grads[h])]
        for values, store in ((probs, weights), (moved, steps)):
            store.append(
                [
                    regroup(values[0], MIXED_TO_SPLIT).astype(BF),
                    regroup(values[1], MIXED_TO_PAIR).astype(BF),
                    values[2].astype(BF),
                ]
            )

    for h in heads:
        for target, left, source, factor in (
            (attended, weights[h], value_lanes[h], None), (grad_query, steps[h], lanes[h], scale)
        ):
            r0 = jnp.concatenate([dot(left[0][b], split_ref[b, source]) for b in blocks], 0)
            r1 = jnp.concatenate([dot(left[1][b], pair_ref[b, source]) for b in pairs], 0)
            r2 = dot(left[2], far_rows[:, source])
            rows = grow(r2, regroup(r1, PAIR_TO_MIXED), jnp.add)
            rows = grow(rows, regroup(r0, SPLIT_TO_MIXED), jnp.add)
            target[:, lanes[h]] = rows if factor is None else rows * factor
        for left, right, target, factor in (
            (steps[h], (query_split_ref, query_pair_ref, query_ref), lanes[h], scale),
            (weights[h], (query_split_ref, query_pair_ref, query_ref), value_lanes[h], None),
        ):
            r0 = jnp.concatenate([dot_tn(left[0][b], right[0][b, target]) for b in blocks], 0)
            r1 = jnp.concatenate([dot_tn(left[1][b], right[1][b, target]) for b in pairs], 0)
            r2 = dot_tn(left[2], right[2][:, target])
            rows = grow(r2[:TOK], regroup(r1, PAIR_TO_MIXED), jnp.add)
            rows = grow(rows, regroup(r0, SPLIT_TO_MIXED), jnp.add)
            near_ref[:, target] = rows if factor is None else rows * factor
            far_ref[:, target] = r2[TOK:] if factor is None else r2[TOK:] * factor

    wide[:, :32, :] = far_ref[TOK:, :].reshape(4, 32, 2 * PART)
    wide[:, 32:, :] = jnp.zeros((4, 32, 2 * PART), F32)
    wide[pl.ds(start, 2)] += far_ref[:TOK, :].reshape(2, 64, 2 * PART)
    around_out_ref[...] = wide[...].astype(BF)
    rows = jnp.concatenate([attended[...], grad_query[...]], 1)
    out_ref[...] = swap_rows(rows).astype(BF)


def finish_kernel(
    attended_ref, valid_ref, order_ref, pick_ref, grad_out_ref, rows_ref, part_ref
):
    rows = jnp.where(valid_ref[...] > 0, dot_tn(order_ref[...], attended_ref[:, :PART]), 0.0).astype(BF)
    rows_ref[...] = rows
    part = dot_tn(rows, grad_out_ref[...]).astype(BF)
    for side in range(2):
        for high in range(2):
            start = side * INNER + high * 2 * PART
            stacked = jnp.concatenate([part[:, start : start + PART], part[:, start + PART : start + 2 * PART]], 0)
            part_ref[side * HALF : (side + 1) * HALF, high * PART : (high + 1) * PART] = dot_tn(
                pick_ref[...], stacked
            ).astype(BF)


def value_kernel(near_ref, around_ref, tokens_ref, out_part_ref, rows_ref, part_ref):
    rows = near_ref[...]
    rows = jnp.concatenate([rows[:64] + jnp.sum(around_ref[...].astype(F32), 0), rows[64:]], 0)
    rows = swap_rows(rows).astype(BF)
    rows_ref[...] = rows
    part_ref[:INNER, :PART] = dot_tn(tokens_ref[:, :INNER], rows[:, PART:]).astype(BF)
    part_ref[:INNER, PART:] = dot_tn(tokens_ref[:, INNER:], rows[:, PART:]).astype(BF)
    part_ref[INNER:, :] = out_part_ref[...]


def middle_kernel(pieces_ref, out_ref):
    yl = lax.axis_index("yl")
    sums = [jnp.sum(pieces_ref[:, member].astype(F32), 0) for member in range(4)]
    halves = slice(0, PART), slice(PART, 2 * PART)
    value = [jnp.concatenate([part[:, lanes] for part in sums], 1) for lanes in halves]
    other = [
        jnp.concatenate([part[rows, lanes] for lanes in halves for rows in (slice(0, 12), slice(12, 24))], 1)
        for part in sums
    ]
    rows = jnp.where(yl == 0, jnp.concatenate(value, 0), jnp.concatenate(other, 0))
    for index in range(16):
        out_ref[index] = rows[3 * index : 3 * index + 3].astype(BF)


def tokens_kernel(
    attended_ref, out_weight_ref, grad_query_ref, order_ref, rows_ref, columns_ref, pair_ref, rest_ref,
    kept_ref, sent_ref,
):
    pair = project(columns_ref[...], pair_ref[...], slice(0, 2 * PART)).astype(BF)
    query = project(columns_ref[...], rest_ref[...], slice(0, PART)).astype(BF)
    order = order_ref[...]
    grad_query = dot_tn(order, grad_query_ref[:, PART:]).astype(BF)
    grad_rows = dot_tn(order, rows_ref[...]).astype(BF)
    mixed = dot(attended_ref[...], out_weight_ref[...])
    grads = dot_nt(grad_query, query) + dot_nt(grad_rows, pair)
    for index, rows in enumerate((mixed, grads)):
        for side in range(2):
            start = side * 2 * TOK
            kept_ref[side, index] = rows[start : start + TOK]
            sent_ref[side, index] = rows[start + TOK : start + 2 * TOK]


SCALARS = pl.BlockSpec(memory_space=pltpu.SMEM)
PAIR_WEIGHT = pl.BlockSpec((INNER, 4 * PART), lambda step: (0, 0))
REST_WEIGHT = pl.BlockSpec((INNER, 4 * PART), lambda step: (1, 0))


def call(kernel, shapes, *operands, scratch=(), flops=0, special={}, near=(), loose=()):
    def whole(leaf):
        return pl.BlockSpec(leaf.shape, lambda step: (0,) * len(leaf.shape))

    specs = [special.get(index) or whole(leaf) for index, leaf in enumerate(operands)]
    operands = [
        leaf if index in near or special.get(index) is SCALARS else pltpu.with_memory_space_constraint(leaf, pltpu.HBM)
        for index, leaf in enumerate(operands)
    ]
    return pl.pallas_call(
        kernel,
        grid=(1,),
        out_shape=[
            leaf if index in loose else pltpu.HBM(leaf.shape, leaf.dtype) for index, leaf in enumerate(shapes)
        ],
        in_specs=specs,
        out_specs=[whole(leaf) for leaf in shapes],
        scratch_shapes=list(scratch),
        compiler_params=pltpu.CompilerParams(vmem_limit_bytes=VMEM_LIMIT),
        cost_estimate=pl.CostEstimate(flops=flops, bytes_accessed=4_000_000, transcendentals=0),
    )(*operands)


def shape(*sizes, kind=BF):
    return jax.ShapeDtypeStruct(sizes, kind)


def reduce_weights(part, kept, sent):
    pieces = lax.all_to_all(part.reshape(32, 24, 2 * PART), PLANE, 0, 0, tiled=True).reshape(8, 4, 24, 2 * PART)
    pieces, sent = lax.optimization_barrier((pieces, sent))
    both = kept + partner(sent, "c")
    beside = partner(both[1].astype(BF), "yh")
    (piece,) = call(middle_kernel, [shape(16, 3, INNER)], pieces, near=(0,), loose=(0,))
    piece = lax.all_to_all(piece, Z, 0, 0, tiled=True)
    piece = jnp.sum(piece.astype(F32), 0)
    full = lax.all_to_all(jnp.broadcast_to(piece[None], (8, 3, INNER)), SLIDE, 0, 0, tiled=True)
    value_share = full[:4].reshape(12, INNER)
    out_share = jnp.concatenate([full[4:6].reshape(6, INNER), full[6:].reshape(6, INNER)], 1)
    mixed = (both[0, 0] + beside[0].astype(F32)).astype(BF)
    grad_tokens = (both[0, 1] + beside[1].astype(F32)).astype(BF)
    return mixed, grad_tokens, value_share, out_share


def one_hot(source, size):
    return (jnp.arange(size, dtype=jnp.int32)[:, None] == source[None, :]).astype(BF)


def on_device(tokens, lengths, w_query, w_key, w_value, w_out, grad_out):
    length = lengths[0]
    core, yh = lax.axis_index("c"), lax.axis_index("yh")
    zh, zl = lax.axis_index("zh"), lax.axis_index("zl")
    block = ((zh * 4 + zl) * 2 + yh) * 2 + core
    turn = (yh * 2 + core) * 2

    (mine,) = call(first_kernel, [shape(16, 3, D)], w_key, w_value, w_query, w_out, loose=(0,))
    tokens, grad_out, mine = lax.optimization_barrier((tokens, grad_out, mine))
    own = jnp.concatenate([tokens[0], grad_out[0]], 0)
    other = partner(own, "yh")
    rows = lax.all_to_all(mine, Z, 0, 0, tiled=True)
    own, rows, length, turn, block, zl = lax.optimization_barrier((own, rows, length, turn, block, zl))
    (chunks,) = call(
        chunk_kernel, [shape(8, 4, 24, 4 * PART)], rows, scratch=[pltpu.VMEM((48, D), F32)], near=(0,), loose=(0,)
    )
    weights = lax.all_to_all(chunks.reshape(32, 24, 4 * PART), PLANE, 0, 0, tiled=True).reshape(D, 4 * PART)

    both = jnp.concatenate([own, other], 0)
    both = jnp.stack([both, partner(both, "c")]).reshape(2, 2, 2, TOK, D)
    inputs = both[:, :, 0].transpose(1, 0, 2, 3).reshape(QUAD, D)
    upstream_rows = both[:, :, 1].transpose(1, 0, 2, 3).reshape(QUAD, D)

    row = jnp.arange(QUAD, dtype=jnp.int32)
    which = (row >> 3) & 3
    within = ((row & 7) << 4) + (reversed4(row >> 5) ^ turn)
    order = one_hot(which * TOK + within, QUAD).T
    valid = ((block ^ (row >> 7)) * TOK + (row & 127) < length).astype(F32)[:, None]

    column = jnp.arange(D, dtype=jnp.int32)
    high, spot, left = column // INNER, column % INNER // 24, column % 24
    columns = one_hot(((high * 8 + left // 3) * 4 + (spot & 3)) * 12 + (spot >> 2) * 3 + left % 3, D)
    column = jnp.arange(HALF, dtype=jnp.int32)
    spot, left = column // 24, column % 24
    inner = (left % 12 // 3 * 4 + (spot & 3)) * 6 + (spot >> 2) * 3 + left % 3
    pick = one_hot(left // 12 * PART + inner, HALF)

    def key_position(member, size):
        return ((member ^ which[:size]) * TOK) + within[:size]

    base = ((row[:TOK] & 7) << 4) + (reversed4(row[:TOK] >> 3) ^ turn)
    pair_base = ((row[:TOK] & 7) << 4) + (reversed4(row[:TOK] >> 4) ^ turn)
    near_position = [(block ^ m) * TOK + base for m in range(4)]
    near_position += [((block ^ (p * 2)) ^ ((row[:TOK] >> 3) & 1)) * TOK + pair_base for p in range(2)]
    near_position = jnp.stack(near_position + near_position[:2])
    parts = [key_position(block, TOK)]
    start = (zl >> 1) * 2
    for index in range(2):
        parts.append(key_position(((zh * 4 + start + index) * 2 + yh) * 2 + core, 64))
    for index in range(4):
        parts.append(key_position(((zh * 4 + index) * 2 + yh) * 2 + core, 32))
    far_position = jnp.broadcast_to(jnp.concatenate(parts)[None], (8, FAR))
    position = jnp.concatenate([near_position, far_position], 1)

    tokens_rows = dot(order, dot(inputs, columns).astype(BF)).astype(BF)
    (
        upstream_rows, order, valid, columns, pick, position, tokens_rows,
    ) = lax.optimization_barrier(
        (upstream_rows, order, valid, columns, pick, position, tokens_rows)
    )

    key_rows, sent = call(
        key_value_kernel,
        (shape(STORED, 2 * PART), shape(4, 64, 2 * PART)),
        tokens_rows, weights,
        special={1: PAIR_WEIGHT},
        near=(0, 1),
        loose=(1,),
        flops=200_000_000,
    )
    around = lax.all_to_all(sent, "zl", 0, 0, tiled=True)
    query_rows, out_weight = call(
        query_kernel,
        (shape(STORED, 2 * PART), shape(PART, D)),
        tokens_rows, upstream_rows, valid, order, pick, weights,
        special={5: REST_WEIGHT},
        flops=3_000_000_000,
    )

    both, near_grads, around = call(
        attention_kernel,
        (shape(QUAD, 2 * PART), shape(QUAD, 2 * PART, kind=F32), shape(4, 64, 2 * PART)),
        lengths, query_rows, key_rows, around, position,
        scratch=[
            pltpu.VMEM((FAR, 2 * PART), BF), pltpu.VMEM((2 * TOK, 2 * PART), F32), pltpu.VMEM((4, 64, 2 * PART), F32),
            pltpu.VMEM((QUAD, PART), F32), pltpu.VMEM((QUAD, PART), F32),
        ],
        special={0: SCALARS},
        near=(3,),
        loose=(2,),
        flops=3_000_000_000,
    )

    around = lax.all_to_all(around, "zl", 0, 0, tiled=True)
    attended, out_part = call(
        finish_kernel,
        (shape(QUAD, PART), shape(INNER, 2 * PART)),
        both, valid, order, pick, upstream_rows,
        flops=3_000_000_000,
    )
    grad_rows, part = call(
        value_kernel,
        (shape(QUAD, 2 * PART), shape(D, 2 * PART)),
        near_grads, around, tokens_rows, out_part,
        near=(1,),
        loose=(1,),
        flops=200_000_000,
    )
    kept, sent = call(
        tokens_kernel,
        (shape(2, 2, TOK, D, kind=F32), shape(2, 2, TOK, D, kind=F32)),
        attended, out_weight, both, order, grad_rows, columns, weights, weights,
        special={6: PAIR_WEIGHT, 7: REST_WEIGHT},
        flops=3_000_000_000,
    )
    mixed, grad_tokens, value_share, out_share = reduce_weights(part, kept, sent)
    return mixed[None], grad_tokens[None], value_share, out_share


def solution(mesh):
    fine = Mesh(mesh.devices.reshape(2, 4, 4, 4, 2, 2), ("yl", "x", "zh", "zl", "yh", "c"))
    seq = ("zh", "zl", "yh", "c")
    rows = P(seq, None)
    whole = P(SLIDE, seq, None)
    return jax.shard_map(
        on_device,
        mesh=fine,
        in_specs=(whole, P(SLIDE), rows, rows, rows, rows, whole),
        out_specs=(whole, whole, rows, rows),
        check_vma=False,
    )
```

time: 133 us -> 128 us (0.962)
  local copies, waits for them, and re-layouts: 7.65 us -> 1.93 us
  Pallas kernels: 24.6 us -> 26.8 us
  waiting for transfers between devices: 26 us -> 24.6 us
    unnamed x23 -> x7, local copies, waits for them, and re-layouts: 5.34 us -> 1.08 us
    pallas_call x9, Pallas kernels: 24.6 us -> 26.8 us  [call(): pl.pallas_call(kernel, grid=(1,), out_shape=[leaf if index in loose else...]
    all_to_all x2, waiting for transfers between devices: 9.06 us -> 7.64 us  [the longest x1 3.97 us: reduce_weights(): lax.all_to_all(part.reshape(32, 24, 2 * PART), PLANE, 0, 0, tiled=True)]
  transfers between devices with their start and end apart: 10 -> 10, of which waited for: 6 -> 6; matrix products, arithmetic and copies ran while one was open for 10% -> 9% of each run, Pallas kernels for 11% -> 12%
where the time goes in v4:
time: 128 us; the launch traced here: 127 us
  starting transfers between devices  52.5 us (41%)
  Pallas kernels  26.8 us (21%)
  waiting for transfers between devices  24.6 us (19%)
  blocking collectives  9.03 us (7%)
  other arithmetic  8.96 us (7%)
  local copies, waits for them, and re-layouts  1.93 us (2%)
  matrix products  1.8 us (1%)
  between operations  1.51 us (1%)
    pallas_call x9, Pallas kernels, call(): pl.pallas_call(kernel, grid=(1,), out_shape=[leaf if index in loose else...  26.8 us
    all_to_all x1, starting transfers between devices, on_device(): rows = lax.all_to_all(mine, Z, 0, 0, tiled=True)  15.2 us
    ppermute x4, starting transfers between devices, partner(): return lax.ppermute(value, axis, [(0, 1), (1, 0)])  12.7 us
    all_to_all x1, blocking collectives, reduce_weights(): lax.all_to_all(jnp.broadcast_to(piece[None], (8, 3, INNER)), SLIDE, 0, 0,...  9.03 us
    all_to_all x1, waiting for transfers between devices, reduce_weights(): piece = lax.all_to_all(piece, Z, 0, 0, tiled=True)  7.66 us
    all_to_all x1, starting transfers between devices, on_device(): lax.all_to_all(chunks.reshape(32, 24, 4 * PART), PLANE, 0, 0, tiled=True)  7.62 us
    all_to_all x1, starting transfers between devices, reduce_weights(): piece = lax.all_to_all(piece, Z, 0, 0, tiled=True)  5.33 us
    all_to_all x1, starting transfers between devices, reduce_weights(): lax.all_to_all(part.reshape(32, 24, 2 * PART), PLANE, 0, 0, tiled=True)  4.96 us
  transfers between devices with their start and end apart: 10, of which 6 were waited for; matrix products, arithmetic and copies ran while one was open for 9% of the time, Pallas kernels for 12%

profile of v4, /device:TPU:2, one launch (start us, length us, event | category | flops | bytes accessed | tf_op | source)
XLA Modules:
  0.0 127.0 jit_solution(18427679788560350724)
XLA Ops:
  0.6 1.4 %shard_map.102 = bf16[16,3,768]{2,1,0:T(4,128)(2,1)} custom-call(bf16[12,384]{1,0:T(8,128)(2,1)} %key_ref.1, bf16[12,384]{1,0:T(8,128)(2,1)} %value_ref.1, bf16[12,384]{1,0:T(8,128)(2,1)} %query_ref.1, bf16[6,768]{1,0:T(8,128)(2,1)} %out_weight_ref.1), custom_call_target="tpu_custom_call" | custom-call | bytes 4000000 | tf_op jit(solution)/shard_map/pallas_call | solution.py:300
  2.1 15.2 %all-to-all-start = ((bf16[16,3,768]{2,1,0:T(4,128)(2,1)}), bf16[16,3,768]{2,1,0:T(4,128)(2,1)S(1)}, u32[]{:S(2)}, u32[]{:S(2)}) async-start(bf16[16,3,768]{2,1,0:T(4,128)(2,1)} %shard_map.102), calls=%async_computation | async-start | bytes 196608 | tf_op jit(solution)/shard_map/all_to_all | solution.py:349
  17.3 1.1 pad_maximum_fusion.1
  18.3 5.1 %collective-permute-start = (bf16[256,768]{1,0:T(8,128)(2,1)S(1)}, bf16[256,768]{1,0:T(8,128)(2,1)S(1)}, u32[]{:S(2)}, u32[]{:S(2)}) collective-permute-start(bf16[256,768]{1,0:T(8,128)(2,1)S(1)} %pad_maximum_fusion.1), channel_id=1, source_target_pairs={{0,2},{2,0},{1,3},{3,1},{4,6},{6,4},{5,7},{7,5},{8,10},{10,8},{9,1... | collective-permute-start | bytes 1179656 | tf_op jit(solution)/shard_map/ppermute | solution.py:44
  24.8 1.4 %fusion.1.columns_ref = bf16[768,768]{1,0:T(8,128)(2,1)} fusion(s32[768]{0:T(1024)S(1)} %fusion.31), kind=kLoop, calls=%fused_computation.2 | loop fusion | flops 1179648 | bytes 1182720 | tf_op jit(solution)/shard_map/convert_element_type | solution.py:335
  26.2 4.6 %all-to-all-done.pieces_ref = bf16[16,3,768]{2,1,0:T(4,128)(2,1)S(1)} async-done(((bf16[16,3,768]{2,1,0:T(4,128)(2,1)}), bf16[16,3,768]{2,1,0:T(4,128)(2,1)S(1)}, u32[]{:S(2)}, u32[]{:S(2)}) %all-to-all-start) | async-done | bytes 73760 | tf_op jit(solution)/shard_map/all_to_all | solution.py:349
  30.9 1.2 shard_map.103
  32.1 7.6 %all-to-all-start.1 = ((bf16[32,24,384]{2,1,0:T(8,128)(2,1)}), bf16[32,24,384]{2,1,0:T(8,128)(2,1)S(1)}, u32[]{:S(2)}, u32[]{:S(2)}) async-start(bf16[32,24,384]{2,1,0:T(8,128)(2,1)} %bitcast.17), calls=%async_computation.1 | async-start | bytes 1179648 | tf_op jit(solution)/shard_map/all_to_all | solution.py:354
  40.0 2.1 %collective-permute-start.1 = (bf16[512,768]{1,0:T(8,128)(2,1)S(1)}, bf16[512,768]{1,0:T(8,128)(2,1)S(1)}, u32[]{:S(2)}, u32[]{:S(2)}) collective-permute-start(bf16[512,768]{1,0:T(8,128)(2,1)S(1)} %constant_dynamic-update-slice_fusion), channel_id=1, source_target_pairs={{0,1},{1,0},{2,3},{3,2},{4,5},{5,4},{6,7},{7,6},{8,9},{9,8},{10,11... | collective-permute-start | bytes 2359304 | tf_op jit(solution)/shard_map/ppermute | solution.py:44
  42.1 1.0 fusion.5.order_ref
  44.7 1.0 copy.16
  45.7 1.8 %convolution_convert_fusion.tokens_ref = bf16[512,768]{1,0:T(8,128)(2,1)S(1)} fusion(bf16[512,768]{1,0:T(8,128)(2,1)S(1)} %bitcast.55, s32[768]{0:T(1024)S(1)} %fusion.31, s32[512]{0:T(512)S(1)} %get-tuple-element.87), kind=kOutput, calls=%fused_computation.6 | convolution fusion | flops 1008271360 | bytes 1577984 | tf_op jit(solution)/shard_map/dot_general | solution.py:32
  47.5 3.7 %all-to-all-done.1 = bf16[32,24,384]{2,1,0:T(8,128)(2,1)S(1)} async-done(((bf16[32,24,384]{2,1,0:T(8,128)(2,1)}), bf16[32,24,384]{2,1,0:T(8,128)(2,1)S(1)}, u32[]{:S(2)}, u32[]{:S(2)}) %all-to-all-start.1) | async-done | bytes 589856 | tf_op jit(solution)/shard_map/all_to_all | solution.py:354
  51.1 1.3 %shard_map.105 = (bf16[896,192]{1,0:T(8,128)(2,1)}, bf16[4,64,192]{2,1,0:T(8,128)(2,1)}) custom-call(bf16[512,768]{1,0:T(8,128)(2,1)S(1)} %convolution_convert_fusion.tokens_ref, bf16[768,384]{1,0:T(8,128)(2,1)S(1)} %bitcast.47), custom_call_target="tpu_custom_call" | custom-call | flops 200000000 | bytes 4000000 | tf_op jit(solution)/shard_map/pallas_call | solution.py:300
  52.5 3.3 %all-to-all-start.2 = ((bf16[4,64,192]{2,1,0:T(8,128)(2,1)}), bf16[4,64,192]{2,1,0:T(8,128)(2,1)S(1)}, u32[]{:S(2)}, u32[]{:S(2)}) async-start(bf16[4,64,192]{2,1,0:T(8,128)(2,1)} %get-tuple-element.51), calls=%async_computation.2 | async-start | bytes 262144 | tf_op jit(solution)/shard_map/all_to_all | solution.py:408
  55.8 4.0 %shard_map.104 = (bf16[896,192]{1,0:T(8,128)(2,1)}, bf16[96,768]{1,0:T(8,128)(2,1)}) custom-call(bf16[512,768]{1,0:T(8,128)(2,1)} %copy-done, bf16[512,768]{1,0:T(8,128)(2,1)} %bitcast.53, f32[512,1]{1,0:T(8,128)} %fusion.13.valid_ref, bf16[512,512]{1,0:T(8,128)(2,1)} %fusion.5.order_ref, bf16[192,192]{1,0:T(8,128)(2,1)} %fusion.14.pick_ref, ...), custom_call_target="tpu_custom_call" | custom-call | flops 3000000000 | bytes 4000000 | tf_op jit(solution)/shard_map/pallas_call | solution.py:300
  59.8 2.2 %all-to-all-done.2.around_ref = bf16[4,64,192]{2,1,0:T(8,128)(2,1)S(1)} async-done(((bf16[4,64,192]{2,1,0:T(8,128)(2,1)}), bf16[4,64,192]{2,1,0:T(8,128)(2,1)S(1)}, u32[]{:S(2)}, u32[]{:S(2)}) %all-to-all-start.2) | async-done | bytes 98336 | tf_op jit(solution)/shard_map/all_to_all | solution.py:408
  62.0 6.6 %shard_map.106 = (bf16[512,192]{1,0:T(8,128)(2,1)}, f32[512,192]{1,0:T(8,128)}, bf16[4,64,192]{2,1,0:T(8,128)(2,1)}) custom-call(s32[1]{0:T(128)} %copy.19.length_ref, bf16[896,192]{1,0:T(8,128)(2,1)} %get-tuple-element.49.query_rows_ref, bf16[896,192]{1,0:T(8,128)(2,1)} %get-tuple-element.50.key_rows_ref, ...), custom_call_target="tpu_custom_call" | custom-call | flops 3000000000 | bytes 4000000 | tf_op jit(solution)/shard_map/pallas_call | solution.py:300
  68.6 3.3 %all-to-all-start.3 = ((bf16[4,64,192]{2,1,0:T(8,128)(2,1)}), bf16[4,64,192]{2,1,0:T(8,128)(2,1)S(1)}, u32[]{:S(2)}, u32[]{:S(2)}) async-start(bf16[4,64,192]{2,1,0:T(8,128)(2,1)} %get-tuple-element.57), calls=%async_computation.3 | async-start | bytes 262144 | tf_op jit(solution)/shard_map/all_to_all | solution.py:431
  71.9 3.4 %shard_map.107 = (bf16[512,96]{1,0:T(8,128)(2,1)}, bf16[384,192]{1,0:T(8,128)(2,1)}) custom-call(bf16[512,192]{1,0:T(8,128)(2,1)} %get-tuple-element.53.attended_ref.grad_query_ref, f32[512,1]{1,0:T(8,128)} %fusion.13.valid_ref, bf16[512,512]{1,0:T(8,128)(2,1)} %fusion.5.order_ref, bf16[192,192]{1,0:T(8,128)(2,1)} %fusion.14.pick_ref, bf16[512,768]{1,0:T(8,128)(2,1)} %bitcast.54), custom_call_target="tpu_custom_call" | custom-call | flops 3000000000 | bytes 4000000 | tf_op jit(solution)/shard_map/pallas_call | solution.py:300
  75.3 2.5 %all-to-all-done.3.around_ref = bf16[4,64,192]{2,1,0:T(8,128)(2,1)S(1)} async-done(((bf16[4,64,192]{2,1,0:T(8,128)(2,1)}), bf16[4,64,192]{2,1,0:T(8,128)(2,1)S(1)}, u32[]{:S(2)}, u32[]{:S(2)}) %all-to-all-start.3) | async-done | bytes 98336 | tf_op jit(solution)/shard_map/all_to_all | solution.py:431
  77.8 2.6 %shard_map.108 = (bf16[512,192]{1,0:T(8,128)(2,1)}, bf16[768,192]{1,0:T(8,128)(2,1)}) custom-call(f32[512,192]{1,0:T(8,128)} %get-tuple-element.56.near_ref, bf16[4,64,192]{2,1,0:T(8,128)(2,1)S(1)} %all-to-all-done.3.around_ref, bf16[512,768]{1,0:T(8,128)(2,1)} %copy-done, bf16[384,192]{1,0:T(8,128)(2,1)} %get-tuple-element.58.out_part_ref), custom_call_target="tpu_custom_call" | custom-call | flops 200000000 | bytes 4000000 | tf_op jit(solution)/shard_map/pallas_call | solution.py:300
  80.4 5.0 %all-to-all-start.4 = ((bf16[32,24,192]{2,1,0:T(8,128)(2,1)}), bf16[32,24,192]{2,1,0:T(8,128)(2,1)S(1)}, u32[]{:S(2)}, u32[]{:S(2)}) async-start(bf16[32,24,192]{2,1,0:T(8,128)(2,1)} %bitcast.19), calls=%async_computation.4 | async-start | bytes 786432 | tf_op jit(solution)/shard_map/all_to_all | solution.py:319
  85.4 5.4 %shard_map.109 = (f32[2,2,128,768]{3,2,1,0:T(8,128)}, f32[2,2,128,768]{3,2,1,0:T(8,128)}) custom-call(bf16[512,96]{1,0:T(8,128)(2,1)} %get-tuple-element.54.attended_ref, bf16[96,768]{1,0:T(8,128)(2,1)} %get-tuple-element.55.out_weight_ref, bf16[512,192]{1,0:T(8,128)(2,1)} %get-tuple-element.53.attended_ref.grad_query_ref, ...), custom_call_target="tpu_custom_call" | custom-call | flops 3000000000 | bytes 4000000 | tf_op jit(solution)/shard_map/pallas_call | solution.py:300
  90.8 4.0 %all-to-all-done.4 = bf16[32,24,192]{2,1,0:T(8,128)(2,1)S(1)} async-done(((bf16[32,24,192]{2,1,0:T(8,128)(2,1)}), bf16[32,24,192]{2,1,0:T(8,128)(2,1)S(1)}, u32[]{:S(2)}, u32[]{:S(2)}) %all-to-all-start.4) | async-done | bytes 294944 | tf_op jit(solution)/shard_map/all_to_all | solution.py:319
  94.7 2.0 %collective-permute-start.2 = (f32[2,2,128,768]{3,2,1,0:T(8,128)}, f32[2,2,128,768]{3,2,1,0:T(8,128)S(1)}, u32[]{:S(2)}, u32[]{:S(2)}) collective-permute-start(f32[2,2,128,768]{3,2,1,0:T(8,128)} %get-tuple-element.64), channel_id=1, source_target_pairs={{0,1},{1,0},{2,3},{3,2},{4,5},{5,4},{6,7},{7,6},{8,9},{9,8},{10,11... | collective-permute-start | bytes 4718600 | tf_op jit(solution)/shard_map/ppermute | solution.py:44
  97.6 5.3 %all-to-all-start.5 = ((bf16[16,3,384]{2,1,0:T(4,128)(2,1)}), bf16[16,3,384]{2,1,0:T(4,128)(2,1)S(1)}, u32[]{:S(2)}, u32[]{:S(2)}) async-start(bf16[16,3,384]{2,1,0:T(4,128)(2,1)} %shard_map.110), calls=%async_computation.5 | async-start | bytes 98304 | tf_op jit(solution)/shard_map/all_to_all | solution.py:324
  102.9 1.7 %add.365 = f32[2,2,128,768]{3,2,1,0:T(8,128)S(1)} add(f32[2,2,128,768]{3,2,1,0:T(8,128)} %get-tuple-element.61, f32[2,2,128,768]{3,2,1,0:T(8,128)S(1)} %collective-permute-done.2) | non-fusion elementwise | flops 393216 | bytes 4718592 | tf_op jit(solution)/shard_map/add | solution.py:321
  104.6 3.5 %collective-permute-start.3 = (bf16[2,128,768]{2,1,0:T(8,128)(2,1)S(1)}, bf16[2,128,768]{2,1,0:T(8,128)(2,1)S(1)}, u32[]{:S(2)}, u32[]{:S(2)}) collective-permute-start(bf16[2,128,768]{2,1,0:T(8,128)(2,1)S(1)} %fusion.8), channel_id=1, source_target_pairs={{0,2},{2,0},{1,3},{3,1},{4,6},{6,4},{5,7},{7,5},{8,10},{10,8},{9,1... | collective-permute-start | bytes 1179656 | tf_op jit(solution)/shard_map/ppermute | solution.py:44
  108.2 7.7 %all-to-all-done.5 = bf16[16,3,384]{2,1,0:T(4,128)(2,1)S(1)} async-done(((bf16[16,3,384]{2,1,0:T(4,128)(2,1)}), bf16[16,3,384]{2,1,0:T(4,128)(2,1)S(1)}, u32[]{:S(2)}, u32[]{:S(2)}) %all-to-all-start.5) | async-done | bytes 36896 | tf_op jit(solution)/shard_map/all_to_all | solution.py:324
  115.9 9.0 %all_to_all.35 = f32[8,3,384]{2,1,0:T(4,128)S(1)} all-to-all(f32[8,3,384]{2,1,0:T(4,128)S(1)} %broadcast_in_dim.5), channel_id=1, replica_groups=mesh['yl'=2,'x'=4,'zh'=4,'zl'=4,'yh'=2,'c'=2] {'yl','x'}, dimensions={0} | all-to-all | bytes 73728 | tf_op jit(solution)/shard_map/all_to_all | solution.py:326
  126.2 0.8 fusion.10
  (39 shorter events, 4.7 us)
Async XLA Ops:
  2.1 28.8 %all-to-all-start = ((bf16[16,3,768]{2,1,0:T(4,128)(2,1)}), bf16[16,3,768]{2,1,0:T(4,128)(2,1)S(1)}, u32[]{:S(2)}, u32[]{:S(2)}) async-start(bf16[16,3,768]{2,1,0:T(4,128)(2,1)} %shard_map.102), calls=%async_computation | async-start | bytes 196608 | tf_op jit(solution)/shard_map/all_to_all | solution.py:349
  18.3 21.6 %collective-permute-start = (bf16[256,768]{1,0:T(8,128)(2,1)S(1)}, bf16[256,768]{1,0:T(8,128)(2,1)S(1)}, u32[]{:S(2)}, u32[]{:S(2)}) collective-permute-start(bf16[256,768]{1,0:T(8,128)(2,1)S(1)} %pad_maximum_fusion.1), channel_id=1, source_target_pairs={{0,2},{2,0},{1,3},{3,1},{4,6},{6,4},{5,7},{7,5},{8,10},{10,8},{9,1... | collective-permute-start | bytes 1179656 | tf_op jit(solution)/shard_map/ppermute | solution.py:44
  32.1 19.0 %all-to-all-start.1 = ((bf16[32,24,384]{2,1,0:T(8,128)(2,1)}), bf16[32,24,384]{2,1,0:T(8,128)(2,1)S(1)}, u32[]{:S(2)}, u32[]{:S(2)}) async-start(bf16[32,24,384]{2,1,0:T(8,128)(2,1)} %bitcast.17), calls=%async_computation.1 | async-start | bytes 1179648 | tf_op jit(solution)/shard_map/all_to_all | solution.py:354
  40.0 4.5 %collective-permute-start.1 = (bf16[512,768]{1,0:T(8,128)(2,1)S(1)}, bf16[512,768]{1,0:T(8,128)(2,1)S(1)}, u32[]{:S(2)}, u32[]{:S(2)}) collective-permute-start(bf16[512,768]{1,0:T(8,128)(2,1)S(1)} %constant_dynamic-update-slice_fusion), channel_id=1, source_target_pairs={{0,1},{1,0},{2,3},{3,2},{4,5},{5,4},{6,7},{7,6},{8,9},{9,8},{10,11... | collective-permute-start | bytes 2359304 | tf_op jit(solution)/shard_map/ppermute | solution.py:44
  47.5 8.4 %copy-start = (bf16[512,768]{1,0:T(8,128)(2,1)}, bf16[512,768]{1,0:T(8,128)(2,1)S(1)}, u32[]{:S(2)}) copy-start(bf16[512,768]{1,0:T(8,128)(2,1)S(1)} %convolution_convert_fusion.tokens_ref) | copy-start | bytes 2359300
  51.1 4.7 %copy-start.1 = (bf16[32,24,384]{2,1,0:T(8,128)(2,1)}, bf16[32,24,384]{2,1,0:T(8,128)(2,1)S(1)}, u32[]{:S(2)}) copy-start(bf16[32,24,384]{2,1,0:T(8,128)(2,1)S(1)} %all-to-all-done.1) | copy-start | bytes 1769476
  52.5 9.5 %all-to-all-start.2 = ((bf16[4,64,192]{2,1,0:T(8,128)(2,1)}), bf16[4,64,192]{2,1,0:T(8,128)(2,1)S(1)}, u32[]{:S(2)}, u32[]{:S(2)}) async-start(bf16[4,64,192]{2,1,0:T(8,128)(2,1)} %get-tuple-element.51), calls=%async_computation.2 | async-start | bytes 262144 | tf_op jit(solution)/shard_map/all_to_all | solution.py:408
  68.6 9.2 %all-to-all-start.3 = ((bf16[4,64,192]{2,1,0:T(8,128)(2,1)}), bf16[4,64,192]{2,1,0:T(8,128)(2,1)S(1)}, u32[]{:S(2)}, u32[]{:S(2)}) async-start(bf16[4,64,192]{2,1,0:T(8,128)(2,1)} %get-tuple-element.57), calls=%async_computation.3 | async-start | bytes 262144 | tf_op jit(solution)/shard_map/all_to_all | solution.py:431
  80.4 14.3 %all-to-all-start.4 = ((bf16[32,24,192]{2,1,0:T(8,128)(2,1)}), bf16[32,24,192]{2,1,0:T(8,128)(2,1)S(1)}, u32[]{:S(2)}, u32[]{:S(2)}) async-start(bf16[32,24,192]{2,1,0:T(8,128)(2,1)} %bitcast.19), calls=%async_computation.4 | async-start | bytes 786432 | tf_op jit(solution)/shard_map/all_to_all | solution.py:319
  94.7 8.2 %collective-permute-start.2 = (f32[2,2,128,768]{3,2,1,0:T(8,128)}, f32[2,2,128,768]{3,2,1,0:T(8,128)S(1)}, u32[]{:S(2)}, u32[]{:S(2)}) collective-permute-start(f32[2,2,128,768]{3,2,1,0:T(8,128)} %get-tuple-element.64), channel_id=1, source_target_pairs={{0,1},{1,0},{2,3},{3,2},{4,5},{5,4},{6,7},{7,6},{8,9},{9,8},{10,11... | collective-permute-start | bytes 4718600 | tf_op jit(solution)/shard_map/ppermute | solution.py:44
  97.6 18.3 %all-to-all-start.5 = ((bf16[16,3,384]{2,1,0:T(4,128)(2,1)}), bf16[16,3,384]{2,1,0:T(4,128)(2,1)S(1)}, u32[]{:S(2)}, u32[]{:S(2)}) async-start(bf16[16,3,384]{2,1,0:T(4,128)(2,1)} %shard_map.110), calls=%async_computation.5 | async-start | bytes 98304 | tf_op jit(solution)/shard_map/all_to_all | solution.py:324
  104.6 21.6 %collective-permute-start.3 = (bf16[2,128,768]{2,1,0:T(8,128)(2,1)S(1)}, bf16[2,128,768]{2,1,0:T(8,128)(2,1)S(1)}, u32[]{:S(2)}, u32[]{:S(2)}) collective-permute-start(bf16[2,128,768]{2,1,0:T(8,128)(2,1)S(1)} %fusion.8), channel_id=1, source_target_pairs={{0,2},{2,0},{1,3},{3,1},{4,6},{6,4},{5,7},{7,5},{8,10},{10,8},{9,1... | collective-permute-start | bytes 1179656 | tf_op jit(solution)/shard_map/ppermute | solution.py:44

commit v5 on v4

--- a/solution.py
+++ b/solution.py
@@ -102,14 +102,20 @@
     out_ref[QUAD + 2 * TOK :, lanes] = rows[:TOK].astype(BF)
 
 
-def key_value_kernel(tokens_ref, weight_ref, out_ref, sent_ref):
-    rows = swap_rows(project(tokens_ref[...], weight_ref[...], slice(0, 2 * PART)))
-    store(out_ref, slice(0, 2 * PART), rows)
+def sent_kernel(even_ref, odd_ref, weight_ref, out_ref):
+    weight = weight_ref[...]
+    even, odd = (project(ref[...], weight, slice(0, 2 * PART)) for ref in (even_ref, odd_ref))
+    lane = lax.broadcasted_iota(jnp.int32, even.shape, 1)
+    rows = jnp.where((lane >= DIM) & (lane < 2 * DIM) | (lane >= 3 * DIM), odd, even).astype(BF)
     for member in range(4):
-        sent_ref[member] = rows[:64].astype(BF)
-
-
-def query_kernel(tokens_ref, grad_out_ref, valid_ref, order_ref, pick_ref, rest_ref, rows_ref, out_ref):
+        out_ref[member] = rows
+
+
+def query_kernel(
+    tokens_ref, grad_out_ref, valid_ref, order_ref, pick_ref, pair_ref, rest_ref, rows_ref, key_rows_ref, out_ref
+):
+    lanes = slice(0, 2 * PART)
+    store(key_rows_ref, lanes, swap_rows(project(tokens_ref[...], pair_ref[...], lanes)))
     rest = rest_ref[...]
     query = swap_rows(project(tokens_ref[...], rest, slice(0, PART)))
     blocks = []
@@ -176,10 +182,9 @@
     weights, steps = [], []
     for h in heads:
         def rows_of(values, reduce, combine):
-            total = reduce(values[2], axis=1, keepdims=True)
-            for value in (values[1], values[0]):
-                total = grow(total, reduce(value, axis=1, keepdims=True), combine)
-            return total
+            total = combine(combine(values[2][:, :TOK], values[2][:, TOK : 2 * TOK]), values[2][:, 2 * TOK :])
+            total = grow(grow(total, values[1], combine), values[0], combine)
+            return reduce(total, axis=1, keepdims=True)
 
         top = rows_of(scores[h], jnp.max, jnp.maximum)
         expo = [jnp.exp(s - top[: s.shape[0]]) for s in scores[h]]
@@ -241,13 +246,17 @@
             ).astype(BF)
 
 
-def value_kernel(near_ref, around_ref, tokens_ref, out_part_ref, rows_ref, part_ref):
+def key_value_grads(near_ref, around_ref):
     rows = near_ref[...]
     rows = jnp.concatenate([rows[:64] + jnp.sum(around_ref[...].astype(F32), 0), rows[64:]], 0)
-    rows = swap_rows(rows).astype(BF)
-    rows_ref[...] = rows
-    part_ref[:INNER, :PART] = dot_tn(tokens_ref[:, :INNER], rows[:, PART:]).astype(BF)
-    part_ref[:INNER, PART:] = dot_tn(tokens_ref[:, INNER:], rows[:, PART:]).astype(BF)
+    return swap_rows(rows).astype(BF)
+
+
+def value_kernel(near_ref, around_ref, tokens_ref, out_part_ref, part_ref):
+    rows = key_value_grads(near_ref, around_ref)
+    part = dot_tn(rows[:, PART:], tokens_ref[...])
+    part_ref[:INNER, :PART] = part[:, :INNER].T.astype(BF)
+    part_ref[:INNER, PART:] = part[:, INNER:].T.astype(BF)
     part_ref[INNER:, :] = out_part_ref[...]
 
 
@@ -265,15 +274,22 @@
         out_ref[index] = rows[3 * index : 3 * index + 3].astype(BF)
 
 
+def last_kernel(pieces_ref, value_ref, out_ref):
+    for x in range(4):
+        value_ref[3 * x : 3 * x + 3, :] = pieces_ref[x]
+        rows, side = (x & 1) * 3, (x >> 1) * INNER
+        out_ref[rows : rows + 3, side : side + INNER] = pieces_ref[4 + x]
+
+
 def tokens_kernel(
-    attended_ref, out_weight_ref, grad_query_ref, order_ref, rows_ref, columns_ref, pair_ref, rest_ref,
+    attended_ref, out_weight_ref, grad_query_ref, order_ref, near_ref, around_ref, columns_ref, pair_ref, rest_ref,
     kept_ref, sent_ref,
 ):
     pair = project(columns_ref[...], pair_ref[...], slice(0, 2 * PART)).astype(BF)
     query = project(columns_ref[...], rest_ref[...], slice(0, PART)).astype(BF)
     order = order_ref[...]
     grad_query = dot_tn(order, grad_query_ref[:, PART:]).astype(BF)
-    grad_rows = dot_tn(order, rows_ref[...]).astype(BF)
+    grad_rows = dot_tn(order, key_value_grads(near_ref, around_ref)).astype(BF)
     mixed = dot(attended_ref[...], out_weight_ref[...])
     grads = dot_nt(grad_query, query) + dot_nt(grad_rows, pair)
     for index, rows in enumerate((mixed, grads)):
@@ -324,8 +340,9 @@
     piece = lax.all_to_all(piece, Z, 0, 0, tiled=True)
     piece = jnp.sum(piece.astype(F32), 0)
     full = lax.all_to_all(jnp.broadcast_to(piece[None], (8, 3, INNER)), SLIDE, 0, 0, tiled=True)
-    value_share = full[:4].reshape(12, INNER)
-    out_share = jnp.concatenate([full[4:6].reshape(6, INNER), full[6:].reshape(6, INNER)], 1)
+    value_share, out_share = call(
+        last_kernel, [shape(12, INNER, kind=F32), shape(6, D, kind=F32)], full, near=(0,), flops=2_500_000_000
+    )
     mixed = (both[0, 0] + beside[0].astype(F32)).astype(BF)
     grad_tokens = (both[0, 1] + beside[1].astype(F32)).astype(BF)
     return mixed, grad_tokens, value_share, out_share
@@ -347,7 +364,8 @@
     own = jnp.concatenate([tokens[0], grad_out[0]], 0)
     other = partner(own, "yh")
     rows = lax.all_to_all(mine, Z, 0, 0, tiled=True)
-    own, rows, length, turn, block, zl = lax.optimization_barrier((own, rows, length, turn, block, zl))
+    wide = jnp.arange(D, dtype=jnp.int32)
+    own, rows, length, turn, block, zl, wide = lax.optimization_barrier((own, rows, length, turn, block, zl, wide))
     (chunks,) = call(
         chunk_kernel, [shape(8, 4, 24, 4 * PART)], rows, scratch=[pltpu.VMEM((48, D), F32)], near=(0,), loose=(0,)
     )
@@ -364,7 +382,7 @@
     order = one_hot(which * TOK + within, QUAD).T
     valid = ((block ^ (row >> 7)) * TOK + (row & 127) < length).astype(F32)[:, None]
 
-    column = jnp.arange(D, dtype=jnp.int32)
+    column = wide
     high, spot, left = column // INNER, column % INNER // 24, column % 24
     columns = one_hot(((high * 8 + left // 3) * 4 + (spot & 3)) * 12 + (spot >> 2) * 3 + left % 3, D)
     column = jnp.arange(HALF, dtype=jnp.int32)
@@ -396,21 +414,26 @@
         (upstream_rows, order, valid, columns, pick, position, tokens_rows)
     )
 
-    key_rows, sent = call(
-        key_value_kernel,
-        (shape(STORED, 2 * PART), shape(4, 64, 2 * PART)),
-        tokens_rows, weights,
-        special={1: PAIR_WEIGHT},
-        near=(0, 1),
-        loose=(1,),
+    (sent,) = call(
+        sent_kernel,
+        [shape(4, 64, 2 * PART)],
+        tokens_rows, tokens_rows, weights,
+        special={
+            0: pl.BlockSpec((64, D), lambda step: (0, 0)),
+            1: pl.BlockSpec((64, D), lambda step: (QUAD // 128, 0)),
+            2: PAIR_WEIGHT,
+        },
+        near=(0, 1, 2),
+        loose=(0,),
         flops=200_000_000,
     )
     around = lax.all_to_all(sent, "zl", 0, 0, tiled=True)
-    query_rows, out_weight = call(
+    query_rows, key_rows, out_weight = call(
         query_kernel,
-        (shape(STORED, 2 * PART), shape(PART, D)),
-        tokens_rows, upstream_rows, valid, order, pick, weights,
-        special={5: REST_WEIGHT},
+        (shape(STORED, 2 * PART), shape(STORED, 2 * PART), shape(PART, D)),
+        tokens_rows, upstream_rows, valid, order, pick, weights, weights,
+        special={5: PAIR_WEIGHT, 6: REST_WEIGHT},
+        loose=(0, 1),
         flops=3_000_000_000,
     )
 
@@ -423,7 +446,7 @@
             pltpu.VMEM((QUAD, PART), F32), pltpu.VMEM((QUAD, PART), F32),
         ],
         special={0: SCALARS},
-        near=(3,),
+        near=(1, 2, 3),
         loose=(2,),
         flops=3_000_000_000,
     )
@@ -435,19 +458,19 @@
         both, valid, order, pick, upstream_rows,
         flops=3_000_000_000,
     )
-    grad_rows, part = call(
+    (part,) = call(
         value_kernel,
-        (shape(QUAD, 2 * PART), shape(D, 2 * PART)),
+        [shape(D, 2 * PART)],
         near_grads, around, tokens_rows, out_part,
         near=(1,),
-        loose=(1,),
+        loose=(0,),
         flops=200_000_000,
     )
     kept, sent = call(
         tokens_kernel,
         (shape(2, 2, TOK, D, kind=F32), shape(2, 2, TOK, D, kind=F32)),
-        attended, out_weight, both, order, grad_rows, columns, weights, weights,
-        special={6: PAIR_WEIGHT, 7: REST_WEIGHT},
+        attended, out_weight, both, order, near_grads, around, columns, weights, weights,
+        special={7: PAIR_WEIGHT, 8: REST_WEIGHT},
         flops=3_000_000_000,
     )
     mixed, grad_tokens, value_share, out_share = reduce_weights(part, kept, sent)

time: 128 us -> 126 us (0.984)
  Pallas kernels: 26.8 us -> 25.4 us
    all_to_all x1, waiting for transfers between devices: 4.58 us -> 6.01 us  [on_device(): rows = lax.all_to_all(mine, Z, 0, 0, tiled=True)]
    all_to_all x1, waiting for transfers between devices: 3.67 us -> 2.25 us  [on_device(): lax.all_to_all(chunks.reshape(32, 24, 4 * PART), PLANE, 0, 0, tiled=True)]
    pallas_call x9 -> x10, Pallas kernels: 26.8 us -> 25.4 us  [call(): pl.pallas_call(kernel, grid=(1,), out_shape=[leaf if index in loose else...]
  transfers between devices with their start and end apart: 10 -> 10, of which waited for: 6 -> 6; matrix products, arithmetic and copies ran while one was open for 9% -> 8% of each run, Pallas kernels for 12% -> 12%
where the time goes in v5:
time: 126 us; the launch traced here: 125 us
  starting transfers between devices  52.3 us (42%)
  Pallas kernels  25.4 us (20%)
  waiting for transfers between devices  25.1 us (20%)
  blocking collectives  9 us (7%)
  other arithmetic  8.23 us (7%)
  matrix products  1.79 us (1%)
  between operations  1.54 us (1%)
  local copies, waits for them, and re-layouts  1.28 us (1%)
    pallas_call x10, Pallas kernels, call(): pl.pallas_call(kernel, grid=(1,), out_shape=[leaf if index in loose else...  25.4 us
    all_to_all x1, starting transfers between devices, on_device(): rows = lax.all_to_all(mine, Z, 0, 0, tiled=True)  15.2 us
    ppermute x4, starting transfers between devices, partner(): return lax.ppermute(value, axis, [(0, 1), (1, 0)])  12.7 us
    all_to_all x1, blocking collectives, reduce_weights(): lax.all_to_all(jnp.broadcast_to(piece[None], (8, 3, INNER)), SLIDE, 0, 0,...  9 us
    all_to_all x1, waiting for transfers between devices, reduce_weights(): piece = lax.all_to_all(piece, Z, 0, 0, tiled=True)  7.78 us
    all_to_all x1, starting transfers between devices, on_device(): lax.all_to_all(chunks.reshape(32, 24, 4 * PART), PLANE, 0, 0, tiled=True)  7.62 us
    all_to_all x1, waiting for transfers between devices, on_device(): rows = lax.all_to_all(mine, Z, 0, 0, tiled=True)  6.01 us
    all_to_all x1, starting transfers between devices, reduce_weights(): lax.all_to_all(part.reshape(32, 24, 2 * PART), PLANE, 0, 0, tiled=True)  5.61 us
  transfers between devices with their start and end apart: 10, of which 6 were waited for; matrix products, arithmetic and copies ran while one was open for 8% of the time, Pallas kernels for 12%

profile of v5, /device:TPU:2, one launch (start us, length us, event | category | flops | bytes accessed | tf_op | source)
XLA Modules:
  0.0 124.6 jit_solution(6532648604966515747)
XLA Ops:
  0.6 1.4 %shard_map.102 = bf16[16,3,768]{2,1,0:T(4,128)(2,1)} custom-call(bf16[12,384]{1,0:T(8,128)(2,1)} %key_ref.1, bf16[12,384]{1,0:T(8,128)(2,1)} %value_ref.1, bf16[12,384]{1,0:T(8,128)(2,1)} %query_ref.1, bf16[6,768]{1,0:T(8,128)(2,1)} %out_weight_ref.1), custom_call_target="tpu_custom_call" | custom-call | bytes 4000000 | tf_op jit(solution)/shard_map/pallas_call | solution.py:316
  2.1 15.2 %all-to-all-start = ((bf16[16,3,768]{2,1,0:T(4,128)(2,1)}), bf16[16,3,768]{2,1,0:T(4,128)(2,1)S(1)}, u32[]{:S(2)}, u32[]{:S(2)}) async-start(bf16[16,3,768]{2,1,0:T(4,128)(2,1)} %shard_map.102), calls=%async_computation | async-start | bytes 196608 | tf_op jit(solution)/shard_map/all_to_all | solution.py:366
  17.3 1.1 pad_maximum_fusion.1
  18.3 5.1 %collective-permute-start = (bf16[256,768]{1,0:T(8,128)(2,1)S(1)}, bf16[256,768]{1,0:T(8,128)(2,1)S(1)}, u32[]{:S(2)}, u32[]{:S(2)}) collective-permute-start(bf16[256,768]{1,0:T(8,128)(2,1)S(1)} %pad_maximum_fusion.1), channel_id=1, source_target_pairs={{0,2},{2,0},{1,3},{3,1},{4,6},{6,4},{5,7},{7,5},{8,10},{10,8},{9,1... | collective-permute-start | bytes 1179656 | tf_op jit(solution)/shard_map/ppermute | solution.py:44
  24.8 6.0 %all-to-all-done.pieces_ref = bf16[16,3,768]{2,1,0:T(4,128)(2,1)S(1)} async-done(((bf16[16,3,768]{2,1,0:T(4,128)(2,1)}), bf16[16,3,768]{2,1,0:T(4,128)(2,1)S(1)}, u32[]{:S(2)}, u32[]{:S(2)}) %all-to-all-start) | async-done | bytes 73760 | tf_op jit(solution)/shard_map/all_to_all | solution.py:366
  30.9 1.2 shard_map.103
  32.1 7.6 %all-to-all-start.1 = ((bf16[32,24,384]{2,1,0:T(8,128)(2,1)}), bf16[32,24,384]{2,1,0:T(8,128)(2,1)S(1)}, u32[]{:S(2)}, u32[]{:S(2)}) async-start(bf16[32,24,384]{2,1,0:T(8,128)(2,1)} %bitcast.17), calls=%async_computation.1 | async-start | bytes 1179648 | tf_op jit(solution)/shard_map/all_to_all | solution.py:372
  40.0 1.0 fusion.5.order_ref
  41.0 2.1 %collective-permute-start.1 = (bf16[512,768]{1,0:T(8,128)(2,1)S(1)}, bf16[512,768]{1,0:T(8,128)(2,1)S(1)}, u32[]{:S(2)}, u32[]{:S(2)}) collective-permute-start(bf16[512,768]{1,0:T(8,128)(2,1)S(1)} %constant_dynamic-update-slice_fusion), channel_id=1, source_target_pairs={{0,1},{1,0},{2,3},{3,2},{4,5},{5,4},{6,7},{7,6},{8,9},{9,8},{10,11... | collective-permute-start | bytes 2359304 | tf_op jit(solution)/shard_map/ppermute | solution.py:44
  43.1 1.4 %fusion.1.columns_ref = bf16[768,768]{1,0:T(8,128)(2,1)} fusion(s32[768]{0:T(1024)S(1)} %fusion.21), kind=kLoop, calls=%fused_computation.2 | loop fusion | flops 1179648 | bytes 1182720 | tf_op jit(solution)/shard_map/convert_element_type | solution.py:352
  46.1 1.0 copy.14
  47.1 1.8 %convolution_convert_fusion.tokens_ref.even_ref.odd_ref = bf16[512,768]{1,0:T(8,128)(2,1)S(1)} fusion(bf16[512,768]{1,0:T(8,128)(2,1)S(1)} %bitcast.56, s32[768]{0:T(1024)S(1)} %fusion.21, s32[512]{0:T(512)S(1)} %get-tuple-element.85), kind=kOutput, calls=%fused_computation.6 | convolution fusion | flops 1008271360 | bytes 1577984 | tf_op jit(solution)/shard_map/dot_general | solution.py:32
  48.9 2.2 %all-to-all-done.1 = bf16[32,24,384]{2,1,0:T(8,128)(2,1)S(1)} async-done(((bf16[32,24,384]{2,1,0:T(8,128)(2,1)}), bf16[32,24,384]{2,1,0:T(8,128)(2,1)S(1)}, u32[]{:S(2)}, u32[]{:S(2)}) %all-to-all-start.1) | async-done | bytes 589856 | tf_op jit(solution)/shard_map/all_to_all | solution.py:372
  51.1 1.0 shard_map.105
  52.1 3.3 %all-to-all-start.2 = ((bf16[4,64,192]{2,1,0:T(8,128)(2,1)}), bf16[4,64,192]{2,1,0:T(8,128)(2,1)S(1)}, u32[]{:S(2)}, u32[]{:S(2)}) async-start(bf16[4,64,192]{2,1,0:T(8,128)(2,1)} %shard_map.105), calls=%async_computation.2 | async-start | bytes 262144 | tf_op jit(solution)/shard_map/all_to_all | solution.py:430
  55.5 3.5 %shard_map.104 = (bf16[896,192]{1,0:T(8,128)(2,1)S(1)}, bf16[896,192]{1,0:T(8,128)(2,1)S(1)}, bf16[96,768]{1,0:T(8,128)(2,1)}) custom-call(bf16[512,768]{1,0:T(8,128)(2,1)} %copy-done, bf16[512,768]{1,0:T(8,128)(2,1)} %bitcast.54, f32[512,1]{1,0:T(8,128)} %fusion.13.valid_ref, bf16[512,512]{1,0:T(8,128)(2,1)} %fusion.5.order_ref, ...), custom_call_target="tpu_custom_call" | custom-call | flops 3000000000 | bytes 4000000 | tf_op jit(solution)/shard_map/pallas_call | solution.py:316
  58.9 2.7 %all-to-all-done.2.around_ref = bf16[4,64,192]{2,1,0:T(8,128)(2,1)S(1)} async-done(((bf16[4,64,192]{2,1,0:T(8,128)(2,1)}), bf16[4,64,192]{2,1,0:T(8,128)(2,1)S(1)}, u32[]{:S(2)}, u32[]{:S(2)}) %all-to-all-start.2) | async-done | bytes 98336 | tf_op jit(solution)/shard_map/all_to_all | solution.py:430
  61.7 5.2 %shard_map.106 = (bf16[512,192]{1,0:T(8,128)(2,1)}, f32[512,192]{1,0:T(8,128)}, bf16[4,64,192]{2,1,0:T(8,128)(2,1)}) custom-call(s32[1]{0:T(128)} %copy.17.length_ref, bf16[896,192]{1,0:T(8,128)(2,1)S(1)} %get-tuple-element.50.query_rows_ref, bf16[896,192]{1,0:T(8,128)(2,1)S(1)} %get-tuple-element.51.key_rows_ref, ...), custom_call_target="tpu_custom_call" | custom-call | flops 3000000000 | bytes 4000000 | tf_op jit(solution)/shard_map/pallas_call | solution.py:316
  66.9 3.3 %all-to-all-start.3 = ((bf16[4,64,192]{2,1,0:T(8,128)(2,1)}), bf16[4,64,192]{2,1,0:T(8,128)(2,1)S(1)}, u32[]{:S(2)}, u32[]{:S(2)}) async-start(bf16[4,64,192]{2,1,0:T(8,128)(2,1)} %get-tuple-element.57), calls=%async_computation.3 | async-start | bytes 262144 | tf_op jit(solution)/shard_map/all_to_all | solution.py:454
  70.2 3.4 %shard_map.107 = (bf16[512,96]{1,0:T(8,128)(2,1)}, bf16[384,192]{1,0:T(8,128)(2,1)}) custom-call(bf16[512,192]{1,0:T(8,128)(2,1)} %get-tuple-element.53.attended_ref.grad_query_ref, f32[512,1]{1,0:T(8,128)} %fusion.13.valid_ref, bf16[512,512]{1,0:T(8,128)(2,1)} %fusion.5.order_ref, bf16[192,192]{1,0:T(8,128)(2,1)} %fusion.14.pick_ref, bf16[512,768]{1,0:T(8,128)(2,1)} %bitcast.55), custom_call_target="tpu_custom_call" | custom-call | flops 3000000000 | bytes 4000000 | tf_op jit(solution)/shard_map/pallas_call | solution.py:316
  73.6 2.5 %all-to-all-done.3.around_ref = bf16[4,64,192]{2,1,0:T(8,128)(2,1)S(1)} async-done(((bf16[4,64,192]{2,1,0:T(8,128)(2,1)}), bf16[4,64,192]{2,1,0:T(8,128)(2,1)S(1)}, u32[]{:S(2)}, u32[]{:S(2)}) %all-to-all-start.3) | async-done | bytes 98336 | tf_op jit(solution)/shard_map/all_to_all | solution.py:454
  76.1 2.7 %shard_map.109 = bf16[768,192]{1,0:T(8,128)(2,1)} custom-call(f32[512,192]{1,0:T(8,128)} %get-tuple-element.56.near_ref, bf16[4,64,192]{2,1,0:T(8,128)(2,1)S(1)} %all-to-all-done.3.around_ref, bf16[512,768]{1,0:T(8,128)(2,1)} %copy-done, bf16[384,192]{1,0:T(8,128)(2,1)} %get-tuple-element.60.out_part_ref), custom_call_target="tpu_custom_call" | custom-call | flops 200000000 | bytes 4000000 | tf_op jit(solution)/shard_map/pallas_call | solution.py:316
  78.8 5.6 %all-to-all-start.4 = ((bf16[32,24,192]{2,1,0:T(8,128)(2,1)}), bf16[32,24,192]{2,1,0:T(8,128)(2,1)S(1)}, u32[]{:S(2)}, u32[]{:S(2)}) async-start(bf16[32,24,192]{2,1,0:T(8,128)(2,1)} %bitcast.19), calls=%async_computation.4 | async-start | bytes 786432 | tf_op jit(solution)/shard_map/all_to_all | solution.py:335
  84.4 5.5 %shard_map.108 = (f32[2,2,128,768]{3,2,1,0:T(8,128)}, f32[2,2,128,768]{3,2,1,0:T(8,128)}) custom-call(bf16[512,96]{1,0:T(8,128)(2,1)} %get-tuple-element.54.attended_ref, bf16[96,768]{1,0:T(8,128)(2,1)} %get-tuple-element.55.out_weight_ref, bf16[512,192]{1,0:T(8,128)(2,1)} %get-tuple-element.53.attended_ref.grad_query_ref, ...), custom_call_target="tpu_custom_call" | custom-call | flops 3000000000 | bytes 4000000 | tf_op jit(solution)/shard_map/pallas_call | solution.py:316
  90.0 3.8 %all-to-all-done.4 = bf16[32,24,192]{2,1,0:T(8,128)(2,1)S(1)} async-done(((bf16[32,24,192]{2,1,0:T(8,128)(2,1)}), bf16[32,24,192]{2,1,0:T(8,128)(2,1)S(1)}, u32[]{:S(2)}, u32[]{:S(2)}) %all-to-all-start.4) | async-done | bytes 294944 | tf_op jit(solution)/shard_map/all_to_all | solution.py:335
  93.7 2.0 %collective-permute-start.2 = (f32[2,2,128,768]{3,2,1,0:T(8,128)}, f32[2,2,128,768]{3,2,1,0:T(8,128)S(1)}, u32[]{:S(2)}, u32[]{:S(2)}) collective-permute-start(f32[2,2,128,768]{3,2,1,0:T(8,128)} %get-tuple-element.62), channel_id=1, source_target_pairs={{0,1},{1,0},{2,3},{3,2},{4,5},{5,4},{6,7},{7,6},{8,9},{9,8},{10,11... | collective-permute-start | bytes 4718600 | tf_op jit(solution)/shard_map/ppermute | solution.py:44
  96.5 4.6 %all-to-all-start.5 = ((bf16[16,3,384]{2,1,0:T(4,128)(2,1)}), bf16[16,3,384]{2,1,0:T(4,128)(2,1)S(1)}, u32[]{:S(2)}, u32[]{:S(2)}) async-start(bf16[16,3,384]{2,1,0:T(4,128)(2,1)} %shard_map.110), calls=%async_computation.5 | async-start | bytes 98304 | tf_op jit(solution)/shard_map/all_to_all | solution.py:340
  101.2 1.6 %add.311 = f32[2,2,128,768]{3,2,1,0:T(8,128)S(1)} add(f32[2,2,128,768]{3,2,1,0:T(8,128)} %get-tuple-element.59, f32[2,2,128,768]{3,2,1,0:T(8,128)S(1)} %collective-permute-done.2) | non-fusion elementwise | flops 393216 | bytes 4718592 | tf_op jit(solution)/shard_map/add | solution.py:337
  102.8 3.5 %collective-permute-start.3 = (bf16[2,128,768]{2,1,0:T(8,128)(2,1)S(1)}, bf16[2,128,768]{2,1,0:T(8,128)(2,1)S(1)}, u32[]{:S(2)}, u32[]{:S(2)}) collective-permute-start(bf16[2,128,768]{2,1,0:T(8,128)(2,1)S(1)} %fusion.8), channel_id=1, source_target_pairs={{0,2},{2,0},{1,3},{3,1},{4,6},{6,4},{5,7},{7,5},{8,10},{10,8},{9,1... | collective-permute-start | bytes 1179656 | tf_op jit(solution)/shard_map/ppermute | solution.py:44
  106.3 7.8 %all-to-all-done.5 = bf16[16,3,384]{2,1,0:T(4,128)(2,1)S(1)} async-done(((bf16[16,3,384]{2,1,0:T(4,128)(2,1)}), bf16[16,3,384]{2,1,0:T(4,128)(2,1)S(1)}, u32[]{:S(2)}, u32[]{:S(2)}) %all-to-all-start.5) | async-done | bytes 36896 | tf_op jit(solution)/shard_map/all_to_all | solution.py:340
  114.1 9.0 %all_to_all.35.pieces_ref = f32[8,3,384]{2,1,0:T(4,128)S(1)} all-to-all(f32[8,3,384]{2,1,0:T(4,128)S(1)} %broadcast_in_dim.5), channel_id=1, replica_groups=mesh['yl'=2,'x'=4,'zh'=4,'zl'=4,'yh'=2,'c'=2] {'yl','x'}, dimensions={0} | all-to-all | bytes 73728 | tf_op jit(solution)/shard_map/all_to_all | solution.py:342
  123.8 0.8 fusion.10
  (37 shorter events, 4.1 us)
Async XLA Ops:
  2.1 28.8 %all-to-all-start = ((bf16[16,3,768]{2,1,0:T(4,128)(2,1)}), bf16[16,3,768]{2,1,0:T(4,128)(2,1)S(1)}, u32[]{:S(2)}, u32[]{:S(2)}) async-start(bf16[16,3,768]{2,1,0:T(4,128)(2,1)} %shard_map.102), calls=%async_computation | async-start | bytes 196608 | tf_op jit(solution)/shard_map/all_to_all | solution.py:366
  18.3 22.6 %collective-permute-start = (bf16[256,768]{1,0:T(8,128)(2,1)S(1)}, bf16[256,768]{1,0:T(8,128)(2,1)S(1)}, u32[]{:S(2)}, u32[]{:S(2)}) collective-permute-start(bf16[256,768]{1,0:T(8,128)(2,1)S(1)} %pad_maximum_fusion.1), channel_id=1, source_target_pairs={{0,2},{2,0},{1,3},{3,1},{4,6},{6,4},{5,7},{7,5},{8,10},{10,8},{9,1... | collective-permute-start | bytes 1179656 | tf_op jit(solution)/shard_map/ppermute | solution.py:44
  32.1 19.0 %all-to-all-start.1 = ((bf16[32,24,384]{2,1,0:T(8,128)(2,1)}), bf16[32,24,384]{2,1,0:T(8,128)(2,1)S(1)}, u32[]{:S(2)}, u32[]{:S(2)}) async-start(bf16[32,24,384]{2,1,0:T(8,128)(2,1)} %bitcast.17), calls=%async_computation.1 | async-start | bytes 1179648 | tf_op jit(solution)/shard_map/all_to_all | solution.py:372
  41.0 4.9 %collective-permute-start.1 = (bf16[512,768]{1,0:T(8,128)(2,1)S(1)}, bf16[512,768]{1,0:T(8,128)(2,1)S(1)}, u32[]{:S(2)}, u32[]{:S(2)}) collective-permute-start(bf16[512,768]{1,0:T(8,128)(2,1)S(1)} %constant_dynamic-update-slice_fusion), channel_id=1, source_target_pairs={{0,1},{1,0},{2,3},{3,2},{4,5},{5,4},{6,7},{7,6},{8,9},{9,8},{10,11... | collective-permute-start | bytes 2359304 | tf_op jit(solution)/shard_map/ppermute | solution.py:44
  48.9 6.6 %copy-start = (bf16[512,768]{1,0:T(8,128)(2,1)}, bf16[512,768]{1,0:T(8,128)(2,1)S(1)}, u32[]{:S(2)}) copy-start(bf16[512,768]{1,0:T(8,128)(2,1)S(1)} %convolution_convert_fusion.tokens_ref.even_ref.odd_ref) | copy-start | bytes 2359300
  51.1 4.3 %copy-start.1 = (bf16[32,24,384]{2,1,0:T(8,128)(2,1)}, bf16[32,24,384]{2,1,0:T(8,128)(2,1)S(1)}, u32[]{:S(2)}) copy-start(bf16[32,24,384]{2,1,0:T(8,128)(2,1)S(1)} %all-to-all-done.1) | copy-start | bytes 1769476
  52.1 9.5 %all-to-all-start.2 = ((bf16[4,64,192]{2,1,0:T(8,128)(2,1)}), bf16[4,64,192]{2,1,0:T(8,128)(2,1)S(1)}, u32[]{:S(2)}, u32[]{:S(2)}) async-start(bf16[4,64,192]{2,1,0:T(8,128)(2,1)} %shard_map.105), calls=%async_computation.2 | async-start | bytes 262144 | tf_op jit(solution)/shard_map/all_to_all | solution.py:430
  66.9 9.2 %all-to-all-start.3 = ((bf16[4,64,192]{2,1,0:T(8,128)(2,1)}), bf16[4,64,192]{2,1,0:T(8,128)(2,1)S(1)}, u32[]{:S(2)}, u32[]{:S(2)}) async-start(bf16[4,64,192]{2,1,0:T(8,128)(2,1)} %get-tuple-element.57), calls=%async_computation.3 | async-start | bytes 262144 | tf_op jit(solution)/shard_map/all_to_all | solution.py:454
  76.1 8.3 %copy-start.2 = (bf16[4,64,192]{2,1,0:T(8,128)(2,1)}, bf16[4,64,192]{2,1,0:T(8,128)(2,1)S(1)}, u32[]{:S(2)}) copy-start(bf16[4,64,192]{2,1,0:T(8,128)(2,1)S(1)} %all-to-all-done.3.around_ref) | copy-start | bytes 294916
  78.8 14.9 %all-to-all-start.4 = ((bf16[32,24,192]{2,1,0:T(8,128)(2,1)}), bf16[32,24,192]{2,1,0:T(8,128)(2,1)S(1)}, u32[]{:S(2)}, u32[]{:S(2)}) async-start(bf16[32,24,192]{2,1,0:T(8,128)(2,1)} %bitcast.19), calls=%async_computation.4 | async-start | bytes 786432 | tf_op jit(solution)/shard_map/all_to_all | solution.py:335
  93.7 7.4 %collective-permute-start.2 = (f32[2,2,128,768]{3,2,1,0:T(8,128)}, f32[2,2,128,768]{3,2,1,0:T(8,128)S(1)}, u32[]{:S(2)}, u32[]{:S(2)}) collective-permute-start(f32[2,2,128,768]{3,2,1,0:T(8,128)} %get-tuple-element.62), channel_id=1, source_target_pairs={{0,1},{1,0},{2,3},{3,2},{4,5},{5,4},{6,7},{7,6},{8,9},{9,8},{10,11... | collective-permute-start | bytes 4718600 | tf_op jit(solution)/shard_map/ppermute | solution.py:44
  96.5 17.5 %all-to-all-start.5 = ((bf16[16,3,384]{2,1,0:T(4,128)(2,1)}), bf16[16,3,384]{2,1,0:T(4,128)(2,1)S(1)}, u32[]{:S(2)}, u32[]{:S(2)}) async-start(bf16[16,3,384]{2,1,0:T(4,128)(2,1)} %shard_map.110), calls=%async_computation.5 | async-start | bytes 98304 | tf_op jit(solution)/shard_map/all_to_all | solution.py:340
  102.8 21.0 %collective-permute-start.3 = (bf16[2,128,768]{2,1,0:T(8,128)(2,1)S(1)}, bf16[2,128,768]{2,1,0:T(8,128)(2,1)S(1)}, u32[]{:S(2)}, u32[]{:S(2)}) collective-permute-start(bf16[2,128,768]{2,1,0:T(8,128)(2,1)S(1)} %fusion.8), channel_id=1, source_target_pairs={{0,2},{2,0},{1,3},{3,1},{4,6},{6,4},{5,7},{7,5},{8,10},{10,8},{9,1... | collective-permute-start | bytes 1179656 | tf_op jit(solution)/shard_map/ppermute | solution.py:44

commit v6 on v5

--- a/solution.py
+++ b/solution.py
@@ -106,7 +106,8 @@
     weight = weight_ref[...]
     even, odd = (project(ref[...], weight, slice(0, 2 * PART)) for ref in (even_ref, odd_ref))
     lane = lax.broadcasted_iota(jnp.int32, even.shape, 1)
-    rows = jnp.where((lane >= DIM) & (lane < 2 * DIM) | (lane >= 3 * DIM), odd, even).astype(BF)
+    rows = jnp.where((lane >= DIM) & (lane < 2 * DIM) | (lane >= 3 * DIM), odd, even)
+    rows = jnp.concatenate([rows[:32], rows[32:]], 1).astype(BF)
     for member in range(4):
         out_ref[member] = rows
 
@@ -141,8 +142,11 @@
     scale = DIM ** -0.5
     length, start = length_ref[0], (lax.axis_index("zl") >> 1) * 2
     far_rows[:TOK, :] = rows_ref[...]
-    far_rows[TOK : 2 * TOK, :] = around_ref[pl.ds(start, 2)].reshape(TOK, 2 * PART)
-    far_rows[2 * TOK :, :] = around_ref[:, :32, :].reshape(TOK, 2 * PART)
+    beside = around_ref[pl.ds(start, 2)]
+    for index in range(4):
+        half = slice((index & 1) * 2 * PART, (index & 1) * 2 * PART + 2 * PART)
+        far_rows[TOK + 32 * index : TOK + 32 * index + 32, :] = beside[index >> 1, :, half]
+        far_rows[2 * TOK + 32 * index : 2 * TOK + 32 * index + 32, :] = around_ref[index, :, : 2 * PART]
     place = lax.broadcasted_iota(jnp.int32, (TOK, FAR), 0)
     lane = lax.broadcasted_iota(jnp.int32, (TOK, FAR), 1)
     used = jnp.where(lane < TOK, TOK, jnp.where(lane < 2 * TOK, TOK // 2, TOK // 4))
@@ -223,9 +227,11 @@
             near_ref[:, target] = rows if factor is None else rows * factor
             far_ref[:, target] = r2[TOK:] if factor is None else r2[TOK:] * factor
 
-    wide[:, :32, :] = far_ref[TOK:, :].reshape(4, 32, 2 * PART)
-    wide[:, 32:, :] = jnp.zeros((4, 32, 2 * PART), F32)
-    wide[pl.ds(start, 2)] += far_ref[:TOK, :].reshape(2, 64, 2 * PART)
+    wide[:, :, : 2 * PART] = far_ref[TOK:, :].reshape(4, 32, 2 * PART)
+    wide[:, :, 2 * PART :] = jnp.zeros((4, 32, 2 * PART), F32)
+    wide[pl.ds(start, 2)] += jnp.stack(
+        [jnp.concatenate([far_ref[r : r + 32, :], far_ref[r + 32 : r + 64, :]], 1) for r in (0, 64)]
+    )
     around_out_ref[...] = wide[...].astype(BF)
     rows = jnp.concatenate([attended[...], grad_query[...]], 1)
     out_ref[...] = swap_rows(rows).astype(BF)
@@ -248,7 +254,9 @@
 
 def key_value_grads(near_ref, around_ref):
     rows = near_ref[...]
-    rows = jnp.concatenate([rows[:64] + jnp.sum(around_ref[...].astype(F32), 0), rows[64:]], 0)
+    first = jnp.sum(around_ref[...].astype(F32), 0)
+    first = jnp.concatenate([first[:, : 2 * PART], first[:, 2 * PART :]], 0)
+    rows = jnp.concatenate([rows[:64] + first, rows[64:]], 0)
     return swap_rows(rows).astype(BF)
 
 
@@ -416,7 +424,7 @@
 
     (sent,) = call(
         sent_kernel,
-        [shape(4, 64, 2 * PART)],
+        [shape(4, 32, 4 * PART)],
         tokens_rows, tokens_rows, weights,
         special={
             0: pl.BlockSpec((64, D), lambda step: (0, 0)),
@@ -439,10 +447,10 @@
 
     both, near_grads, around = call(
         attention_kernel,
-        (shape(QUAD, 2 * PART), shape(QUAD, 2 * PART, kind=F32), shape(4, 64, 2 * PART)),
+        (shape(QUAD, 2 * PART), shape(QUAD, 2 * PART, kind=F32), shape(4, 32, 4 * PART)),
         lengths, query_rows, key_rows, around, position,
         scratch=[
-            pltpu.VMEM((FAR, 2 * PART), BF), pltpu.VMEM((2 * TOK, 2 * PART), F32), pltpu.VMEM((4, 64, 2 * PART), F32),
+            pltpu.VMEM((FAR, 2 * PART), BF), pltpu.VMEM((2 * TOK, 2 * PART), F32), pltpu.VMEM((4, 32, 4 * PART), F32),
             pltpu.VMEM((QUAD, PART), F32), pltpu.VMEM((QUAD, PART), F32),
         ],
         special={0: SCALARS},

time: 126 us -> 125 us (level)
  no operation moved by 1% of the time
where the time goes in v6:
time: 125 us; the launch traced here: 124 us
  starting transfers between devices  52.2 us (42%)
  Pallas kernels  25.5 us (20%)
  waiting for transfers between devices  24.6 us (20%)
  blocking collectives  9 us (7%)
  other arithmetic  8.24 us (7%)
  matrix products  1.79 us (1%)
  between operations  1.54 us (1%)
  local copies, waits for them, and re-layouts  1.28 us (1%)
    pallas_call x10, Pallas kernels, call(): pl.pallas_call(kernel, grid=(1,), out_shape=[leaf if index in loose else...  25.5 us
    all_to_all x1, starting transfers between devices, on_device(): rows = lax.all_to_all(mine, Z, 0, 0, tiled=True)  15.2 us
    ppermute x4, starting transfers between devices, partner(): return lax.ppermute(value, axis, [(0, 1), (1, 0)])  12.7 us
    all_to_all x1, blocking collectives, reduce_weights(): lax.all_to_all(jnp.broadcast_to(piece[None], (8, 3, INNER)), SLIDE, 0, 0,...  9 us
    all_to_all x1, waiting for transfers between devices, reduce_weights(): piece = lax.all_to_all(piece, Z, 0, 0, tiled=True)  7.78 us
    all_to_all x1, starting transfers between devices, on_device(): lax.all_to_all(chunks.reshape(32, 24, 4 * PART), PLANE, 0, 0, tiled=True)  7.62 us
    all_to_all x1, waiting for transfers between devices, on_device(): rows = lax.all_to_all(mine, Z, 0, 0, tiled=True)  6 us
    all_to_all x1, starting transfers between devices, reduce_weights(): lax.all_to_all(part.reshape(32, 24, 2 * PART), PLANE, 0, 0, tiled=True)  5.35 us
  transfers between devices with their start and end apart: 10, of which 6 were waited for; matrix products, arithmetic and copies ran while one was open for 8% of the time, Pallas kernels for 12%

profile of v6, /device:TPU:2, one launch (start us, length us, event | category | flops | bytes accessed | tf_op | source)
XLA Modules:
  0.0 124.1 jit_solution(14550468968868179054)
XLA Ops:
  0.6 1.4 %shard_map.102 = bf16[16,3,768]{2,1,0:T(4,128)(2,1)} custom-call(bf16[12,384]{1,0:T(8,128)(2,1)} %key_ref.1, bf16[12,384]{1,0:T(8,128)(2,1)} %value_ref.1, bf16[12,384]{1,0:T(8,128)(2,1)} %query_ref.1, bf16[6,768]{1,0:T(8,128)(2,1)} %out_weight_ref.1), custom_call_target="tpu_custom_call" | custom-call | bytes 4000000 | tf_op jit(solution)/shard_map/pallas_call | solution.py:324
  2.1 15.2 %all-to-all-start = ((bf16[16,3,768]{2,1,0:T(4,128)(2,1)}), bf16[16,3,768]{2,1,0:T(4,128)(2,1)S(1)}, u32[]{:S(2)}, u32[]{:S(2)}) async-start(bf16[16,3,768]{2,1,0:T(4,128)(2,1)} %shard_map.102), calls=%async_computation | async-start | bytes 196608 | tf_op jit(solution)/shard_map/all_to_all | solution.py:374
  17.3 1.1 pad_maximum_fusion.1
  18.3 5.1 %collective-permute-start = (bf16[256,768]{1,0:T(8,128)(2,1)S(1)}, bf16[256,768]{1,0:T(8,128)(2,1)S(1)}, u32[]{:S(2)}, u32[]{:S(2)}) collective-permute-start(bf16[256,768]{1,0:T(8,128)(2,1)S(1)} %pad_maximum_fusion.1), channel_id=1, source_target_pairs={{0,2},{2,0},{1,3},{3,1},{4,6},{6,4},{5,7},{7,5},{8,10},{10,8},{9,1... | collective-permute-start | bytes 1179656 | tf_op jit(solution)/shard_map/ppermute | solution.py:44
  24.8 6.0 %all-to-all-done.pieces_ref = bf16[16,3,768]{2,1,0:T(4,128)(2,1)S(1)} async-done(((bf16[16,3,768]{2,1,0:T(4,128)(2,1)}), bf16[16,3,768]{2,1,0:T(4,128)(2,1)S(1)}, u32[]{:S(2)}, u32[]{:S(2)}) %all-to-all-start) | async-done | bytes 73760 | tf_op jit(solution)/shard_map/all_to_all | solution.py:374
  30.9 1.2 shard_map.103
  32.1 7.6 %all-to-all-start.1 = ((bf16[32,24,384]{2,1,0:T(8,128)(2,1)}), bf16[32,24,384]{2,1,0:T(8,128)(2,1)S(1)}, u32[]{:S(2)}, u32[]{:S(2)}) async-start(bf16[32,24,384]{2,1,0:T(8,128)(2,1)} %bitcast.17), calls=%async_computation.1 | async-start | bytes 1179648 | tf_op jit(solution)/shard_map/all_to_all | solution.py:380
  40.0 1.0 fusion.5.order_ref
  41.0 2.1 %collective-permute-start.1 = (bf16[512,768]{1,0:T(8,128)(2,1)S(1)}, bf16[512,768]{1,0:T(8,128)(2,1)S(1)}, u32[]{:S(2)}, u32[]{:S(2)}) collective-permute-start(bf16[512,768]{1,0:T(8,128)(2,1)S(1)} %constant_dynamic-update-slice_fusion), channel_id=1, source_target_pairs={{0,1},{1,0},{2,3},{3,2},{4,5},{5,4},{6,7},{7,6},{8,9},{9,8},{10,11... | collective-permute-start | bytes 2359304 | tf_op jit(solution)/shard_map/ppermute | solution.py:44
  43.1 1.4 %fusion.1.columns_ref = bf16[768,768]{1,0:T(8,128)(2,1)} fusion(s32[768]{0:T(1024)S(1)} %fusion.21), kind=kLoop, calls=%fused_computation.2 | loop fusion | flops 1179648 | bytes 1182720 | tf_op jit(solution)/shard_map/convert_element_type | solution.py:360
  46.1 1.0 copy.14
  47.1 1.8 %convolution_convert_fusion.tokens_ref.even_ref.odd_ref = bf16[512,768]{1,0:T(8,128)(2,1)S(1)} fusion(bf16[512,768]{1,0:T(8,128)(2,1)S(1)} %bitcast.56, s32[768]{0:T(1024)S(1)} %fusion.21, s32[512]{0:T(512)S(1)} %get-tuple-element.85), kind=kOutput, calls=%fused_computation.6 | convolution fusion | flops 1008271360 | bytes 1577984 | tf_op jit(solution)/shard_map/dot_general | solution.py:32
  48.9 2.2 %all-to-all-done.1 = bf16[32,24,384]{2,1,0:T(8,128)(2,1)S(1)} async-done(((bf16[32,24,384]{2,1,0:T(8,128)(2,1)}), bf16[32,24,384]{2,1,0:T(8,128)(2,1)S(1)}, u32[]{:S(2)}, u32[]{:S(2)}) %all-to-all-start.1) | async-done | bytes 589856 | tf_op jit(solution)/shard_map/all_to_all | solution.py:380
  51.1 1.0 shard_map.105
  52.2 3.3 %all-to-all-start.2 = ((bf16[4,32,384]{2,1,0:T(8,128)(2,1)}), bf16[4,32,384]{2,1,0:T(8,128)(2,1)S(1)}, u32[]{:S(2)}, u32[]{:S(2)}) async-start(bf16[4,32,384]{2,1,0:T(8,128)(2,1)} %shard_map.105), calls=%async_computation.2 | async-start | bytes 196608 | tf_op jit(solution)/shard_map/all_to_all | solution.py:438
  55.5 3.4 %shard_map.104 = (bf16[896,192]{1,0:T(8,128)(2,1)S(1)}, bf16[896,192]{1,0:T(8,128)(2,1)S(1)}, bf16[96,768]{1,0:T(8,128)(2,1)}) custom-call(bf16[512,768]{1,0:T(8,128)(2,1)} %copy-done, bf16[512,768]{1,0:T(8,128)(2,1)} %bitcast.54, f32[512,1]{1,0:T(8,128)} %fusion.13.valid_ref, bf16[512,512]{1,0:T(8,128)(2,1)} %fusion.5.order_ref, ...), custom_call_target="tpu_custom_call" | custom-call | flops 3000000000 | bytes 4000000 | tf_op jit(solution)/shard_map/pallas_call | solution.py:324
  59.0 2.3 %all-to-all-done.2.around_ref = bf16[4,32,384]{2,1,0:T(8,128)(2,1)S(1)} async-done(((bf16[4,32,384]{2,1,0:T(8,128)(2,1)}), bf16[4,32,384]{2,1,0:T(8,128)(2,1)S(1)}, u32[]{:S(2)}, u32[]{:S(2)}) %all-to-all-start.2) | async-done | bytes 98336 | tf_op jit(solution)/shard_map/all_to_all | solution.py:438
  61.3 5.3 %shard_map.106 = (bf16[512,192]{1,0:T(8,128)(2,1)}, f32[512,192]{1,0:T(8,128)}, bf16[4,32,384]{2,1,0:T(8,128)(2,1)}) custom-call(s32[1]{0:T(128)} %copy.17.length_ref, bf16[896,192]{1,0:T(8,128)(2,1)S(1)} %get-tuple-element.50.query_rows_ref, bf16[896,192]{1,0:T(8,128)(2,1)S(1)} %get-tuple-element.51.key_rows_ref, ...), custom_call_target="tpu_custom_call" | custom-call | flops 3000000000 | bytes 4000000 | tf_op jit(solution)/shard_map/pallas_call | solution.py:324
  66.6 3.3 %all-to-all-start.3 = ((bf16[4,32,384]{2,1,0:T(8,128)(2,1)}), bf16[4,32,384]{2,1,0:T(8,128)(2,1)S(1)}, u32[]{:S(2)}, u32[]{:S(2)}) async-start(bf16[4,32,384]{2,1,0:T(8,128)(2,1)} %get-tuple-element.57), calls=%async_computation.3 | async-start | bytes 196608 | tf_op jit(solution)/shard_map/all_to_all | solution.py:462
  69.9 3.4 %shard_map.107 = (bf16[512,96]{1,0:T(8,128)(2,1)}, bf16[384,192]{1,0:T(8,128)(2,1)}) custom-call(bf16[512,192]{1,0:T(8,128)(2,1)} %get-tuple-element.53.attended_ref.grad_query_ref, f32[512,1]{1,0:T(8,128)} %fusion.13.valid_ref, bf16[512,512]{1,0:T(8,128)(2,1)} %fusion.5.order_ref, bf16[192,192]{1,0:T(8,128)(2,1)} %fusion.14.pick_ref, bf16[512,768]{1,0:T(8,128)(2,1)} %bitcast.55), custom_call_target="tpu_custom_call" | custom-call | flops 3000000000 | bytes 4000000 | tf_op jit(solution)/shard_map/pallas_call | solution.py:324
  73.3 2.4 %all-to-all-done.3.around_ref = bf16[4,32,384]{2,1,0:T(8,128)(2,1)S(1)} async-done(((bf16[4,32,384]{2,1,0:T(8,128)(2,1)}), bf16[4,32,384]{2,1,0:T(8,128)(2,1)S(1)}, u32[]{:S(2)}, u32[]{:S(2)}) %all-to-all-start.3) | async-done | bytes 98336 | tf_op jit(solution)/shard_map/all_to_all | solution.py:462
  75.7 2.7 %shard_map.109 = bf16[768,192]{1,0:T(8,128)(2,1)} custom-call(f32[512,192]{1,0:T(8,128)} %get-tuple-element.56.near_ref, bf16[4,32,384]{2,1,0:T(8,128)(2,1)S(1)} %all-to-all-done.3.around_ref, bf16[512,768]{1,0:T(8,128)(2,1)} %copy-done, bf16[384,192]{1,0:T(8,128)(2,1)} %get-tuple-element.60.out_part_ref), custom_call_target="tpu_custom_call" | custom-call | flops 200000000 | bytes 4000000 | tf_op jit(solution)/shard_map/pallas_call | solution.py:324
  78.4 5.3 %all-to-all-start.4 = ((bf16[32,24,192]{2,1,0:T(8,128)(2,1)}), bf16[32,24,192]{2,1,0:T(8,128)(2,1)S(1)}, u32[]{:S(2)}, u32[]{:S(2)}) async-start(bf16[32,24,192]{2,1,0:T(8,128)(2,1)} %bitcast.19), calls=%async_computation.4 | async-start | bytes 786432 | tf_op jit(solution)/shard_map/all_to_all | solution.py:343
  83.8 5.5 %shard_map.108 = (f32[2,2,128,768]{3,2,1,0:T(8,128)}, f32[2,2,128,768]{3,2,1,0:T(8,128)}) custom-call(bf16[512,96]{1,0:T(8,128)(2,1)} %get-tuple-element.54.attended_ref, bf16[96,768]{1,0:T(8,128)(2,1)} %get-tuple-element.55.out_weight_ref, bf16[512,192]{1,0:T(8,128)(2,1)} %get-tuple-element.53.attended_ref.grad_query_ref, ...), custom_call_target="tpu_custom_call" | custom-call | flops 3000000000 | bytes 4000000 | tf_op jit(solution)/shard_map/pallas_call | solution.py:324
  89.3 3.8 %all-to-all-done.4 = bf16[32,24,192]{2,1,0:T(8,128)(2,1)S(1)} async-done(((bf16[32,24,192]{2,1,0:T(8,128)(2,1)}), bf16[32,24,192]{2,1,0:T(8,128)(2,1)S(1)}, u32[]{:S(2)}, u32[]{:S(2)}) %all-to-all-start.4) | async-done | bytes 294944 | tf_op jit(solution)/shard_map/all_to_all | solution.py:343
  93.1 2.0 %collective-permute-start.2 = (f32[2,2,128,768]{3,2,1,0:T(8,128)}, f32[2,2,128,768]{3,2,1,0:T(8,128)S(1)}, u32[]{:S(2)}, u32[]{:S(2)}) collective-permute-start(f32[2,2,128,768]{3,2,1,0:T(8,128)} %get-tuple-element.62), channel_id=1, source_target_pairs={{0,1},{1,0},{2,3},{3,2},{4,5},{5,4},{6,7},{7,6},{8,9},{9,8},{10,11... | collective-permute-start | bytes 4718600 | tf_op jit(solution)/shard_map/ppermute | solution.py:44
  95.9 4.8 %all-to-all-start.5 = ((bf16[16,3,384]{2,1,0:T(4,128)(2,1)}), bf16[16,3,384]{2,1,0:T(4,128)(2,1)S(1)}, u32[]{:S(2)}, u32[]{:S(2)}) async-start(bf16[16,3,384]{2,1,0:T(4,128)(2,1)} %shard_map.110), calls=%async_computation.5 | async-start | bytes 98304 | tf_op jit(solution)/shard_map/all_to_all | solution.py:348
  100.7 1.6 %add.311 = f32[2,2,128,768]{3,2,1,0:T(8,128)S(1)} add(f32[2,2,128,768]{3,2,1,0:T(8,128)} %get-tuple-element.59, f32[2,2,128,768]{3,2,1,0:T(8,128)S(1)} %collective-permute-done.2) | non-fusion elementwise | flops 393216 | bytes 4718592 | tf_op jit(solution)/shard_map/add | solution.py:345
  102.3 3.5 %collective-permute-start.3 = (bf16[2,128,768]{2,1,0:T(8,128)(2,1)S(1)}, bf16[2,128,768]{2,1,0:T(8,128)(2,1)S(1)}, u32[]{:S(2)}, u32[]{:S(2)}) collective-permute-start(bf16[2,128,768]{2,1,0:T(8,128)(2,1)S(1)} %fusion.8), channel_id=1, source_target_pairs={{0,2},{2,0},{1,3},{3,1},{4,6},{6,4},{5,7},{7,5},{8,10},{10,8},{9,1... | collective-permute-start | bytes 1179656 | tf_op jit(solution)/shard_map/ppermute | solution.py:44
  105.8 7.8 %all-to-all-done.5 = bf16[16,3,384]{2,1,0:T(4,128)(2,1)S(1)} async-done(((bf16[16,3,384]{2,1,0:T(4,128)(2,1)}), bf16[16,3,384]{2,1,0:T(4,128)(2,1)S(1)}, u32[]{:S(2)}, u32[]{:S(2)}) %all-to-all-start.5) | async-done | bytes 36896 | tf_op jit(solution)/shard_map/all_to_all | solution.py:348
  113.7 9.0 %all_to_all.35.pieces_ref = f32[8,3,384]{2,1,0:T(4,128)S(1)} all-to-all(f32[8,3,384]{2,1,0:T(4,128)S(1)} %broadcast_in_dim.5), channel_id=1, replica_groups=mesh['yl'=2,'x'=4,'zh'=4,'zl'=4,'yh'=2,'c'=2] {'yl','x'}, dimensions={0} | all-to-all | bytes 73728 | tf_op jit(solution)/shard_map/all_to_all | solution.py:350
  123.3 0.8 fusion.10
  (37 shorter events, 4.1 us)
Async XLA Ops:
  2.1 28.8 %all-to-all-start = ((bf16[16,3,768]{2,1,0:T(4,128)(2,1)}), bf16[16,3,768]{2,1,0:T(4,128)(2,1)S(1)}, u32[]{:S(2)}, u32[]{:S(2)}) async-start(bf16[16,3,768]{2,1,0:T(4,128)(2,1)} %shard_map.102), calls=%async_computation | async-start | bytes 196608 | tf_op jit(solution)/shard_map/all_to_all | solution.py:374
  18.3 22.6 %collective-permute-start = (bf16[256,768]{1,0:T(8,128)(2,1)S(1)}, bf16[256,768]{1,0:T(8,128)(2,1)S(1)}, u32[]{:S(2)}, u32[]{:S(2)}) collective-permute-start(bf16[256,768]{1,0:T(8,128)(2,1)S(1)} %pad_maximum_fusion.1), channel_id=1, source_target_pairs={{0,2},{2,0},{1,3},{3,1},{4,6},{6,4},{5,7},{7,5},{8,10},{10,8},{9,1... | collective-permute-start | bytes 1179656 | tf_op jit(solution)/shard_map/ppermute | solution.py:44
  32.1 19.0 %all-to-all-start.1 = ((bf16[32,24,384]{2,1,0:T(8,128)(2,1)}), bf16[32,24,384]{2,1,0:T(8,128)(2,1)S(1)}, u32[]{:S(2)}, u32[]{:S(2)}) async-start(bf16[32,24,384]{2,1,0:T(8,128)(2,1)} %bitcast.17), calls=%async_computation.1 | async-start | bytes 1179648 | tf_op jit(solution)/shard_map/all_to_all | solution.py:380
  41.0 4.9 %collective-permute-start.1 = (bf16[512,768]{1,0:T(8,128)(2,1)S(1)}, bf16[512,768]{1,0:T(8,128)(2,1)S(1)}, u32[]{:S(2)}, u32[]{:S(2)}) collective-permute-start(bf16[512,768]{1,0:T(8,128)(2,1)S(1)} %constant_dynamic-update-slice_fusion), channel_id=1, source_target_pairs={{0,1},{1,0},{2,3},{3,2},{4,5},{5,4},{6,7},{7,6},{8,9},{9,8},{10,11... | collective-permute-start | bytes 2359304 | tf_op jit(solution)/shard_map/ppermute | solution.py:44
  48.9 6.6 %copy-start = (bf16[512,768]{1,0:T(8,128)(2,1)}, bf16[512,768]{1,0:T(8,128)(2,1)S(1)}, u32[]{:S(2)}) copy-start(bf16[512,768]{1,0:T(8,128)(2,1)S(1)} %convolution_convert_fusion.tokens_ref.even_ref.odd_ref) | copy-start | bytes 2359300
  51.1 4.4 %copy-start.1 = (bf16[32,24,384]{2,1,0:T(8,128)(2,1)}, bf16[32,24,384]{2,1,0:T(8,128)(2,1)S(1)}, u32[]{:S(2)}) copy-start(bf16[32,24,384]{2,1,0:T(8,128)(2,1)S(1)} %all-to-all-done.1) | copy-start | bytes 1769476
  52.2 9.1 %all-to-all-start.2 = ((bf16[4,32,384]{2,1,0:T(8,128)(2,1)}), bf16[4,32,384]{2,1,0:T(8,128)(2,1)S(1)}, u32[]{:S(2)}, u32[]{:S(2)}) async-start(bf16[4,32,384]{2,1,0:T(8,128)(2,1)} %shard_map.105), calls=%async_computation.2 | async-start | bytes 196608 | tf_op jit(solution)/shard_map/all_to_all | solution.py:438
  66.6 9.1 %all-to-all-start.3 = ((bf16[4,32,384]{2,1,0:T(8,128)(2,1)}), bf16[4,32,384]{2,1,0:T(8,128)(2,1)S(1)}, u32[]{:S(2)}, u32[]{:S(2)}) async-start(bf16[4,32,384]{2,1,0:T(8,128)(2,1)} %get-tuple-element.57), calls=%async_computation.3 | async-start | bytes 196608 | tf_op jit(solution)/shard_map/all_to_all | solution.py:462
  75.7 8.1 %copy-start.2 = (bf16[4,32,384]{2,1,0:T(8,128)(2,1)}, bf16[4,32,384]{2,1,0:T(8,128)(2,1)S(1)}, u32[]{:S(2)}) copy-start(bf16[4,32,384]{2,1,0:T(8,128)(2,1)S(1)} %all-to-all-done.3.around_ref) | copy-start | bytes 294916
  78.4 14.7 %all-to-all-start.4 = ((bf16[32,24,192]{2,1,0:T(8,128)(2,1)}), bf16[32,24,192]{2,1,0:T(8,128)(2,1)S(1)}, u32[]{:S(2)}, u32[]{:S(2)}) async-start(bf16[32,24,192]{2,1,0:T(8,128)(2,1)} %bitcast.19), calls=%async_computation.4 | async-start | bytes 786432 | tf_op jit(solution)/shard_map/all_to_all | solution.py:343
  93.1 7.6 %collective-permute-start.2 = (f32[2,2,128,768]{3,2,1,0:T(8,128)}, f32[2,2,128,768]{3,2,1,0:T(8,128)S(1)}, u32[]{:S(2)}, u32[]{:S(2)}) collective-permute-start(f32[2,2,128,768]{3,2,1,0:T(8,128)} %get-tuple-element.62), channel_id=1, source_target_pairs={{0,1},{1,0},{2,3},{3,2},{4,5},{5,4},{6,7},{7,6},{8,9},{9,8},{10,11... | collective-permute-start | bytes 4718600 | tf_op jit(solution)/shard_map/ppermute | solution.py:44
  95.9 17.7 %all-to-all-start.5 = ((bf16[16,3,384]{2,1,0:T(4,128)(2,1)}), bf16[16,3,384]{2,1,0:T(4,128)(2,1)S(1)}, u32[]{:S(2)}, u32[]{:S(2)}) async-start(bf16[16,3,384]{2,1,0:T(4,128)(2,1)} %shard_map.110), calls=%async_computation.5 | async-start | bytes 98304 | tf_op jit(solution)/shard_map/all_to_all | solution.py:348
  102.3 21.0 %collective-permute-start.3 = (bf16[2,128,768]{2,1,0:T(8,128)(2,1)S(1)}, bf16[2,128,768]{2,1,0:T(8,128)(2,1)S(1)}, u32[]{:S(2)}, u32[]{:S(2)}) collective-permute-start(bf16[2,128,768]{2,1,0:T(8,128)(2,1)S(1)} %fusion.8), channel_id=1, source_target_pairs={{0,2},{2,0},{1,3},{3,1},{4,6},{6,4},{5,7},{7,5},{8,10},{10,8},{9,1... | collective-permute-start | bytes 1179656 | tf_op jit(solution)/shard_map/ppermute | solution.py:44
